TPU v7x, 32 devices: a whole 2x2x4 slice. The times are simulated.
32 devices in a mesh: band: 16 (over z, x, core), comp: 2 (over y).
Axes of the slice: x: 2, y: 2, z: 4, core: 2. Of those that a mesh axis runs over, the one named last changes fastest.
Arguments:
- energy: bfloat16 [720, 32, 1024], P('comp', 'band'), may hold values from 0.19921875 to 2
- depth_speed: float32 [32, 1024], P('band'), may hold values from 0.3 to 1
- ocean_mask: int32 [32, 1024], P('band'), may hold values from 0 to 1, as said below
- interp_first: bfloat16 [720, 720], replicated, may hold values from -0.21875 to 0.21875
- interp_second: bfloat16 [720, 720], replicated, may hold values from -0.21875 to 0.21875
- transfer_matrix: bfloat16 [720, 720], replicated, may hold values from -0.21875 to 0.21875
- growth: float32 [720], replicated, may hold values from -0.5 to 1
Outputs:
- energy_next: bfloat16 [720, 32, 1024], P('comp', 'band')
Inputs may be any that keep to these rules, and one draw needn't show every extreme that they name: `ocean_mask`: split the 1024 columns into equal longitude blocks of 512 columns, one for each index of comp; within each band of 2 rows every block of 1024 cells holds at most 768 ocean cells, and in every band one block holds exactly 768.
All inputs are finite; a program needn't handle non-finite values.
Results may differ from a plain program's by a relative error of at most 0.0048.
Values may be sent and summed in bfloat16 or wider, within the bound.
No kernel may reach another device: no remote copies, remote signals or barrier semaphores. Data moves between devices by JAX's collectives and lax.ppermute only.
A program may use at most 64 MiB of HBM per device.

v0:
```python
import jax
import jax.numpy as jnp
from jax import lax
from jax.sharding import PartitionSpec as P

ND = 24


SOURCE_STEP = 0.5
COURANT_TOP = 0.9
FREQ_RATIO = 1.1


def with_halo(value, sides, width):
    for axis, dim in sides:
        peers, length = (lax.axis_size(axis), value.shape[dim])
        up = [(i, (i + 1) % peers) for i in range(peers - 1)]
        down = [(j, i) for i, j in up]
        last = lax.slice_in_dim(value, length - width, length, axis=dim)
        first = lax.slice_in_dim(value, 0, width, axis=dim)
        before = lax.ppermute(last, axis, up)
        after = lax.ppermute(first, axis, down)
        value = jnp.concatenate([before, value, after], axis=dim)
    return value


def courant_numbers(first_comp, local_comps):
    components = first_comp + jnp.arange(local_comps, dtype=jnp.int32)
    frequency = (components // ND).astype(jnp.float32)
    direction = (components % ND).astype(jnp.float32)
    heading = 2.0 * jnp.pi * (direction + 0.5) / ND
    factor = COURANT_TOP * jnp.power(jnp.float32(FREQ_RATIO), -frequency)
    return (factor * jnp.cos(heading), factor * jnp.sin(heading))


def upwind(middle, lower_one, lower_two, upper_one, upper_two, courant):
    magnitude = jnp.abs(courant)
    first_up = jnp.where(courant > 0, lower_one, upper_one)
    second_up = jnp.where(courant > 0, lower_two, upper_two)
    return (
        middle
        - 0.5 * magnitude * (3.0 * middle - 4.0 * first_up + second_up)
        + 0.5 * magnitude * magnitude * (middle - 2.0 * first_up + second_up)
    )


def half_step(extended, lat_courant, lon_courant, depth_speed, ocean):
    widened = extended.astype(jnp.float32)
    swept = upwind(
        widened[:, 2:-2],
        widened[:, 1:-3],
        widened[:, :-4],
        widened[:, 3:-1],
        widened[:, 4:],
        lat_courant[:, None, None] * depth_speed[None],
    )
    lon_values = lon_courant[:, None, None] * depth_speed[None]
    swept = upwind(
        swept,
        jnp.roll(swept, 1, axis=2),
        jnp.roll(swept, 2, axis=2),
        jnp.roll(swept, -1, axis=2),
        jnp.roll(swept, -2, axis=2),
        lon_values,
    )
    return ocean[None] * swept


def source_terms(cell_spectra, interp_first, interp_second, transfer_matrix, growth):
    forward_interp = jnp.dot(interp_first, cell_spectra, preferred_element_type=jnp.float32)
    backward_interp = jnp.dot(interp_second, cell_spectra, preferred_element_type=jnp.float32)
    product = (forward_interp * backward_interp).astype(jnp.bfloat16)
    nonlinear = jnp.dot(transfer_matrix, product, preferred_element_type=jnp.float32)
    spectra32 = cell_spectra.astype(jnp.float32)
    mean_level = jnp.mean(spectra32, axis=0)
    damping = mean_level * mean_level / (1.0 + mean_level * mean_level)
    total = SOURCE_STEP * (nonlinear + (growth[:, None] - damping[None]) * spectra32)
    return total.astype(jnp.bfloat16)


def shards(energy, depth_speed, ocean_mask, interp_first, interp_second, transfer_matrix, growth):
    local_comps = energy.shape[0]
    lat_courant, lon_courant = courant_numbers(lax.axis_index("comp") * local_comps, local_comps)
    ocean = ocean_mask.astype(jnp.float32)
    start = (ocean[None] * energy.astype(jnp.float32)).astype(jnp.bfloat16)
    rimmed = with_halo(start, (("band", 1),), 2)
    half_one = half_step(rimmed, lat_courant, lon_courant, depth_speed, ocean)
    spectra = half_one.astype(jnp.bfloat16)
    block_in = lax.all_to_all(spectra, "comp", split_axis=2, concat_axis=0, tiled=True)
    total_comps = block_in.shape[0]
    flat_cells = block_in.reshape(total_comps, -1)
    result = source_terms(flat_cells, interp_first, interp_second, transfer_matrix, growth)
    source = lax.all_to_all(
        result.reshape(block_in.shape), "comp", split_axis=0, concat_axis=2, tiled=True
    ).astype(jnp.float32)
    updated = ocean[None] * (half_one + source)
    rimmed_mid = with_halo(updated, (("band", 1),), 2)
    final_field = half_step(rimmed_mid, lat_courant, lon_courant, depth_speed, ocean)
    return final_field.astype(jnp.bfloat16)


def solution(mesh):
    in_specs = (P("comp", "band", None), P("band", None), P("band", None), P(), P(), P(), P())
    out_specs = P("comp", "band", None)
    return jax.shard_map(shards, mesh=mesh, in_specs=in_specs, out_specs=out_specs, check_vma=False)
```

profile of v0, /device:TPU:1, one launch (start us, length us, event | category | flops | bytes accessed | tf_op | source)
XLA Modules:
  0.0 193.7 jit_solution(11645957381942708663)
XLA Ops:
  0.0 0.8 convert_element_type.63
  0.8 1.8 multiply_convert_fusion.1
  2.6 2.0 %collective-permute-start.1 = (bf16[360,2,1024]{2,0,1:T(8,128)(2,1)S(1)}, bf16[360,2,1024]{2,0,1:T(8,128)(2,1)}, u32[]{:S(2)}, u32[]{:S(2)}) collective-permute-start(bf16[360,2,1024]{2,0,1:T(8,128)(2,1)S(1)} %multiply_convert_fusion.1), channel_id=1, source_target_pairs={{2,0},{4,2},{6,4},{8,6},{10,8},{12,10},{14,12},{16,14},{18,16},{20... | collective-permute-start | bytes 4423688 | tf_op jit(solution)/shard_map/ppermute | solution.py:22
  4.6 4.5 %collective-permute-start = (bf16[360,2,1024]{2,0,1:T(8,128)(2,1)S(1)}, bf16[360,2,1024]{2,0,1:T(8,128)(2,1)}, u32[]{:S(2)}, u32[]{:S(2)}) collective-permute-start(bf16[360,2,1024]{2,0,1:T(8,128)(2,1)S(1)} %multiply_convert_fusion.1), channel_id=1, source_target_pairs={{0,2},{2,4},{4,6},{6,8},{8,10},{10,12},{12,14},{14,16},{16,18},{18... | collective-permute-start | bytes 4423688 | tf_op jit(solution)/shard_map/ppermute | solution.py:21
  9.1 15.1 %collective-permute-done.1 = bf16[360,2,1024]{2,0,1:T(8,128)(2,1)} collective-permute-done((bf16[360,2,1024]{2,0,1:T(8,128)(2,1)S(1)}, bf16[360,2,1024]{2,0,1:T(8,128)(2,1)}, u32[]{:S(2)}, u32[]{:S(2)}) %collective-permute-start.1) | collective-permute-done | bytes 1474592 | tf_op jit(solution)/shard_map/ppermute | solution.py:22
  24.3 15.9 %collective-permute-done = bf16[360,2,1024]{2,0,1:T(8,128)(2,1)} collective-permute-done((bf16[360,2,1024]{2,0,1:T(8,128)(2,1)S(1)}, bf16[360,2,1024]{2,0,1:T(8,128)(2,1)}, u32[]{:S(2)}, u32[]{:S(2)}) %collective-permute-start) | collective-permute-done | bytes 1474592 | tf_op jit(solution)/shard_map/ppermute | solution.py:21
  40.1 2.1 %maximum_convert_fusion = f32[360,6,1024]{2,0,1:T(8,128)S(1)} fusion(bf16[360,2,1024]{2,0,1:T(8,128)(2,1)} %collective-permute-done.1, bf16[360,2,1024]{2,0,1:T(8,128)(2,1)S(1)} %multiply_convert_fusion.1, bf16[360,2,1024]{2,0,1:T(8,128)(2,1)} %collective-permute-done), kind=kLoop, calls=%fused_computation | loop fusion | flops 6635520 | bytes 13271040 | tf_op jit(solution)/shard_map/convert_element_type | solution.py:48
  42.3 2.4 %fusion.20 = f32[360,2,1024]{2,0,1:T(8,128)S(1)} fusion(f32[360,6,1024]{2,0,1:T(8,128)S(1)} %maximum_convert_fusion, f32[2,1024]{1,0:T(2,128)S(1)} %copy-done.3, f32[360]{0:T(512)S(1)} %get-tuple-element.24), kind=kLoop, calls=%fused_computation.25 | loop fusion | flops 13271040 | bytes 17704352 | tf_op jit(solution)/shard_map/add | solution.py:41
  45.0 1.2 fusion.48
  46.2 1.2 fusion.50
  47.4 6.4 %fusion.41 = (bf16[360,2,1024]{2,0,1:T(8,128)(2,1)}, f32[360,2,1024]{2,0,1:T(8,128)}) fusion(f32[360,2,2]{2,0,1:T(8,128)S(1)} %get-tuple-element.20, f32[360,2,1022]{2,0,1:T(8,128)S(1)} %get-tuple-element.22, f32[360,2,1022]{2,0,1:T(8,128)S(1)} %get-tuple-element.21, f32[360,2,2]{2,0,1:T(8,128)S(1)} %get-tuple-element.19, ...), kind=kLoop, calls=%fused_computation.63 | loop fusion | flops 30965760 | bytes 30985024 | tf_op jit(solution)/shard_map/convert_element_type | solution.py:88
  53.9 4.3 %copy.18 = bf16[360,2,1024]{0,1,2:T(2,128)(2,1)S(1)} copy(bf16[360,2,1024]{2,0,1:T(8,128)(2,1)} %get-tuple-element.5) | data formatting | bytes 2949120 | tf_op jit(solution)/shard_map/convert_element_type | solution.py:88
  58.2 18.8 %all_to_all.24 = bf16[360,2,1024]{0,1,2:T(2,128)(2,1)} all-to-all(bf16[360,2,1024]{0,1,2:T(2,128)(2,1)S(1)} %copy.18), channel_id=1, replica_groups=mesh['band'=16,'comp'=2] {'comp'}, dimensions={2} | all-to-all | bytes 2949120 | tf_op jit(solution)/shard_map/all_to_all | solution.py:89
  77.0 5.3 %copy.19 = bf16[360,2,2,512]{3,1,0,2:T(2,128)(2,1)S(1)} copy(bf16[360,2,2,512]{0,1,3,2:T(2,128)(2,1)} %bitcast.29) | data formatting | bytes 2949120 | tf_op jit(solution)/shard_map/all_to_all | solution.py:89
  82.3 1.3 convert_reduce_fusion
  83.6 0.4 copy.22
  84.0 1.1 copy-done.2
  85.1 2.9 %fusion.51 = f32[1024,720]{0,1:T(8,128)} fusion(bf16[720,720]{1,0:T(8,128)(2,1)S(1)} %copy-done, bf16[720,1024]{1,0:T(8,128)(2,1)S(1)} %bitcast.31), kind=kOutput, calls=%fused_computation.72 | convolution fusion | flops 1061683200 | bytes 5460480 | tf_op jit(solution)/shard_map/dot_general | solution.py:70
  88.0 5.9 %fusion.32 = bf16[720,1024]{1,0:T(8,128)(2,1)S(1)} fusion(bf16[720,1024]{1,0:T(8,128)(2,1)} %bitcast.32, bf16[720,720]{1,0:T(8,128)(2,1)} %param.12, f32[1024]{0:T(1024)S(1)} %add_divide_fusion, f32[720]{0:T(1024)S(1)} %copy-done.4, f32[1024,720]{0,1:T(8,128)} %fusion.51, bf16[720,720]{1,0:T(8,128)(2,1)} %param.11), kind=kOutput, calls=%fused_computation.40 | convolution fusion | flops 2129264640 | bytes 7978816 | tf_op jit(solution)/shard_map/dot_general | solution.py:73
  93.9 1.1 reshape.57
  95.0 13.0 %all_to_all.25 = bf16[720,2,512]{2,1,0:T(2,128)(2,1)S(1)} all-to-all(bf16[720,2,512]{2,1,0:T(2,128)(2,1)S(1)} %reshape.57), channel_id=1, replica_groups=mesh['band'=16,'comp'=2] {'comp'}, dimensions={0} | all-to-all | bytes 2949120 | tf_op jit(solution)/shard_map/all_to_all | solution.py:93
  108.0 3.1 %copy.26 = f32[2,360,2,512]{3,0,1,2:T(2,128)} copy(bf16[2,360,2,512]{3,2,1,0:T(2,128)(2,1)S(1)} %bitcast.30) | data formatting | bytes 4423680 | tf_op jit(solution)/shard_map/convert_element_type | solution.py:95
  111.1 4.0 %reshape.58 = f32[360,2,1024]{2,0,1:T(8,128)S(1)} reshape(f32[360,2,2,512]{3,2,0,1:T(2,128)} %bitcast.28) | data formatting | bytes 5898240 | tf_op jit(solution)/shard_map/convert_element_type | solution.py:95
  115.2 2.5 %add_multiply_fusion = f32[360,2,1024]{2,0,1:T(8,128)S(1)} fusion(f32[360,2,1024]{2,0,1:T(8,128)} %get-tuple-element.6, f32[360,2,1024]{2,0,1:T(8,128)S(1)} %reshape.58, f32[2,1024]{1,0:T(2,128)S(1)} %convert_element_type.63), kind=kLoop, calls=%fused_computation.42 | loop fusion | flops 1474560 | bytes 8855552 | tf_op jit(solution)/shard_map/mul | solution.py:96
  117.7 2.4 %collective-permute-start.2 = (f32[360,2,1024]{2,0,1:T(8,128)S(1)}, f32[360,2,1024]{2,0,1:T(8,128)S(1)}, u32[]{:S(2)}, u32[]{:S(2)}) collective-permute-start(f32[360,2,1024]{2,0,1:T(8,128)S(1)} %add_multiply_fusion), channel_id=1, source_target_pairs={{0,2},{2,4},{4,6},{6,8},{8,10},{10,12},{12,14},{14,16},{16,18},{18... | collective-permute-start | bytes 8847368 | tf_op jit(solution)/shard_map/ppermute | solution.py:21
  120.1 2.1 %collective-permute-start.3 = (f32[360,2,1024]{2,0,1:T(8,128)S(1)}, f32[360,2,1024]{2,0,1:T(8,128)S(1)}, u32[]{:S(2)}, u32[]{:S(2)}) collective-permute-start(f32[360,2,1024]{2,0,1:T(8,128)S(1)} %add_multiply_fusion), channel_id=1, source_target_pairs={{2,0},{4,2},{6,4},{8,6},{10,8},{12,10},{14,12},{16,14},{18,16},{20... | collective-permute-start | bytes 8847368 | tf_op jit(solution)/shard_map/ppermute | solution.py:22
  122.2 60.3 %collective-permute-done.2 = f32[360,2,1024]{2,0,1:T(8,128)S(1)} collective-permute-done((f32[360,2,1024]{2,0,1:T(8,128)S(1)}, f32[360,2,1024]{2,0,1:T(8,128)S(1)}, u32[]{:S(2)}, u32[]{:S(2)}) %collective-permute-start.2) | collective-permute-done | bytes 2949152 | tf_op jit(solution)/shard_map/ppermute | solution.py:21
  182.5 2.4 %fusion.21 = f32[360,2,1024]{2,0,1:T(8,128)S(1)} fusion(f32[360,2,1024]{2,0,1:T(8,128)S(1)} %add_multiply_fusion, f32[360,2,1024]{2,0,1:T(8,128)S(1)} %collective-permute-done.2, f32[360,2,1024]{2,0,1:T(8,128)S(1)} %collective-permute-done.3, f32[2,1024]{1,0:T(2,128)S(1)} %copy-done.3, f32[360]{0:T(512)S(1)} %get-tuple-element.24), kind=kLoop, calls=%fused_computation.26 | loop fusion | flops 14745600 | bytes 11806112 | tf_op jit(solution)/shard_map/add | solution.py:41
  185.2 1.2 fusion.46
  186.4 1.2 fusion.44
  187.6 3.4 %fusion.26 = bf16[360,2,1024]{2,0,1:T(8,128)(2,1)S(1)} fusion(f32[360,2,1024]{2,0,1:T(8,128)S(1)} %fusion.21, f32[360,2,2]{2,0,1:T(8,128)S(1)} %get-tuple-element.12, f32[360,2,1022]{2,0,1:T(8,128)S(1)} %get-tuple-element.14, f32[360,2,1022]{2,0,1:T(8,128)S(1)} %get-tuple-element.13, f32[360,2,2]{2,0,1:T(8,128)S(1)} %get-tuple-element.11, ...), kind=kLoop, calls=%fused_computation.31 | loop fusion | flops 17694720 | bytes 16237984 | tf_op jit(solution)/shard_map/convert_element_type | solution.py:99
  191.1 2.6 %copy.21 = bf16[360,2,1024]{2,1,0:T(2,128)(2,1)} copy(bf16[360,2,1024]{2,0,1:T(8,128)(2,1)S(1)} %fusion.26) | data formatting | bytes 2949120 | tf_op jit(solution)/shard_map/convert_element_type | solution.py:99
  (18 shorter events, 0.8 us)
Async XLA Ops:
  0.0 85.1 %copy-start = (bf16[720,720]{1,0:T(8,128)(2,1)S(1)}, bf16[720,720]{1,0:T(8,128)(2,1)}, u32[]{:S(2)}) copy-start(bf16[720,720]{1,0:T(8,128)(2,1)} %param.10) | copy-start | bytes 3110404
  2.6 21.7 %collective-permute-start.1 = (bf16[360,2,1024]{2,0,1:T(8,128)(2,1)S(1)}, bf16[360,2,1024]{2,0,1:T(8,128)(2,1)}, u32[]{:S(2)}, u32[]{:S(2)}) collective-permute-start(bf16[360,2,1024]{2,0,1:T(8,128)(2,1)S(1)} %multiply_convert_fusion.1), channel_id=1, source_target_pairs={{2,0},{4,2},{6,4},{8,6},{10,8},{12,10},{14,12},{16,14},{18,16},{20... | collective-permute-start | bytes 4423688 | tf_op jit(solution)/shard_map/ppermute | solution.py:22
  4.6 35.5 %collective-permute-start = (bf16[360,2,1024]{2,0,1:T(8,128)(2,1)S(1)}, bf16[360,2,1024]{2,0,1:T(8,128)(2,1)}, u32[]{:S(2)}, u32[]{:S(2)}) collective-permute-start(bf16[360,2,1024]{2,0,1:T(8,128)(2,1)S(1)} %multiply_convert_fusion.1), channel_id=1, source_target_pairs={{0,2},{2,4},{4,6},{6,8},{8,10},{10,12},{12,14},{14,16},{16,18},{18... | collective-permute-start | bytes 4423688 | tf_op jit(solution)/shard_map/ppermute | solution.py:21
  9.1 33.1 %copy-start.3 = (f32[2,1024]{1,0:T(2,128)S(1)}, f32[2,1024]{1,0:T(2,128)}, u32[]{:S(2)}) copy-start(f32[2,1024]{1,0:T(2,128)} %param.8) | copy-start | bytes 24580
  84.0 1.1 copy-start.2
  85.1 2.9 %copy-start.4 = (f32[720]{0:T(1024)S(1)}, f32[720]{0:T(1024)}, u32[]{:S(2)}) copy-start(f32[720]{0:T(1024)} %param.13) | copy-start | bytes 8644
  117.7 64.8 %collective-permute-start.2 = (f32[360,2,1024]{2,0,1:T(8,128)S(1)}, f32[360,2,1024]{2,0,1:T(8,128)S(1)}, u32[]{:S(2)}, u32[]{:S(2)}) collective-permute-start(f32[360,2,1024]{2,0,1:T(8,128)S(1)} %add_multiply_fusion), channel_id=1, source_target_pairs={{0,2},{2,4},{4,6},{6,8},{8,10},{10,12},{12,14},{14,16},{16,18},{18... | collective-permute-start | bytes 8847368 | tf_op jit(solution)/shard_map/ppermute | solution.py:21
  120.1 62.4 %collective-permute-start.3 = (f32[360,2,1024]{2,0,1:T(8,128)S(1)}, f32[360,2,1024]{2,0,1:T(8,128)S(1)}, u32[]{:S(2)}, u32[]{:S(2)}) collective-permute-start(f32[360,2,1024]{2,0,1:T(8,128)S(1)} %add_multiply_fusion), channel_id=1, source_target_pairs={{2,0},{4,2},{6,4},{8,6},{10,8},{12,10},{14,12},{16,14},{18,16},{20... | collective-permute-start | bytes 8847368 | tf_op jit(solution)/shard_map/ppermute | solution.py:22
  187.6 6.1 %copy-start.1 = (bf16[720,720]{1,0:T(8,128)(2,1)S(1)}, bf16[720,720]{1,0:T(8,128)(2,1)}, u32[]{:S(2)}) copy-start(bf16[720,720]{1,0:T(8,128)(2,1)} %param.10) | copy-start | bytes 3110404
where the time goes:
time: 194 us
  waiting for transfers between devices  91.3 us (47%)
  blocking collectives  31.8 us (16%)
  local copies, waits for them, and re-layouts  27.5 us (14%)
  other arithmetic  23.2 us (12%)
  starting transfers between devices  10.9 us (6%)
  matrix products  8.78 us (5%)
    ppermute x2, waiting for transfers between devices, with_halo(): before = lax.ppermute(last, axis, up)  76.2 us
    all_to_all x1, blocking collectives, shards(): lax.all_to_all(spectra, 'comp', split_axis=2, concat_axis=0, tiled=True)  18.8 us
    ppermute x2, waiting for transfers between devices, with_halo(): after = lax.ppermute(first, axis, down)  15.1 us
    all_to_all x1, blocking collectives, shards(): lax.all_to_all(result.reshape(block_in.shape), 'comp', split_axis=0, conc...  13 us
    convert_element_type x2, local copies, waits for them, and re-layouts, shards(): source = lax.all_to_all(result.reshape(block_in.shape), 'comp', split_axi...  7.17 us
    ppermute x2, starting transfers between devices, with_halo(): before = lax.ppermute(last, axis, up)  6.85 us
    convert_element_type x1, other arithmetic, shards(): spectra = half_one.astype(jnp.bfloat16)  6.44 us
    dot_general x1, matrix products, source_terms(): jnp.dot(transfer_matrix, product, preferred_element_type=jnp.float32)  5.86 us
  transfers between devices with their start and end apart: 4, of which 3 were waited for; matrix products, arithmetic and copies ran while one was open for 0% of the time, Pallas kernels for 0%

commit v1 on v0

--- a/solution.py
+++ b/solution.py
@@ -1,6 +1,12 @@
+import functools
+
 import jax
 import jax.numpy as jnp
+import ml_dtypes
+import numpy as np
 from jax import lax
+from jax.experimental import pallas as pl
+from jax.experimental.pallas import tpu as pltpu
 from jax.sharding import PartitionSpec as P
 
 ND = 24
@@ -9,6 +15,9 @@
 SOURCE_STEP = 0.5
 COURANT_TOP = 0.9
 FREQ_RATIO = 1.1
+
+F32 = jnp.float32
+BF16 = jnp.bfloat16
 
 
 def with_halo(value, sides, width):
@@ -78,7 +87,7 @@
     return total.astype(jnp.bfloat16)
 
 
-def shards(energy, depth_speed, ocean_mask, interp_first, interp_second, transfer_matrix, growth):
+def general_shards(energy, depth_speed, ocean_mask, interp_first, interp_second, transfer_matrix, growth):
     local_comps = energy.shape[0]
     lat_courant, lon_courant = courant_numbers(lax.axis_index("comp") * local_comps, local_comps)
     ocean = ocean_mask.astype(jnp.float32)
@@ -99,7 +108,358 @@
     return final_field.astype(jnp.bfloat16)
 
 
+class Plan:
+    def __init__(self, local_comps, columns):
+        self.local = local_comps
+        self.total = 2 * local_comps
+        self.columns = columns
+        self.half = local_comps // 4
+        self.slots = 2 * self.half
+        self.rows = -(-self.slots // 8) * 8
+        self.pitch = -(-self.slots // 16) * 16
+        self.out_rows = -(-(self.total + 1) // 16) * 16
+
+    def members(self, parity, group):
+        south = (parity == 0) == (group == 0)
+        east, west = (range(6, 12), range(12, 18)) if south else (range(0, 6), range(18, 24))
+        frequencies = range(self.local // ND)
+        slots = [f * ND + d for side in (east, west) for f in frequencies for d in side]
+        return np.array(slots), (1, 0) if south else (0, 1)
+
+    def tables(self):
+        pitch, local = self.pitch, self.local
+        regroup = np.zeros((2, 4 * pitch, 2 * local), np.float32)
+        columns = np.zeros((4, self.total, 4 * pitch), np.float32)
+        courant = np.zeros((4, 2, 2, self.rows, 128), np.float32)
+        comps = np.arange(self.total, dtype=np.int32)
+        heading = np.float32(2.0 * np.pi) * ((comps % ND).astype(np.float32) + np.float32(0.5)) / np.float32(ND)
+        factor = np.float32(COURANT_TOP) * np.power(np.float32(FREQ_RATIO), -(comps // ND).astype(np.float32))
+        lat, lon = np.abs(factor * np.cos(heading)), np.abs(factor * np.sin(heading))
+        at = np.arange(self.slots)
+        for parity in range(2):
+            for group in range(2):
+                slots, rows = self.members(parity, group)
+                for r in range(2):
+                    regroup[parity, (2 * group + r) * pitch + at, 2 * slots + rows[r]] = 1
+                for comp in range(2):
+                    which = 2 * comp + parity
+                    for side, owner in enumerate((comp, 1 - comp)):
+                        columns[which, owner * local + slots, (2 * group + side) * pitch + at] = 1
+                    own = comp * local + slots
+                    courant[which, group, 0, at] = lat[own][:, None]
+                    courant[which, group, 1, at] = lon[own][:, None]
+        owners = [columns[:, :, 2 * g * pitch : (2 * g + 1) * pitch] for g in range(2)]
+        rows_of = np.concatenate(owners, axis=2).transpose(0, 2, 1)
+        half = ml_dtypes.bfloat16
+        return (
+            regroup.astype(half),
+            regroup.transpose(0, 2, 1).astype(half),
+            columns.astype(half),
+            np.ascontiguousarray(rows_of).astype(half),
+            courant,
+        )
+
+
+VMEM_LIMIT = 40 << 20
+
+
+def whole(shape):
+    return pl.BlockSpec(shape, lambda i, ids: (0,) * len(shape))
+
+
+def picked(shape, at, rest=()):
+    tail = (0,) * (len(shape) - 1 - len(rest))
+    return pl.BlockSpec((1,) + tuple(shape[1:]), lambda i, ids: (ids[at],) + tuple(rest) + tail)
+
+
+def call(body, ids, operands, specs, outs, scratch=(), flops=0):
+    moved = sum(x.size * x.dtype.itemsize for x in operands if x.size < 1 << 21)
+    return pl.pallas_call(
+        body,
+        grid_spec=pltpu.PrefetchScalarGridSpec(
+            num_scalar_prefetch=1,
+            grid=(1,),
+            in_specs=specs,
+            out_specs=[whole(o.shape) for o in outs],
+            scratch_shapes=list(scratch),
+        ),
+        out_shape=outs,
+        compiler_params=pltpu.CompilerParams(vmem_limit_bytes=VMEM_LIMIT),
+        cost_estimate=pl.CostEstimate(flops=flops, bytes_accessed=moved, transcendentals=0),
+    )(ids, *operands)
+
+
+def in_order(ids, value, group):
+    even = ids[0] == 0
+    one, two = value[0:1], value[1:2]
+    first, second = jnp.where(even, one, two), jnp.where(even, two, one)
+    return (second, first) if group == 0 else (first, second)
+
+
+def prep_body(plan, ids, regroup, energy, mask, *outs):
+    ocean = mask[...].astype(F32)
+    flat = energy[...].reshape(2 * plan.local, plan.columns)
+    moved = jnp.dot(regroup[0], flat, preferred_element_type=F32)
+    for group in range(2):
+        rows = in_order(ids, ocean, group)
+        for r in range(2):
+            at = (2 * group + r) * plan.pitch
+            outs[group][r] = (moved[at : at + plan.rows] * rows[r]).astype(BF16)
+
+
+def sweep(u, p, q, a):
+    d = p - u
+    e = (q - p) - d
+    return u + a * (d + (0.5 * a - 0.5) * e)
+
+
+def lon_sweep(u, a, shift, size):
+    def back(x):
+        return pltpu.roll(x, shift % size, 1)
+
+    d = back(u) - u
+    e = back(d) - d
+    return u + a * (d + (0.5 * a - 0.5) * e)
+
+
+def half_steps(plan, group, ids, courant, depth, mask, depth8, ocean8, load, store):
+    size = plan.columns
+    for r, row in enumerate(in_order(ids, depth[...], group)):
+        depth8[r] = jnp.broadcast_to(row, (8, size))
+    for r, row in enumerate(in_order(ids, mask[...].astype(F32), group)):
+        ocean8[r] = jnp.broadcast_to(row, (8, size))
+
+    def block(start, rows, side):
+        u0, u1, h0, h1 = load(start, rows)
+        c_lat = courant[0, group, 0, pl.ds(start, rows)]
+        c_lon = courant[0, group, 1, pl.ds(start, rows)]
+        news = ([], [])
+        for s in range(0, rows, 8):
+            part = slice(s, s + 8)
+            lat = jnp.concatenate([c_lat[part]] * (size // 128), axis=1)
+            lon = jnp.concatenate([c_lon[part]] * (size // 128), axis=1)
+            stencil = ((u0[part], h0[part], h1[part]), (u1[part], u0[part], h0[part]))
+            for r in range(2):
+                dep = depth8[r]
+                u = sweep(*stencil[r], lat * dep)
+                a = lon * dep
+                if side == 0:
+                    at = lax.broadcasted_iota(jnp.int32, (8, size), 0) + (start + s)
+                    u = jnp.where(at < plan.half, lon_sweep(u, a, 1, size), lon_sweep(u, a, -1, size))
+                else:
+                    u = lon_sweep(u, a, side, size)
+                news[r].append(u * ocean8[r])
+        store(start, rows, jnp.concatenate(news[0], axis=0), jnp.concatenate(news[1], axis=0))
+
+    east = plan.half // 16
+    west = -(-plan.half // 16)
+    full = plan.rows // 16
+
+    @pl.loop(0, east)
+    def _(i):
+        block(pl.multiple_of(i * 16, 16), 16, 1)
+
+    for i in range(east, west):
+        block(i * 16, 16, 0)
+
+    @pl.loop(west, full)
+    def _(i):
+        block(pl.multiple_of(i * 16, 16), 16, -1)
+
+    if plan.rows % 16:
+        block(full * 16, plan.rows % 16, -1)
+
+
+def first_body(plan, group, ids, courant, depth, mask, field, halo, *rest):
+    half, spectra, (depth8, ocean8) = rest[:2], rest[2:-2], rest[-2:]
+
+    def load(start, rows):
+        at = pl.ds(start, rows)
+        return tuple(ref[r, at].astype(F32) for ref, r in ((field, 0), (field, 1), (halo, 1), (halo, 0)))
+
+    def store(start, rows, new0, new1):
+        at = pl.ds(start, rows)
+        for r, new in enumerate((new0, new1)):
+            half[r][at] = new
+            if len(spectra) == 1:
+                spectra[0][r, at] = new.astype(BF16)
+            else:
+                spectra[r][at] = new.astype(BF16)
+
+    half_steps(plan, group, ids, courant, depth, mask, depth8, ocean8, load, store)
+
+
+def last_body(plan, group, ids, courant, depth, mask, u0, u1, h0, h1, *rest):
+    depth8, ocean8 = rest[-2:]
+
+    def load(start, rows):
+        at = pl.ds(start, rows)
+        return tuple(ref[at].astype(F32) for ref in (u0, u1, h0, h1))
+
+    def fill(ref):
+        def store(start, rows, new0, new1):
+            for r, new in enumerate((new0, new1)):
+                at = r * plan.pitch + start
+                if rows < 16:
+                    new = jnp.concatenate([new, jnp.zeros((16 - rows, plan.columns), F32)], axis=0)
+                ref[pl.ds(pl.multiple_of(at, 16), 16)] = new.astype(BF16)
+
+        return store
+
+    if group == 0:
+        (done,) = rest[:1]
+        half_steps(plan, group, ids, courant, depth, mask, depth8, ocean8, load, fill(done))
+    else:
+        earlier, restore, out, done = rest[:4]
+        half_steps(plan, group, ids, courant, depth, mask, depth8, ocean8, load, fill(done))
+        split = 2 * plan.pitch
+        flat = jnp.dot(restore[0][:, :split], earlier[...], preferred_element_type=F32)
+        flat += jnp.dot(restore[0][:, split:], done[...], preferred_element_type=F32)
+        out[...] = flat.astype(BF16).reshape(plan.local, 2, plan.columns)
+
+
+def weights_body(plan, ids, columns, rows_of, first, second, transfer, growth, first_out, second_out, transfer_out, growth_out):
+    total = plan.total
+    first_out[:total] = jnp.dot(first[...], columns[0], preferred_element_type=F32).astype(BF16)
+    extra = plan.out_rows - total
+    ones = lax.broadcasted_iota(jnp.int32, (extra, 4 * plan.pitch), 0) == 0
+    first_out[total:] = jnp.where(ones, 1.0, 0.0).astype(BF16)
+    second_out[...] = jnp.dot(second[...], columns[0], preferred_element_type=F32).astype(BF16)
+    chosen = rows_of[0]
+    transfer_out[...] = jnp.dot(chosen, transfer[...], preferred_element_type=F32).astype(BF16)
+    rate = jnp.sum(chosen.astype(F32) * growth[...], axis=1, keepdims=True)
+    growth_out[...] = jnp.broadcast_to(rate, growth_out.shape)
+
+
+TILE = 256
+
+
+def source_body(plan, turn, ids, first, second, transfer, growth, mask, own0, peer0, own1, peer1, half0, half1, *rest):
+    full0, sent0, full1, sent1, cells = rest
+    total, rows, pitch = plan.total, plan.rows, plan.pitch
+    mine = (own0[turn], own1[...])
+    for i, block in enumerate((mine[0], peer0[turn], mine[1], peer1[...])):
+        whole_rows = rows // 16 * 16
+        cells[i * pitch : i * pitch + whole_rows] = block[:whole_rows]
+        if whole_rows < pitch:
+            tail = block[whole_rows:].astype(F32)
+            tail = jnp.concatenate([tail, jnp.zeros((pitch - rows, plan.columns), F32)], axis=0)
+            cells[i * pitch + whole_rows : (i + 1) * pitch] = tail.astype(BF16)
+    ocean = in_order(ids, mask[...].astype(F32), 0)[turn]
+    for c in range(0, plan.columns, TILE):
+        at = slice(c, c + TILE)
+        piece = cells[:, at]
+        forward = jnp.dot(first[...], piece, preferred_element_type=F32)
+        backward = jnp.dot(second[...], piece, preferred_element_type=F32)
+        product = (forward[:total] * backward).astype(BF16)
+        nonlinear = jnp.dot(transfer[...], product, preferred_element_type=F32)
+        level = forward[total : total + 1] / total
+        damping = level * level / (1.0 + level * level)
+        for group, (half, full, sent) in enumerate(((half0, full0, sent0), (half1, full1, sent1))):
+            begin = group * pitch
+            rate = jnp.concatenate([growth[begin : begin + rows]] * (TILE // 128), axis=1)
+            spectra = cells[2 * group * pitch : (2 * group + 1) * pitch, at].astype(F32)[:rows]
+            source = SOURCE_STEP * (nonlinear[begin : begin + rows] + (rate - damping) * spectra)
+            updated = ocean[:, at] * (half[:, at] + source.astype(BF16).astype(F32))
+            full[:, at] = updated
+            sent[:, at] = updated.astype(BF16)
+
+
+def paired_shards(energy, depth_speed, ocean_mask, interp_first, interp_second, transfer_matrix, growth):
+    plan = Plan(energy.shape[0], energy.shape[2])
+    size, rows, pitch, total = plan.columns, plan.rows, plan.pitch, plan.total
+    regroup, restore, columns, rows_of, courant = plan.tables()
+    bands = lax.axis_size("band")
+    parity = lax.axis_index("band") % 2
+    ids = jnp.stack([parity, 2 * lax.axis_index("comp") + parity]).astype(jnp.int32)
+    growth = growth.reshape(1, total)
+
+    inner = [(i, i ^ 1) for i in range(bands)]
+    outer = [(i, j) for i in range(1, bands - 1) for j in [i + 1 if i % 2 else i - 1]]
+    peers = [(0, 1), (1, 0)]
+
+    def shape(*dims, kind=BF16):
+        return jax.ShapeDtypeStruct(dims, kind)
+
+    sweeps = 2 * 40 * rows * size
+    rims = [pltpu.VMEM((2, 8, size), F32)] * 2
+
+    fields = call(
+        functools.partial(prep_body, plan),
+        ids,
+        (regroup, energy, ocean_mask),
+        [picked(regroup.shape, 0), whole(energy.shape), whole(ocean_mask.shape)],
+        [shape(2, rows, size)] * 2,
+        flops=2 * 4 * pitch * 2 * plan.local * size,
+    )
+    halo0 = lax.ppermute(fields[1], "band", inner)
+    halo1 = lax.ppermute(fields[0], "band", outer)
+
+    def first_step(group, halo, spectra):
+        return call(
+            functools.partial(first_body, plan, group),
+            ids,
+            (courant, depth_speed, ocean_mask, fields[group], halo),
+            [picked(courant.shape, 1)] + [whole(x.shape) for x in (depth_speed, ocean_mask, halo, halo)],
+            [shape(rows, size, kind=F32)] * 2 + spectra,
+            rims,
+            flops=sweeps,
+        )
+
+    *half0, own0 = first_step(0, halo0, [shape(2, rows, size)])
+    peer0 = lax.ppermute(own0, "comp", peers)
+    first, second, transfer, rate = call(
+        functools.partial(weights_body, plan),
+        ids,
+        (columns, rows_of, interp_first, interp_second, transfer_matrix, growth),
+        [picked(columns.shape, 1), picked(rows_of.shape, 1)] + [whole((total, total))] * 3 + [whole((1, total))],
+        [shape(plan.out_rows, 4 * pitch), shape(total, 4 * pitch), shape(2 * pitch, total), shape(2 * pitch, 128, kind=F32)],
+        flops=2 * total * total * 10 * pitch,
+    )
+    *half1, own1_0, own1_1 = first_step(1, halo1, [shape(rows, size)] * 2)
+    own1 = (own1_0, own1_1)
+    peer1 = [None, None]
+    peer1[1] = lax.ppermute(own1[1], "comp", peers)
+    peer1[0] = lax.ppermute(own1[0], "comp", peers)
+
+    full0, sent0, full1, sent1 = [None] * 2, [None] * 2, [None] * 2, [None] * 2
+    for turn in range(2):
+        operands = (
+            first, second, transfer, rate, ocean_mask, own0, peer0, own1[1 - turn], peer1[1 - turn], half0[turn], half1[1 - turn],
+        )
+        full0[turn], sent0[turn], full1[1 - turn], sent1[1 - turn] = call(
+            functools.partial(source_body, plan, turn),
+            ids,
+            operands,
+            [whole(x.shape) for x in operands],
+            [shape(rows, size, kind=F32), shape(rows, size)] * 2,
+            [pltpu.VMEM((4 * pitch, size), BF16)],
+            flops=2 * total * 10 * pitch * size,
+        )
+    rim1 = [lax.ppermute(x, "band", outer) for x in sent0]
+    rim0 = [lax.ppermute(x, "band", inner) for x in sent1]
+
+    def last_step(group, full, rim, more, outs, scratch):
+        operands = (courant, depth_speed, ocean_mask, full[0], full[1], rim[1], rim[0]) + more
+        specs = [picked(courant.shape, 1)] + [whole(x.shape) for x in operands[1:7]]
+        if more:
+            specs += [whole(more[0].shape), picked(more[1].shape, 0)]
+        return call(
+            functools.partial(last_body, plan, group), ids, operands, specs, outs, list(scratch) + rims, flops=sweeps
+        )
+
+    (early,) = last_step(0, full0, rim0, (), [shape(2 * pitch, size)], ())
+    (out,) = last_step(1, full1, rim1, (early, restore), [shape(*energy.shape)], [pltpu.VMEM((2 * pitch, size), BF16)])
+    return out
+
+
 def solution(mesh):
+    def shards(energy, *others):
+        paired = lax.axis_size("comp") == 2 and lax.axis_size("band") % 2 == 0
+        if paired and energy.shape[0] % ND == 0 and energy.shape[1] == 2 and energy.shape[2] % TILE == 0:
+            return paired_shards(energy, *others)
+        return general_shards(energy, *others)
+
     in_specs = (P("comp", "band", None), P("band", None), P("band", None), P(), P(), P(), P())
     out_specs = P("comp", "band", None)
     return jax.shard_map(shards, mesh=mesh, in_specs=in_specs, out_specs=out_specs, check_vma=False)

time: 194 us -> 79.1 us (0.41)
  waiting for transfers between devices: 91.3 us -> 29 us
  blocking collectives: 31.8 us -> 0 us
  Pallas kernels: 0 us -> 28.3 us
  other arithmetic: 23.2 us -> 0.07 us
  local copies, waits for them, and re-layouts: 27.5 us -> 7.13 us
  matrix products: 8.78 us -> 0 us
  starting transfers between devices: 10.9 us -> 14.1 us
    ppermute x4 -> x9, waiting for transfers between devices: 91.3 us -> 29 us  [the longest x1 12.3 us: paired_shards(): halo1 = lax.ppermute(fields[0], 'band', outer)]
    all_to_all x2 -> x0, blocking collectives: 31.8 us -> none  [the longest x1 18.8 us: shards(): lax.all_to_all(spectra, 'comp', split_axis=2, concat_axis=0, tiled=True)]
    pallas_call x0 -> x8, Pallas kernels: none -> 28.3 us  [call(): pl.pallas_call(body, grid_spec=pltpu.PrefetchScalarGridSpec(num_scalar_pr...]
    convert_element_type x5 -> x0, other arithmetic: 14.6 us -> none  [the longest x1 6.44 us: shards(): spectra = half_one.astype(jnp.bfloat16)]
    convert_element_type x4 -> x0, local copies, waits for them, and re-layouts: 14.1 us -> none  [the longest x2 7.17 us: shards(): source = lax.all_to_all(result.reshape(block_in.shape), 'comp', split_axi...]
    dot_general x2 -> x0, matrix products: 8.78 us -> none  [the longest x1 5.86 us: source_terms(): jnp.dot(transfer_matrix, product, preferred_element_type=jnp.float32)]
    unnamed x12 -> x30, local copies, waits for them, and re-layouts: 1.52 us -> 7.13 us
    slice x8 -> x0, local copies, waits for them, and re-layouts: 5.47 us -> none  [the longest x4 2.74 us: half_step(): jnp.roll(swept, 1, axis=2)]
  transfers between devices with their start and end apart: 4 -> 9, of which waited for: 3 -> 5; matrix products, arithmetic and copies ran while one was open for 0% -> 0% of each run, Pallas kernels for 0% -> 26%
where the time goes in v1:
time: 79.1 us; the launch traced here: 78.7 us
  waiting for transfers between devices  29 us (37%)
  Pallas kernels  28.3 us (36%)
  starting transfers between devices  14.1 us (18%)
  local copies, waits for them, and re-layouts  7.13 us (9%)
    pallas_call x8, Pallas kernels, call(): pl.pallas_call(body, grid_spec=pltpu.PrefetchScalarGridSpec(num_scalar_pr...  28.3 us
    ppermute x1, waiting for transfers between devices, paired_shards(): halo1 = lax.ppermute(fields[0], 'band', outer)  12.3 us
    ppermute x2, waiting for transfers between devices, paired_shards(): rim1 = [lax.ppermute(x, 'band', outer) for x in sent0]  11.5 us
    unnamed x30, local copies, waits for them, and re-layouts  7.13 us
    ppermute x2, starting transfers between devices, paired_shards(): rim1 = [lax.ppermute(x, 'band', outer) for x in sent0]  6.61 us
    ppermute x1, starting transfers between devices, paired_shards(): halo1 = lax.ppermute(fields[0], 'band', outer)  4.46 us
    ppermute x1, waiting for transfers between devices, paired_shards(): peer1[1] = lax.ppermute(own1[1], 'comp', peers)  3.95 us
  transfers between devices with their start and end apart: 9, of which 5 were waited for; matrix products, arithmetic and copies ran while one was open for 0% of the time, Pallas kernels for 26%

profile of v1, /device:TPU:1, one launch (start us, length us, event | category | flops | bytes accessed | tf_op | source)
XLA Modules:
  0.0 78.7 jit_solution(17524893495975916070)
XLA Ops:
  0.0 0.1 pad_add_fusion.ids
  0.1 0.7 copy-done.8
  0.8 1.4 %copy-done.10 = bf16[360,2,1024]{2,1,0:T(2,128)(2,1)S(1)} copy-done((bf16[360,2,1024]{2,1,0:T(2,128)(2,1)S(1)}, bf16[360,2,1024]{2,1,0:T(2,128)(2,1)}, u32[]{:S(2)}) %copy-start.10) | copy-done | bytes 1474584
  2.1 1.7 %copy-done.13 = bf16[2,768,720]{2,1,0:T(8,128)(2,1)S(1)} copy-done((bf16[2,768,720]{2,1,0:T(8,128)(2,1)S(1)}, bf16[2,768,720]{2,1,0:T(8,128)(2,1)}, u32[]{:S(2)}) %copy-start.13) | copy-done | bytes 2211864
  3.8 1.9 %shard_map.119 = (bf16[2,184,1024]{2,1,0:T(8,128)(2,1)S(1)}, bf16[2,184,1024]{2,1,0:T(8,128)(2,1)S(1)}) custom-call(s32[2]{0:T(128)S(1)} %pad_add_fusion.ids, bf16[2,768,720]{2,1,0:T(8,128)(2,1)S(1)} %copy-done.13, bf16[360,2,1024]{2,1,0:T(2,128)(2,1)S(1)} %copy-done.10, s32[2,1024]{1,0:T(2,128)S(1)} %copy-done.8), custom_call_target="tpu_custom_call" | custom-call | flops 1132462080 | bytes 3694592 | tf_op jit(solution)/shard_map/pallas_call | solution.py:177
  5.8 0.1 collective-permute-start
  5.9 4.5 %collective-permute-start.2 = (bf16[2,184,1024]{2,1,0:T(8,128)(2,1)S(1)}, bf16[2,184,1024]{2,1,0:T(8,128)(2,1)S(1)}, u32[]{:S(2)}, u32[]{:S(2)}) collective-permute-start(bf16[2,184,1024]{2,1,0:T(8,128)(2,1)S(1)} %get-tuple-element.30.field), channel_id=1, source_target_pairs={{2,4},{4,2},{6,8},{8,6},{10,12},{12,10},{14,16},{16,14},{18,20},{2... | collective-permute-start | bytes 2261000 | tf_op jit(solution)/shard_map/ppermute | solution.py:396
  10.4 0.0 copy-start.1
  10.4 3.0 %shard_map.120 = (f32[184,1024]{1,0:T(8,128)S(1)}, f32[184,1024]{1,0:T(8,128)S(1)}, bf16[2,184,1024]{2,1,0:T(8,128)(2,1)S(1)}) custom-call(s32[2]{0:T(128)S(1)} %pad_add_fusion.ids, f32[4,2,2,184,128]{4,3,2,1,0:T(8,128)S(1)} %copy-done, f32[2,1024]{1,0:T(2,128)S(1)} %copy-done.7, s32[2,1024]{1,0:T(2,128)S(1)} %copy-done.9, ...), custom_call_target="tpu_custom_call" | custom-call | flops 15073280 | bytes 3031040 | tf_op jit(solution)/shard_map/pallas_call | solution.py:177
  13.4 0.0 copy-start.14
  13.4 1.3 %collective-permute-start.1 = (bf16[2,184,1024]{2,1,0:T(8,128)(2,1)S(1)}, bf16[2,184,1024]{2,1,0:T(8,128)(2,1)S(1)}, u32[]{:S(2)}, u32[]{:S(2)}) collective-permute-start(bf16[2,184,1024]{2,1,0:T(8,128)(2,1)S(1)} %get-tuple-element.32.own0), channel_id=1, source_target_pairs={{0,1},{1,0},{2,3},{3,2},{4,5},{5,4},{6,7},{7,6},{8,9},{9,8},{10,11... | collective-permute-start | bytes 2261000 | tf_op jit(solution)/shard_map/ppermute | solution.py:410
  14.7 12.3 %collective-permute-done.2.halo = bf16[2,184,1024]{2,1,0:T(8,128)(2,1)S(1)} collective-permute-done((bf16[2,184,1024]{2,1,0:T(8,128)(2,1)S(1)}, bf16[2,184,1024]{2,1,0:T(8,128)(2,1)S(1)}, u32[]{:S(2)}, u32[]{:S(2)}) %collective-permute-start.2) | collective-permute-done | bytes 753696 | tf_op jit(solution)/shard_map/ppermute | solution.py:396
  27.0 3.0 %shard_map.121 = (f32[184,1024]{1,0:T(8,128)S(1)}, f32[184,1024]{1,0:T(8,128)S(1)}, bf16[184,1024]{1,0:T(8,128)(2,1)S(1)}, bf16[184,1024]{1,0:T(8,128)(2,1)S(1)}) custom-call(s32[2]{0:T(128)S(1)} %pad_add_fusion.ids, f32[4,2,2,184,128]{4,3,2,1,0:T(8,128)S(1)} %copy-done, f32[2,1024]{1,0:T(2,128)S(1)} %copy-done.7, s32[2,1024]{1,0:T(2,128)S(1)} %copy-done.9, ...), custom_call_target="tpu_custom_call" | custom-call | flops 15073280 | bytes 3031040 | tf_op jit(solution)/shard_map/pallas_call | solution.py:177
  30.0 0.9 %copy-done.11 = f32[184,1024]{1,0:T(8,128)} copy-done((f32[184,1024]{1,0:T(8,128)}, f32[184,1024]{1,0:T(8,128)S(1)}, u32[]{:S(2)}) %copy-start.11) | copy-done | bytes 753688
  30.9 1.2 %collective-permute-start.4 = (bf16[184,1024]{1,0:T(8,128)(2,1)S(1)}, bf16[184,1024]{1,0:T(8,128)(2,1)S(1)}, u32[]{:S(2)}, u32[]{:S(2)}) collective-permute-start(bf16[184,1024]{1,0:T(8,128)(2,1)S(1)} %get-tuple-element.37.own1), channel_id=1, source_target_pairs={{0,1},{1,0},{2,3},{3,2},{4,5},{5,4},{6,7},{7,6},{8,9},{9,8},{10,11... | collective-permute-start | bytes 1130504 | tf_op jit(solution)/shard_map/ppermute | solution.py:422
  32.1 0.2 collective-permute-start.3
  32.4 1.2 %copy-done.5 = bf16[720,720]{1,0:T(8,128)(2,1)S(1)} copy-done((bf16[720,720]{1,0:T(8,128)(2,1)S(1)}, bf16[720,720]{1,0:T(8,128)(2,1)}, u32[]{:S(2)}) %copy-start.5) | copy-done | bytes 1036824
  33.6 1.2 %copy-done.6 = bf16[720,720]{1,0:T(8,128)(2,1)S(1)} copy-done((bf16[720,720]{1,0:T(8,128)(2,1)S(1)}, bf16[720,720]{1,0:T(8,128)(2,1)}, u32[]{:S(2)}) %copy-start.6) | copy-done | bytes 1036824
  34.8 2.9 %shard_map.118 = (bf16[736,768]{1,0:T(8,128)(2,1)S(1)}, bf16[720,768]{1,0:T(8,128)(2,1)S(1)}, bf16[384,720]{1,0:T(8,128)(2,1)S(1)}, f32[384,128]{1,0:T(8,128)S(1)}) custom-call(s32[2]{0:T(128)S(1)} %pad_add_fusion.ids, bf16[4,720,768]{2,1,0:T(8,128)(2,1)S(1)} %copy-done.1, bf16[4,384,720]{2,1,0:T(8,128)(2,1)S(1)} %copy-done.2, ...), custom_call_target="tpu_custom_call" | custom-call | flops 1990656000 | bytes 5325120 | tf_op jit(solution)/shard_map/pallas_call | solution.py:177
  37.8 4.0 %collective-permute-done.4.peer1 = bf16[184,1024]{1,0:T(8,128)(2,1)S(1)} collective-permute-done((bf16[184,1024]{1,0:T(8,128)(2,1)S(1)}, bf16[184,1024]{1,0:T(8,128)(2,1)S(1)}, u32[]{:S(2)}, u32[]{:S(2)}) %collective-permute-start.4) | collective-permute-done | bytes 376864 | tf_op jit(solution)/shard_map/ppermute | solution.py:422
  41.7 4.3 %shard_map.123 = (f32[184,1024]{1,0:T(8,128)S(1)}, bf16[184,1024]{1,0:T(8,128)(2,1)S(1)}, f32[184,1024]{1,0:T(8,128)S(1)}, bf16[184,1024]{1,0:T(8,128)(2,1)S(1)}) custom-call(s32[2]{0:T(128)S(1)} %pad_add_fusion.ids, bf16[736,768]{1,0:T(8,128)(2,1)S(1)} %get-tuple-element.26.first, bf16[720,768]{1,0:T(8,128)(2,1)S(1)} %get-tuple-element.27.second, ...), custom_call_target="tpu_custom_call" | custom-call | flops 2831155200 | bytes 6762496 | tf_op jit(solution)/shard_map/pallas_call | solution.py:177
  46.1 0.1 collective-permute-start.7
  46.1 1.2 %collective-permute-done.3.peer1 = bf16[184,1024]{1,0:T(8,128)(2,1)S(1)} collective-permute-done((bf16[184,1024]{1,0:T(8,128)(2,1)S(1)}, bf16[184,1024]{1,0:T(8,128)(2,1)S(1)}, u32[]{:S(2)}, u32[]{:S(2)}) %collective-permute-start.3) | collective-permute-done | bytes 376864 | tf_op jit(solution)/shard_map/ppermute | solution.py:423
  47.4 4.3 %shard_map.122 = (f32[184,1024]{1,0:T(8,128)S(1)}, bf16[184,1024]{1,0:T(8,128)(2,1)S(1)}, f32[184,1024]{1,0:T(8,128)S(1)}, bf16[184,1024]{1,0:T(8,128)(2,1)S(1)}) custom-call(s32[2]{0:T(128)S(1)} %pad_add_fusion.ids, bf16[736,768]{1,0:T(8,128)(2,1)S(1)} %get-tuple-element.26.first, bf16[720,768]{1,0:T(8,128)(2,1)S(1)} %get-tuple-element.27.second, ...), custom_call_target="tpu_custom_call" | custom-call | flops 2831155200 | bytes 6762496 | tf_op jit(solution)/shard_map/pallas_call | solution.py:177
  51.7 0.1 collective-permute-start.8
  51.8 4.5 %collective-permute-start.6 = (bf16[184,1024]{1,0:T(8,128)(2,1)S(1)}, bf16[184,1024]{1,0:T(8,128)(2,1)S(1)}, u32[]{:S(2)}, u32[]{:S(2)}) collective-permute-start(bf16[184,1024]{1,0:T(8,128)(2,1)S(1)} %get-tuple-element.42), channel_id=1, source_target_pairs={{2,4},{4,2},{6,8},{8,6},{10,12},{12,10},{14,16},{16,14},{18,20},{2... | collective-permute-start | bytes 1130504 | tf_op jit(solution)/shard_map/ppermute | solution.py:439
  56.3 2.1 %collective-permute-start.5 = (bf16[184,1024]{1,0:T(8,128)(2,1)S(1)}, bf16[184,1024]{1,0:T(8,128)(2,1)S(1)}, u32[]{:S(2)}, u32[]{:S(2)}) collective-permute-start(bf16[184,1024]{1,0:T(8,128)(2,1)S(1)} %get-tuple-element.41), channel_id=1, source_target_pairs={{2,4},{4,2},{6,8},{8,6},{10,12},{12,10},{14,16},{16,14},{18,20},{2... | collective-permute-start | bytes 1130504 | tf_op jit(solution)/shard_map/ppermute | solution.py:439
  58.4 0.0 copy-start.3
  58.4 3.0 %shard_map.124.rest_0_ = bf16[384,1024]{1,0:T(8,128)(2,1)S(1)} custom-call(s32[2]{0:T(128)S(1)} %pad_add_fusion.ids, f32[4,2,2,184,128]{4,3,2,1,0:T(8,128)S(1)} %copy-done, f32[2,1024]{1,0:T(2,128)S(1)} %copy-done.7, s32[2,1024]{1,0:T(2,128)S(1)} %copy-done.9, f32[184,1024]{1,0:T(8,128)S(1)} %get-tuple-element.43.u0, f32[184,1024]{1,0:T(8,128)S(1)} %get-tuple-element.44.u1, ...), custom_call_target="tpu_custom_call" | custom-call | flops 15073280 | bytes 3784704 | tf_op jit(solution)/shard_map/pallas_call | solution.py:177
  61.4 7.5 %collective-permute-done.6.h1 = bf16[184,1024]{1,0:T(8,128)(2,1)S(1)} collective-permute-done((bf16[184,1024]{1,0:T(8,128)(2,1)S(1)}, bf16[184,1024]{1,0:T(8,128)(2,1)S(1)}, u32[]{:S(2)}, u32[]{:S(2)}) %collective-permute-start.6) | collective-permute-done | bytes 376864 | tf_op jit(solution)/shard_map/ppermute | solution.py:439
  68.9 4.0 %collective-permute-done.5.h0 = bf16[184,1024]{1,0:T(8,128)(2,1)S(1)} collective-permute-done((bf16[184,1024]{1,0:T(8,128)(2,1)S(1)}, bf16[184,1024]{1,0:T(8,128)(2,1)S(1)}, u32[]{:S(2)}, u32[]{:S(2)}) %collective-permute-start.5) | collective-permute-done | bytes 376864 | tf_op jit(solution)/shard_map/ppermute | solution.py:439
  72.9 5.8 %shard_map.125 = bf16[360,2,1024]{2,1,0:T(2,128)(2,1)} custom-call(s32[2]{0:T(128)S(1)} %pad_add_fusion.ids, f32[4,2,2,184,128]{4,3,2,1,0:T(8,128)S(1)} %copy-done, f32[2,1024]{1,0:T(2,128)S(1)} %copy-done.7, s32[2,1024]{1,0:T(2,128)S(1)} %copy-done.9, f32[184,1024]{1,0:T(8,128)S(1)} %get-tuple-element.36.u0, f32[184,1024]{1,0:T(8,128)S(1)} %get-tuple-element.40.u1, ...), custom_call_target="tpu_custom_call" | custom-call | flops 15073280 | bytes 6782976 | tf_op jit(solution)/shard_map/pallas_call | solution.py:177
  (26 shorter events, 0.1 us)
Async XLA Ops:
  0.1 0.7 copy-start.8
  0.8 1.4 %copy-start.10 = (bf16[360,2,1024]{2,1,0:T(2,128)(2,1)S(1)}, bf16[360,2,1024]{2,1,0:T(2,128)(2,1)}, u32[]{:S(2)}) copy-start(bf16[360,2,1024]{2,1,0:T(2,128)(2,1)} %energy.1) | copy-start | bytes 4423684
  2.1 1.7 %copy-start.13 = (bf16[2,768,720]{2,1,0:T(8,128)(2,1)S(1)}, bf16[2,768,720]{2,1,0:T(8,128)(2,1)}, u32[]{:S(2)}) copy-start(bf16[2,768,720]{2,1,0:T(8,128)(2,1)} %constant.31.clone.regroup) | copy-start | bytes 6635524
  3.8 6.6 %copy-start = (f32[4,2,2,184,128]{4,3,2,1,0:T(8,128)S(1)}, f32[4,2,2,184,128]{4,3,2,1,0:T(8,128)}, u32[]{:S(2)}) copy-start(f32[4,2,2,184,128]{4,3,2,1,0:T(8,128)} %constant.32.clone.courant) | copy-start | bytes 4521988
  3.8 6.6 %copy-start.7 = (f32[2,1024]{1,0:T(2,128)S(1)}, f32[2,1024]{1,0:T(2,128)}, u32[]{:S(2)}) copy-start(f32[2,1024]{1,0:T(2,128)} %depth.7) | copy-start | bytes 24580
  3.8 6.6 %copy-start.9 = (s32[2,1024]{1,0:T(2,128)S(1)}, s32[2,1024]{1,0:T(2,128)}, u32[]{:S(2)}) copy-start(s32[2,1024]{1,0:T(2,128)} %mask.13) | copy-start | bytes 24580
  3.8 28.5 %copy-start.2 = (bf16[4,384,720]{2,1,0:T(8,128)(2,1)S(1)}, bf16[4,384,720]{2,1,0:T(8,128)(2,1)}, u32[]{:S(2)}) copy-start(bf16[4,384,720]{2,1,0:T(8,128)(2,1)} %constant.34.clone.rows_of) | copy-start | bytes 6635524
  5.8 4.6 %collective-permute-start = (bf16[2,184,1024]{2,1,0:T(8,128)(2,1)S(1)}, bf16[2,184,1024]{2,1,0:T(8,128)(2,1)S(1)}, u32[]{:S(2)}, u32[]{:S(2)}) collective-permute-start(bf16[2,184,1024]{2,1,0:T(8,128)(2,1)S(1)} %get-tuple-element.31.field), channel_id=1, source_target_pairs={{0,2},{2,0},{4,6},{6,4},{8,10},{10,8},{12,14},{14,12},{16,18},{18,... | collective-permute-start | bytes 2261000 | tf_op jit(solution)/shard_map/ppermute | solution.py:395
  5.9 21.1 %collective-permute-start.2 = (bf16[2,184,1024]{2,1,0:T(8,128)(2,1)S(1)}, bf16[2,184,1024]{2,1,0:T(8,128)(2,1)S(1)}, u32[]{:S(2)}, u32[]{:S(2)}) collective-permute-start(bf16[2,184,1024]{2,1,0:T(8,128)(2,1)S(1)} %get-tuple-element.30.field), channel_id=1, source_target_pairs={{2,4},{4,2},{6,8},{8,6},{10,12},{12,10},{14,16},{16,14},{18,20},{2... | collective-permute-start | bytes 2261000 | tf_op jit(solution)/shard_map/ppermute | solution.py:396
  10.4 21.9 %copy-start.1 = (bf16[4,720,768]{2,1,0:T(8,128)(2,1)S(1)}, bf16[4,720,768]{2,1,0:T(8,128)(2,1)}, u32[]{:S(2)}) copy-start(bf16[4,720,768]{2,1,0:T(8,128)(2,1)} %constant.33.clone.columns) | copy-start | bytes 13271044
  13.4 18.7 %copy-start.14 = (f32[720]{0:T(1024)S(1)}, f32[720]{0:T(1024)}, u32[]{:S(2)}) copy-start(f32[720]{0:T(1024)} %param.18) | copy-start | bytes 8644
  13.4 18.9 %copy-start.4 = (bf16[720,720]{1,0:T(8,128)(2,1)S(1)}, bf16[720,720]{1,0:T(8,128)(2,1)}, u32[]{:S(2)}) copy-start(bf16[720,720]{1,0:T(8,128)(2,1)} %first.1) | copy-start | bytes 3110404
  13.4 28.3 %collective-permute-start.1 = (bf16[2,184,1024]{2,1,0:T(8,128)(2,1)S(1)}, bf16[2,184,1024]{2,1,0:T(8,128)(2,1)S(1)}, u32[]{:S(2)}, u32[]{:S(2)}) collective-permute-start(bf16[2,184,1024]{2,1,0:T(8,128)(2,1)S(1)} %get-tuple-element.32.own0), channel_id=1, source_target_pairs={{0,1},{1,0},{2,3},{3,2},{4,5},{5,4},{6,7},{7,6},{8,9},{9,8},{10,11... | collective-permute-start | bytes 2261000 | tf_op jit(solution)/shard_map/ppermute | solution.py:410
  30.0 0.9 %copy-start.11 = (f32[184,1024]{1,0:T(8,128)}, f32[184,1024]{1,0:T(8,128)S(1)}, u32[]{:S(2)}) copy-start(f32[184,1024]{1,0:T(8,128)S(1)} %get-tuple-element.35.half1) | copy-start | bytes 2260996
  30.9 10.8 %collective-permute-start.4 = (bf16[184,1024]{1,0:T(8,128)(2,1)S(1)}, bf16[184,1024]{1,0:T(8,128)(2,1)S(1)}, u32[]{:S(2)}, u32[]{:S(2)}) collective-permute-start(bf16[184,1024]{1,0:T(8,128)(2,1)S(1)} %get-tuple-element.37.own1), channel_id=1, source_target_pairs={{0,1},{1,0},{2,3},{3,2},{4,5},{5,4},{6,7},{7,6},{8,9},{9,8},{10,11... | collective-permute-start | bytes 1130504 | tf_op jit(solution)/shard_map/ppermute | solution.py:422
  32.1 15.2 %collective-permute-start.3 = (bf16[184,1024]{1,0:T(8,128)(2,1)S(1)}, bf16[184,1024]{1,0:T(8,128)(2,1)S(1)}, u32[]{:S(2)}, u32[]{:S(2)}) collective-permute-start(bf16[184,1024]{1,0:T(8,128)(2,1)S(1)} %get-tuple-element.33.own1), channel_id=1, source_target_pairs={{0,1},{1,0},{2,3},{3,2},{4,5},{5,4},{6,7},{7,6},{8,9},{9,8},{10,11... | collective-permute-start | bytes 1130504 | tf_op jit(solution)/shard_map/ppermute | solution.py:423
  32.4 1.2 %copy-start.5 = (bf16[720,720]{1,0:T(8,128)(2,1)S(1)}, bf16[720,720]{1,0:T(8,128)(2,1)}, u32[]{:S(2)}) copy-start(bf16[720,720]{1,0:T(8,128)(2,1)} %second.1) | copy-start | bytes 3110404
  33.6 1.2 %copy-start.6 = (bf16[720,720]{1,0:T(8,128)(2,1)S(1)}, bf16[720,720]{1,0:T(8,128)(2,1)}, u32[]{:S(2)}) copy-start(bf16[720,720]{1,0:T(8,128)(2,1)} %transfer.1) | copy-start | bytes 3110404
  41.7 5.6 %copy-start.12 = (f32[184,1024]{1,0:T(8,128)S(1)}, f32[184,1024]{1,0:T(8,128)}, u32[]{:S(2)}) copy-start(f32[184,1024]{1,0:T(8,128)} %copy-done.11) | copy-start | bytes 2260996
  46.1 12.3 %collective-permute-start.7 = (bf16[184,1024]{1,0:T(8,128)(2,1)S(1)}, bf16[184,1024]{1,0:T(8,128)(2,1)S(1)}, u32[]{:S(2)}, u32[]{:S(2)}) collective-permute-start(bf16[184,1024]{1,0:T(8,128)(2,1)S(1)} %get-tuple-element.45), channel_id=1, source_target_pairs={{0,2},{2,0},{4,6},{6,4},{8,10},{10,8},{12,14},{14,12},{16,18},{18,... | collective-permute-start | bytes 1130504 | tf_op jit(solution)/shard_map/ppermute | solution.py:440
  51.7 6.7 %collective-permute-start.8 = (bf16[184,1024]{1,0:T(8,128)(2,1)S(1)}, bf16[184,1024]{1,0:T(8,128)(2,1)S(1)}, u32[]{:S(2)}, u32[]{:S(2)}) collective-permute-start(bf16[184,1024]{1,0:T(8,128)(2,1)S(1)} %get-tuple-element.46), channel_id=1, source_target_pairs={{0,2},{2,0},{4,6},{6,4},{8,10},{10,8},{12,14},{14,12},{16,18},{18,... | collective-permute-start | bytes 1130504 | tf_op jit(solution)/shard_map/ppermute | solution.py:440
  51.8 17.1 %collective-permute-start.6 = (bf16[184,1024]{1,0:T(8,128)(2,1)S(1)}, bf16[184,1024]{1,0:T(8,128)(2,1)S(1)}, u32[]{:S(2)}, u32[]{:S(2)}) collective-permute-start(bf16[184,1024]{1,0:T(8,128)(2,1)S(1)} %get-tuple-element.42), channel_id=1, source_target_pairs={{2,4},{4,2},{6,8},{8,6},{10,12},{12,10},{14,16},{16,14},{18,20},{2... | collective-permute-start | bytes 1130504 | tf_op jit(solution)/shard_map/ppermute | solution.py:439
  56.3 16.6 %collective-permute-start.5 = (bf16[184,1024]{1,0:T(8,128)(2,1)S(1)}, bf16[184,1024]{1,0:T(8,128)(2,1)S(1)}, u32[]{:S(2)}, u32[]{:S(2)}) collective-permute-start(bf16[184,1024]{1,0:T(8,128)(2,1)S(1)} %get-tuple-element.41), channel_id=1, source_target_pairs={{2,4},{4,2},{6,8},{8,6},{10,12},{12,10},{14,16},{16,14},{18,20},{2... | collective-permute-start | bytes 1130504 | tf_op jit(solution)/shard_map/ppermute | solution.py:439
  58.4 14.5 %copy-start.3 = (bf16[2,720,768]{2,1,0:T(8,128)(2,1)S(1)}, bf16[2,720,768]{2,1,0:T(8,128)(2,1)}, u32[]{:S(2)}) copy-start(bf16[2,720,768]{2,1,0:T(8,128)(2,1)} %constant.35.clone.rest_1_) | copy-start | bytes 6635524

commit v2 on v1

v2 whole, which is shorter than its diff:
```python
import functools
import math

import jax
import jax.numpy as jnp
from jax import lax
from jax.experimental import pallas as pl
from jax.experimental.pallas import tpu as pltpu
from jax.sharding import PartitionSpec as P

ND = 24


SOURCE_STEP = 0.5
COURANT_TOP = 0.9
FREQ_RATIO = 1.1

F32 = jnp.float32
BF16 = jnp.bfloat16


def with_halo(value, sides, width):
    for axis, dim in sides:
        peers, length = (lax.axis_size(axis), value.shape[dim])
        up = [(i, (i + 1) % peers) for i in range(peers - 1)]
        down = [(j, i) for i, j in up]
        last = lax.slice_in_dim(value, length - width, length, axis=dim)
        first = lax.slice_in_dim(value, 0, width, axis=dim)
        before = lax.ppermute(last, axis, up)
        after = lax.ppermute(first, axis, down)
        value = jnp.concatenate([before, value, after], axis=dim)
    return value


def courant_numbers(first_comp, local_comps):
    components = first_comp + jnp.arange(local_comps, dtype=jnp.int32)
    frequency = (components // ND).astype(jnp.float32)
    direction = (components % ND).astype(jnp.float32)
    heading = 2.0 * jnp.pi * (direction + 0.5) / ND
    factor = COURANT_TOP * jnp.power(jnp.float32(FREQ_RATIO), -frequency)
    return (factor * jnp.cos(heading), factor * jnp.sin(heading))


def upwind(middle, lower_one, lower_two, upper_one, upper_two, courant):
    magnitude = jnp.abs(courant)
    first_up = jnp.where(courant > 0, lower_one, upper_one)
    second_up = jnp.where(courant > 0, lower_two, upper_two)
    return (
        middle
        - 0.5 * magnitude * (3.0 * middle - 4.0 * first_up + second_up)
        + 0.5 * magnitude * magnitude * (middle - 2.0 * first_up + second_up)
    )


def half_step(extended, lat_courant, lon_courant, depth_speed, ocean):
    widened = extended.astype(jnp.float32)
    swept = upwind(
        widened[:, 2:-2],
        widened[:, 1:-3],
        widened[:, :-4],
        widened[:, 3:-1],
        widened[:, 4:],
        lat_courant[:, None, None] * depth_speed[None],
    )
    lon_values = lon_courant[:, None, None] * depth_speed[None]
    swept = upwind(
        swept,
        jnp.roll(swept, 1, axis=2),
        jnp.roll(swept, 2, axis=2),
        jnp.roll(swept, -1, axis=2),
        jnp.roll(swept, -2, axis=2),
        lon_values,
    )
    return ocean[None] * swept


def source_terms(cell_spectra, interp_first, interp_second, transfer_matrix, growth):
    forward_interp = jnp.dot(interp_first, cell_spectra, preferred_element_type=jnp.float32)
    backward_interp = jnp.dot(interp_second, cell_spectra, preferred_element_type=jnp.float32)
    product = (forward_interp * backward_interp).astype(jnp.bfloat16)
    nonlinear = jnp.dot(transfer_matrix, product, preferred_element_type=jnp.float32)
    spectra32 = cell_spectra.astype(jnp.float32)
    mean_level = jnp.mean(spectra32, axis=0)
    damping = mean_level * mean_level / (1.0 + mean_level * mean_level)
    total = SOURCE_STEP * (nonlinear + (growth[:, None] - damping[None]) * spectra32)
    return total.astype(jnp.bfloat16)


def general_shards(energy, depth_speed, ocean_mask, interp_first, interp_second, transfer_matrix, growth):
    local_comps = energy.shape[0]
    lat_courant, lon_courant = courant_numbers(lax.axis_index("comp") * local_comps, local_comps)
    ocean = ocean_mask.astype(jnp.float32)
    start = (ocean[None] * energy.astype(jnp.float32)).astype(jnp.bfloat16)
    rimmed = with_halo(start, (("band", 1),), 2)
    half_one = half_step(rimmed, lat_courant, lon_courant, depth_speed, ocean)
    spectra = half_one.astype(jnp.bfloat16)
    block_in = lax.all_to_all(spectra, "comp", split_axis=2, concat_axis=0, tiled=True)
    total_comps = block_in.shape[0]
    flat_cells = block_in.reshape(total_comps, -1)
    result = source_terms(flat_cells, interp_first, interp_second, transfer_matrix, growth)
    source = lax.all_to_all(
        result.reshape(block_in.shape), "comp", split_axis=0, concat_axis=2, tiled=True
    ).astype(jnp.float32)
    updated = ocean[None] * (half_one + source)
    rimmed_mid = with_halo(updated, (("band", 1),), 2)
    final_field = half_step(rimmed_mid, lat_courant, lon_courant, depth_speed, ocean)
    return final_field.astype(jnp.bfloat16)


class Plan:
    def __init__(self, local_comps, columns):
        self.local = local_comps
        self.total = 2 * local_comps
        self.columns = columns
        self.half = local_comps // 4
        self.slots = 2 * self.half
        self.rows = -(-self.slots // 8) * 8
        self.pitch = -(-self.slots // 16) * 16
        self.out_rows = -(-(self.total + 1) // 16) * 16

    def slot_parts(self, slot):
        east = slot < self.half
        j = jnp.where(east, slot, slot - self.half)
        f = (j * 10923) >> 16
        return east, f, j - 6 * f

    def courant(self, ids, group):
        east, f, turn = self.slot_parts(lax.broadcasted_iota(jnp.int32, (self.rows, 128), 0))
        factor = jnp.where(ids[1] >= 2, COURANT_TOP * FREQ_RATIO ** -(self.local // ND), COURANT_TOP).astype(F32)
        for bit in range(self.local.bit_length()):
            if 1 << bit < self.local // ND:
                factor = factor * jnp.where((f >> bit) & 1 == 1, FREQ_RATIO ** -(1 << bit), 1.0)
        falling = east == jnp.logical_not(southward(ids, group))
        place = jnp.where(falling, turn, 5 - turn)
        cosine, sine = factor, factor
        for i in range(6):
            cosine = jnp.where(place == i, factor * math.cos(2 * math.pi * (i + 0.5) / ND), cosine)
            sine = jnp.where(place == i, factor * math.sin(2 * math.pi * (i + 0.5) / ND), sine)
        return cosine, sine

    def slot_comp(self, slot, south):
        east, f, turn = self.slot_parts(slot)
        comp = ND * f + turn + jnp.where(east, jnp.where(south, 6, 0), jnp.where(south, 12, 18))
        return jnp.where(slot < self.slots, comp, -4 * self.total)


def southward(ids, group):
    return ids[0] == group


def actual_row(r, south):
    return jnp.where(south, 1 - r, r)


def one_hot(match):
    return jnp.where(match, 1.0, 0.0).astype(BF16)


def spread(value, width):
    parts = [value] * (width // 128)
    if width % 128:
        parts.append(value[:, : width % 128])
    return jnp.concatenate(parts, axis=1)


VMEM = pl.BlockSpec(memory_space=pltpu.VMEM)
SMEM = pl.BlockSpec(memory_space=pltpu.SMEM)


def call(body, ids, operands, outs, scratch=(), limit=40, cost=1.0):
    return pl.pallas_call(
        body,
        in_specs=[SMEM] + [VMEM] * len(operands),
        out_specs=[VMEM] * len(outs),
        scratch_shapes=list(scratch),
        out_shape=outs,
        compiler_params=pltpu.CompilerParams(vmem_limit_bytes=int(limit * 2**20)),
        cost_estimate=pl.CostEstimate(flops=int(cost * 1.1e9), bytes_accessed=0, transcendentals=0),
    )(ids, *operands)


def in_order(ids, value, group):
    south = southward(ids, group)
    one, two = value[0:1], value[1:2]
    return jnp.where(south, two, one), jnp.where(south, one, two)


def prep_body(plan, ids, energy, mask, field0, field1, courant, regroup):
    for group in range(2):
        courant[group, 0], courant[group, 1] = plan.courant(ids, group)
    width, pitch = 2 * plan.local, plan.pitch
    column = lax.broadcasted_iota(jnp.int32, (pitch, width), 1)
    for group in range(2):
        south = southward(ids, group)
        comp = plan.slot_comp(lax.broadcasted_iota(jnp.int32, (pitch, 128), 0), south)
        for r in range(2):
            begin = (2 * group + r) * pitch
            regroup[begin : begin + pitch] = one_hot(spread(2 * comp + actual_row(r, south), width) == column)
    ocean = mask[...].astype(F32)
    flat = energy[...].reshape(width, plan.columns)
    moved = jnp.dot(regroup[...], flat, preferred_element_type=F32)
    for group, field in enumerate((field0, field1)):
        rows = in_order(ids, ocean, group)
        for r in range(2):
            at = (2 * group + r) * pitch
            field[r] = (moved[at : at + plan.rows] * rows[r]).astype(BF16)


def sweep(u, p, q, a):
    d = p - u
    e = (q - p) - d
    return u + a * (d + (0.5 * a - 0.5) * e)


def lon_sweep(u, a, shift, size):
    def back(x):
        return pltpu.roll(x, shift % size, 1)

    d = back(u) - u
    e = back(d) - d
    return u + a * (d + (0.5 * a - 0.5) * e)


def half_steps(plan, group, ids, courant, depth, mask, depth8, ocean8, load, store):
    size = plan.columns
    for r, row in enumerate(in_order(ids, depth[...], group)):
        depth8[r] = jnp.broadcast_to(row, (8, size))
    for r, row in enumerate(in_order(ids, mask[...].astype(F32), group)):
        ocean8[r] = jnp.broadcast_to(row, (8, size))

    def block(start, rows, side):
        u0, u1, h0, h1 = load(start, rows)
        c_lat = courant[group, 0, pl.ds(start, rows)]
        c_lon = courant[group, 1, pl.ds(start, rows)]
        news = ([], [])
        for s in range(0, rows, 8):
            part = slice(s, s + 8)
            lat, lon = spread(c_lat[part], size), spread(c_lon[part], size)
            stencil = ((u0[part], h0[part], h1[part]), (u1[part], u0[part], h0[part]))
            for r in range(2):
                dep = depth8[r]
                u = sweep(*stencil[r], lat * dep)
                a = lon * dep
                if side == 0:
                    at = lax.broadcasted_iota(jnp.int32, (8, size), 0) + (start + s)
                    u = jnp.where(at < plan.half, lon_sweep(u, a, 1, size), lon_sweep(u, a, -1, size))
                else:
                    u = lon_sweep(u, a, side, size)
                news[r].append(u * ocean8[r])
        store(start, rows, jnp.concatenate(news[0], axis=0), jnp.concatenate(news[1], axis=0))

    east = plan.half // 16
    west = -(-plan.half // 16)
    full = plan.rows // 16

    @pl.loop(0, east, unroll=2)
    def _(i):
        block(pl.multiple_of(i * 16, 16), 16, 1)

    for i in range(east, west):
        block(i * 16, 16, 0)

    @pl.loop(west, full, unroll=2)
    def _(i):
        block(pl.multiple_of(i * 16, 16), 16, -1)

    if plan.rows % 16:
        block(full * 16, plan.rows % 16, -1)


def first_body(plan, group, ids, courant, depth, mask, field, halo, *rest):
    half, spectra, (depth8, ocean8) = rest[:2], rest[2:-2], rest[-2:]

    def load(start, rows):
        at = pl.ds(start, rows)
        return tuple(ref[r, at].astype(F32) for ref, r in ((field, 0), (field, 1), (halo, 1), (halo, 0)))

    def store(start, rows, new0, new1):
        at = pl.ds(start, rows)
        for r, new in enumerate((new0, new1)):
            half[r][at] = new
            if len(spectra) == 1:
                spectra[0][r, at] = new.astype(BF16)
            else:
                spectra[r][at] = new.astype(BF16)

    half_steps(plan, group, ids, courant, depth, mask, depth8, ocean8, load, store)


def last_body(plan, group, ids, courant, depth, mask, u0, u1, h0, h1, *rest):
    *rest, done, depth8, ocean8 = rest
    width, pitch = 2 * plan.local, plan.pitch

    def load(start, rows):
        at = pl.ds(start, rows)
        return tuple(ref[at].astype(F32) for ref in (u0, u1, h0, h1))

    def store(start, rows, new0, new1):
        for r, new in enumerate((new0, new1)):
            at = r * pitch + start
            if rows < 16:
                new = jnp.concatenate([new, jnp.zeros((16 - rows, plan.columns), F32)], axis=0)
            done[pl.ds(pl.multiple_of(at, 16), 16)] = new.astype(BF16)

    half_steps(plan, group, ids, courant, depth, mask, depth8, ocean8, load, store)
    if group == 0:
        partial, restore = rest
        tables = []
        for g in range(2):
            lane = lax.broadcasted_iota(jnp.int32, (8, 2 * pitch), 1)
            r = jnp.where(lane >= pitch, 1, 0)
            south = southward(ids, g)
            target = 2 * plan.slot_comp(lane - pitch * r, south) + actual_row(r, south)
            target = jnp.concatenate([target] * (width // 8), axis=0)
            tables.append(one_hot(target == lax.broadcasted_iota(jnp.int32, (width, 2 * pitch), 0)))
        restore[...] = tables[1]
        partial[...] = jnp.dot(tables[0], done[...], preferred_element_type=F32)
    else:
        partial, restore, out = rest
        flat = partial[...] + jnp.dot(restore[...], done[...], preferred_element_type=F32)
        out[...] = flat.astype(BF16).reshape(plan.local, 2, plan.columns)


def weights_body(plan, ids, first, second, transfer, growth, first_out, second_out, transfer_out, growth_out, columns):
    total, local, pitch = plan.total, plan.local, plan.pitch
    comp_index = ids[1] // 2
    chosen = []
    for group in range(2):
        south = southward(ids, group)
        lane = lax.broadcasted_iota(jnp.int32, (8, 2 * pitch), 1)
        other = jnp.where(lane >= pitch, 1, 0)
        owner = jnp.where(other == 0, comp_index, 1 - comp_index)
        source = plan.slot_comp(lane - pitch * other, south) + local * owner
        source = jnp.concatenate([source] * (total // 8), axis=0)
        hot = one_hot(source == lax.broadcasted_iota(jnp.int32, (total, 2 * pitch), 0))
        columns[:, 2 * group * pitch : 2 * (group + 1) * pitch] = hot
        comp = plan.slot_comp(lax.broadcasted_iota(jnp.int32, (pitch, 128), 0), south) + local * comp_index
        chosen.append(spread(comp, total) == lax.broadcasted_iota(jnp.int32, (pitch, total), 1))
    first_out[:total] = jnp.dot(first[...], columns[...], preferred_element_type=F32).astype(BF16)
    extra = plan.out_rows - total
    first_out[total:] = one_hot(lax.broadcasted_iota(jnp.int32, (extra, 4 * pitch), 0) == 0)
    second_out[...] = jnp.dot(second[...], columns[...], preferred_element_type=F32).astype(BF16)
    for group in range(2):
        at = slice(group * pitch, (group + 1) * pitch)
        pick = jnp.where(chosen[group], 1.0, 0.0)
        transfer_out[at] = jnp.dot(pick.astype(BF16), transfer[...], preferred_element_type=F32).astype(BF16)
        rate = jnp.sum(pick * growth[...], axis=1, keepdims=True)
        growth_out[at] = jnp.broadcast_to(rate, (pitch, 128))


TILE = 256


def fill_cells(plan, cells, blocks):
    rows, pitch = plan.rows, plan.pitch
    for i, block in enumerate(blocks):
        whole_rows = rows // 16 * 16
        cells[i * pitch : i * pitch + whole_rows] = block[:whole_rows]
        if whole_rows < pitch:
            tail = block[whole_rows:].astype(F32)
            tail = jnp.concatenate([tail, jnp.zeros((pitch - rows, plan.columns), F32)], axis=0)
            cells[i * pitch + whole_rows : (i + 1) * pitch] = tail.astype(BF16)


def early_body(plan, ids, first, second, own0, peer0, own1_0, own1_1, *rest):
    outs, cells = rest[:4], rest[4]
    own1 = (own1_0, own1_1)
    known = 3 * plan.pitch
    for turn in range(2):
        fill_cells(plan, cells, (own0[turn], peer0[turn], own1[1 - turn][...]))
        for c in range(0, plan.columns, TILE):
            at = slice(c, c + TILE)
            outs[2 * turn][:, at] = jnp.dot(first[:, :known], cells[:, at], preferred_element_type=F32)
            outs[2 * turn + 1][:, at] = jnp.dot(second[:, :known], cells[:, at], preferred_element_type=F32)


def source_body(plan, turn, ids, first, second, transfer, growth, mask, *rest):
    (early_first, early_second, own0, own1, peer1, half0, half1, full0, sent0, full1, sent1, cells) = rest
    total, rows, pitch = plan.total, plan.rows, plan.pitch
    known = 3 * pitch
    fill_cells(plan, cells, (peer1[...],))
    ocean = in_order(ids, mask[...].astype(F32), 0)[turn]
    for c in range(0, plan.columns, TILE):
        at = slice(c, c + TILE)
        piece = cells[:, at]
        forward = early_first[:, at] + jnp.dot(first[:, known:], piece, preferred_element_type=F32)
        backward = early_second[:, at] + jnp.dot(second[:, known:], piece, preferred_element_type=F32)
        product = (forward[:total] * backward).astype(BF16)
        nonlinear = jnp.dot(transfer[...], product, preferred_element_type=F32)
        level = forward[total : total + 1] / total
        damping = level * level / (1.0 + level * level)
        for group, (own, half, full, sent) in enumerate(((own0, half0, full0, sent0), (own1, half1, full1, sent1))):
            begin = group * pitch
            rate = spread(growth[begin : begin + rows], TILE)
            spectra = (own[turn, :, at] if group == 0 else own[:, at]).astype(F32)
            source = SOURCE_STEP * (nonlinear[begin : begin + rows] + (rate - damping) * spectra)
            updated = ocean[:, at] * (half[:, at] + source.astype(BF16).astype(F32))
            full[:, at] = updated
            sent[:, at] = updated.astype(BF16)


def paired_shards(energy, depth_speed, ocean_mask, interp_first, interp_second, transfer_matrix, growth):
    plan = Plan(energy.shape[0], energy.shape[2])
    size, rows, pitch, total = plan.columns, plan.rows, plan.pitch, plan.total
    bands = lax.axis_size("band")
    parity = lax.axis_index("band") % 2
    ids = jnp.stack([parity, 2 * lax.axis_index("comp") + parity]).astype(jnp.int32)

    inner = [(i, i ^ 1) for i in range(bands)]
    outer = [(i, j) for i in range(1, bands - 1) for j in [i + 1 if i % 2 else i - 1]]
    peers = [(0, 1), (1, 0)]

    def shape(*dims, kind=BF16):
        return jax.ShapeDtypeStruct(dims, kind)

    rims = [pltpu.VMEM((2, 8, size), F32)] * 2

    field0, field1, courant = call(
        functools.partial(prep_body, plan),
        ids,
        (energy, ocean_mask),
        [shape(2, rows, size)] * 2 + [shape(2, 2, rows, 128, kind=F32)],
        [pltpu.VMEM((4 * pitch, 2 * plan.local), BF16)],
        cost=2,
    )
    halo0 = lax.ppermute(field1, "band", inner)
    halo1 = lax.ppermute(field0, "band", outer)

    def first_step(group, field, halo, spectra):
        operands = (courant, depth_speed, ocean_mask, field, halo)
        outs = [shape(rows, size, kind=F32)] * 2 + spectra
        return call(functools.partial(first_body, plan, group), ids, operands, outs, rims, limit=20, cost=2)

    *half0, own0 = first_step(0, field0, halo0, [shape(2, rows, size)])
    peer0 = lax.ppermute(own0, "comp", peers)
    first, second, transfer, rate = call(
        functools.partial(weights_body, plan),
        ids,
        (interp_first, interp_second, transfer_matrix, growth.reshape(1, total)),
        [shape(plan.out_rows, 4 * pitch), shape(total, 4 * pitch), shape(2 * pitch, total), shape(2 * pitch, 128, kind=F32)],
        [pltpu.VMEM((total, 4 * pitch), BF16)],
        cost=3,
    )
    *half1, own1_0, own1_1 = first_step(1, field1, halo1, [shape(rows, size)] * 2)
    own1 = (own1_0, own1_1)
    peer1 = [None, None]
    peer1[1] = lax.ppermute(own1[1], "comp", peers)
    peer1[0] = lax.ppermute(own1[0], "comp", peers)
    early = call(
        functools.partial(early_body, plan),
        ids,
        (first, second, own0, peer0, own1_0, own1_1),
        [shape(plan.out_rows, size, kind=F32), shape(total, size, kind=F32)] * 2,
        [pltpu.VMEM((3 * pitch, size), BF16)],
        limit=30,
        cost=4,
    )

    full0, sent0, full1, sent1 = [None] * 2, [None] * 2, [None] * 2, [None] * 2
    for turn in range(2):
        full0[turn], sent0[turn], full1[1 - turn], sent1[1 - turn] = call(
            functools.partial(source_body, plan, turn),
            ids,
            (first, second, transfer, rate, ocean_mask, early[2 * turn], early[2 * turn + 1])
            + (own0, own1[1 - turn], peer1[1 - turn], half0[turn], half1[1 - turn]),
            [shape(rows, size, kind=F32), shape(rows, size)] * 2,
            [pltpu.VMEM((pitch, size), BF16)],
            limit=30,
            cost=4,
        )
    rim1 = [lax.ppermute(x, "band", outer) for x in sent0]
    rim0 = [lax.ppermute(x, "band", inner) for x in sent1]

    def last_step(group, full, rim, more, outs, cost):
        operands = (courant, depth_speed, ocean_mask, full[0], full[1], rim[1], rim[0]) + more
        scratch = [pltpu.VMEM((2 * pitch, size), BF16)] + rims
        return call(functools.partial(last_body, plan, group), ids, operands, outs, scratch, limit=30, cost=cost)

    width = 2 * plan.local
    full0[0], rim1[0] = lax.optimization_barrier((full0[0], rim1[0]))
    more = last_step(0, full0, rim0, (), [shape(width, size, kind=F32), shape(width, 2 * pitch)], 3)
    (out,) = last_step(1, full1, rim1, tuple(more), [shape(*energy.shape)], 4)
    return out


def solution(mesh):
    def shards(energy, *others):
        paired = lax.axis_size("comp") == 2 and lax.axis_size("band") % 2 == 0
        if paired and energy.shape[0] % ND == 0 and energy.shape[1] == 2 and energy.shape[2] % TILE == 0:
            return paired_shards(energy, *others)
        return general_shards(energy, *others)

    in_specs = (P("comp", "band", None), P("band", None), P("band", None), P(), P(), P(), P())
    out_specs = P("comp", "band", None)
    return jax.shard_map(shards, mesh=mesh, in_specs=in_specs, out_specs=out_specs, check_vma=False)
```

time: 79.1 us -> 67.1 us (0.85)
  the two profiles are of different devices: /device:TPU:1 before, /device:TPU:9 now
where the time goes in v2:
time: 67.1 us; the launch traced here: 66.8 us
  Pallas kernels  28.1 us (42%)
  waiting for transfers between devices  23.2 us (35%)
  starting transfers between devices  13.2 us (20%)
  local copies, waits for them, and re-layouts  2.11 us (3%)
    pallas_call x9, Pallas kernels, call(): pl.pallas_call(body, in_specs=[SMEM] + [VMEM] * len(operands), out_specs=...  28.1 us
    ppermute x1, waiting for transfers between devices, paired_shards(): halo1 = lax.ppermute(field0, 'band', outer)  11.5 us
    ppermute x2, waiting for transfers between devices, paired_shards(): rim1 = [lax.ppermute(x, 'band', outer) for x in sent0]  7.57 us
    ppermute x2, starting transfers between devices, paired_shards(): rim1 = [lax.ppermute(x, 'band', outer) for x in sent0]  6 us
    ppermute x1, waiting for transfers between devices, paired_shards(): peer1[1] = lax.ppermute(own1[1], 'comp', peers)  4.05 us
    ppermute x1, starting transfers between devices, paired_shards(): halo1 = lax.ppermute(field0, 'band', outer)  3.03 us
    unnamed x16, local copies, waits for them, and re-layouts  2.1 us
  transfers between devices with their start and end apart: 9, of which 3 were waited for; matrix products, arithmetic and copies ran while one was open for 0% of the time, Pallas kernels for 32%

profile of v2, /device:TPU:9, one launch (start us, length us, event | category | flops | bytes accessed | tf_op | source)
XLA Modules:
  0.0 66.8 jit_solution(3572703151696347645)
XLA Ops:
  0.0 0.1 pad_add_fusion.ids
  0.1 1.4 %copy-done = bf16[360,2,1024]{2,1,0:T(2,128)(2,1)S(1)} copy-done((bf16[360,2,1024]{2,1,0:T(2,128)(2,1)S(1)}, bf16[360,2,1024]{2,1,0:T(2,128)(2,1)}, u32[]{:S(2)}) %copy-start) | copy-done | bytes 1474584
  1.5 0.7 %copy-done.4 = s32[2,1024]{1,0:T(2,128)S(1)} copy-done((s32[2,1024]{1,0:T(2,128)S(1)}, s32[2,1024]{1,0:T(2,128)}, u32[]{:S(2)}) %copy-start.4) | copy-done | bytes 8216
  2.1 2.2 %shard_map.73 = (bf16[2,184,1024]{2,1,0:T(8,128)(2,1)S(1)}, bf16[2,184,1024]{2,1,0:T(8,128)(2,1)S(1)}, f32[2,2,184,128]{3,2,1,0:T(8,128)S(1)}) custom-call(s32[2]{0:T(128)S(1)} %pad_add_fusion.ids, bf16[360,2,1024]{2,1,0:T(2,128)(2,1)S(1)} %copy-done, s32[2,1024]{1,0:T(2,128)S(1)} %copy-done.4), custom_call_target="tpu_custom_call" | custom-call | flops 2200000000 | tf_op jit(solution)/shard_map/pallas_call | solution.py:171
  4.4 0.7 %collective-permute-start = (bf16[2,184,1024]{2,1,0:T(8,128)(2,1)S(1)}, bf16[2,184,1024]{2,1,0:T(8,128)(2,1)S(1)}, u32[]{:S(2)}, u32[]{:S(2)}) collective-permute-start(bf16[2,184,1024]{2,1,0:T(8,128)(2,1)S(1)} %get-tuple-element.41.field), channel_id=1, source_target_pairs={{0,2},{2,0},{4,6},{6,4},{8,10},{10,8},{12,14},{14,12},{16,18},{18,... | collective-permute-start | bytes 2261000 | tf_op jit(solution)/shard_map/ppermute | solution.py:426
  5.1 3.0 %collective-permute-start.2 = (bf16[2,184,1024]{2,1,0:T(8,128)(2,1)S(1)}, bf16[2,184,1024]{2,1,0:T(8,128)(2,1)S(1)}, u32[]{:S(2)}, u32[]{:S(2)}) collective-permute-start(bf16[2,184,1024]{2,1,0:T(8,128)(2,1)S(1)} %get-tuple-element.40.field), channel_id=1, source_target_pairs={{2,4},{4,2},{6,8},{8,6},{10,12},{12,10},{14,16},{16,14},{18,20},{2... | collective-permute-start | bytes 2261000 | tf_op jit(solution)/shard_map/ppermute | solution.py:427
  8.1 0.0 collective-permute-done.halo
  8.2 0.0 copy-start.7
  8.2 0.0 copy-start.1
  8.2 0.0 copy-start.2
  8.2 0.0 copy-start.3
  8.2 2.2 %shard_map.75 = (f32[184,1024]{1,0:T(8,128)S(1)}, f32[184,1024]{1,0:T(8,128)S(1)}, bf16[2,184,1024]{2,1,0:T(8,128)(2,1)S(1)}) custom-call(s32[2]{0:T(128)S(1)} %pad_add_fusion.ids, f32[2,2,184,128]{3,2,1,0:T(8,128)S(1)} %get-tuple-element.35.courant, f32[2,1024]{1,0:T(2,128)S(1)} %copy-done.6, s32[2,1024]{1,0:T(2,128)S(1)} %copy-done.4, ...), custom_call_target="tpu_custom_call" | custom-call | flops 2200000000 | tf_op jit(solution)/shard_map/pallas_call | solution.py:171
  10.5 1.3 %collective-permute-start.1 = (bf16[2,184,1024]{2,1,0:T(8,128)(2,1)S(1)}, bf16[2,184,1024]{2,1,0:T(8,128)(2,1)S(1)}, u32[]{:S(2)}, u32[]{:S(2)}) collective-permute-start(bf16[2,184,1024]{2,1,0:T(8,128)(2,1)S(1)} %get-tuple-element.42.own0.rest_2_), channel_id=1, source_target_pairs={{0,1},{1,0},{2,3},{3,2},{4,5},{5,4},{6,7},{7,6},{8,9},{9,8},{10,11... | collective-permute-start | bytes 2261000 | tf_op jit(solution)/shard_map/ppermute | solution.py:435
  11.8 0.0 copy-start.5
  11.8 3.1 %shard_map.74 = (bf16[736,768]{1,0:T(8,128)(2,1)S(1)}, bf16[720,768]{1,0:T(8,128)(2,1)S(1)}, bf16[384,720]{1,0:T(8,128)(2,1)S(1)}, f32[384,128]{1,0:T(8,128)S(1)}) custom-call(s32[2]{0:T(128)S(1)} %pad_add_fusion.ids, bf16[720,720]{1,0:T(8,128)(2,1)S(1)} %copy-done.1, bf16[720,720]{1,0:T(8,128)(2,1)S(1)} %copy-done.2, bf16[720,720]{1,0:T(8,128)(2,1)S(1)} %copy-done.3, ...), custom_call_target="tpu_custom_call" | custom-call | flops 3300000000 | tf_op jit(solution)/shard_map/pallas_call | solution.py:171
  14.9 11.5 %collective-permute-done.2.halo = bf16[2,184,1024]{2,1,0:T(8,128)(2,1)S(1)} collective-permute-done((bf16[2,184,1024]{2,1,0:T(8,128)(2,1)S(1)}, bf16[2,184,1024]{2,1,0:T(8,128)(2,1)S(1)}, u32[]{:S(2)}, u32[]{:S(2)}) %collective-permute-start.2) | collective-permute-done | bytes 753696 | tf_op jit(solution)/shard_map/ppermute | solution.py:427
  26.4 2.2 %shard_map.76 = (f32[184,1024]{1,0:T(8,128)S(1)}, f32[184,1024]{1,0:T(8,128)S(1)}, bf16[184,1024]{1,0:T(8,128)(2,1)S(1)}, bf16[184,1024]{1,0:T(8,128)(2,1)S(1)}) custom-call(s32[2]{0:T(128)S(1)} %pad_add_fusion.ids, f32[2,2,184,128]{3,2,1,0:T(8,128)S(1)} %get-tuple-element.35.courant, f32[2,1024]{1,0:T(2,128)S(1)} %copy-done.6, s32[2,1024]{1,0:T(2,128)S(1)} %copy-done.5, ...), custom_call_target="tpu_custom_call" | custom-call | flops 2200000000 | tf_op jit(solution)/shard_map/pallas_call | solution.py:171
  28.7 1.3 %collective-permute-start.4 = (bf16[184,1024]{1,0:T(8,128)(2,1)S(1)}, bf16[184,1024]{1,0:T(8,128)(2,1)S(1)}, u32[]{:S(2)}, u32[]{:S(2)}) collective-permute-start(bf16[184,1024]{1,0:T(8,128)(2,1)S(1)} %get-tuple-element.44.own1_1.rest_3_), channel_id=1, source_target_pairs={{0,1},{1,0},{2,3},{3,2},{4,5},{5,4},{6,7},{7,6},{8,9},{9,8},{10,11... | collective-permute-start | bytes 1130504 | tf_op jit(solution)/shard_map/ppermute | solution.py:447
  30.0 0.2 collective-permute-start.3
  30.2 5.3 %shard_map.77 = (f32[736,1024]{1,0:T(8,128)S(1)}, f32[720,1024]{1,0:T(8,128)S(1)}, f32[736,1024]{1,0:T(8,128)S(1)}, f32[720,1024]{1,0:T(8,128)S(1)}) custom-call(s32[2]{0:T(128)S(1)} %pad_add_fusion.ids, bf16[736,768]{1,0:T(8,128)(2,1)S(1)} %get-tuple-element.36.first, bf16[720,768]{1,0:T(8,128)(2,1)S(1)} %get-tuple-element.37.second, ...), custom_call_target="tpu_custom_call" | custom-call | flops 4400000000 | tf_op jit(solution)/shard_map/pallas_call | solution.py:171
  35.5 4.0 %collective-permute-done.4.rest_4_ = bf16[184,1024]{1,0:T(8,128)(2,1)S(1)} collective-permute-done((bf16[184,1024]{1,0:T(8,128)(2,1)S(1)}, bf16[184,1024]{1,0:T(8,128)(2,1)S(1)}, u32[]{:S(2)}, u32[]{:S(2)}) %collective-permute-start.4) | collective-permute-done | bytes 376864 | tf_op jit(solution)/shard_map/ppermute | solution.py:447
  39.6 2.8 %shard_map.79 = (f32[184,1024]{1,0:T(8,128)S(1)}, bf16[184,1024]{1,0:T(8,128)(2,1)S(1)}, f32[184,1024]{1,0:T(8,128)S(1)}, bf16[184,1024]{1,0:T(8,128)(2,1)S(1)}) custom-call(s32[2]{0:T(128)S(1)} %pad_add_fusion.ids, bf16[736,768]{1,0:T(8,128)(2,1)S(1)} %get-tuple-element.36.first, bf16[720,768]{1,0:T(8,128)(2,1)S(1)} %get-tuple-element.37.second, ...), custom_call_target="tpu_custom_call" | custom-call | flops 4400000000 | tf_op jit(solution)/shard_map/pallas_call | solution.py:171
  42.3 3.8 %collective-permute-start.6 = (bf16[184,1024]{1,0:T(8,128)(2,1)S(1)}, bf16[184,1024]{1,0:T(8,128)(2,1)S(1)}, u32[]{:S(2)}, u32[]{:S(2)}) collective-permute-start(bf16[184,1024]{1,0:T(8,128)(2,1)S(1)} %get-tuple-element.57), channel_id=1, source_target_pairs={{2,4},{4,2},{6,8},{8,6},{10,12},{12,10},{14,16},{16,14},{18,20},{2... | collective-permute-start | bytes 1130504 | tf_op jit(solution)/shard_map/ppermute | solution.py:471
  46.1 0.1 collective-permute-start.7
  46.2 2.8 %shard_map.78 = (f32[184,1024]{1,0:T(8,128)S(1)}, bf16[184,1024]{1,0:T(8,128)(2,1)S(1)}, f32[184,1024]{1,0:T(8,128)S(1)}, bf16[184,1024]{1,0:T(8,128)(2,1)S(1)}) custom-call(s32[2]{0:T(128)S(1)} %pad_add_fusion.ids, bf16[736,768]{1,0:T(8,128)(2,1)S(1)} %get-tuple-element.36.first, bf16[720,768]{1,0:T(8,128)(2,1)S(1)} %get-tuple-element.37.second, ...), custom_call_target="tpu_custom_call" | custom-call | flops 4400000000 | tf_op jit(solution)/shard_map/pallas_call | solution.py:171
  49.0 0.5 collective-permute-start.8
  49.6 2.2 %collective-permute-start.5 = (bf16[184,1024]{1,0:T(8,128)(2,1)S(1)}, bf16[184,1024]{1,0:T(8,128)(2,1)S(1)}, u32[]{:S(2)}, u32[]{:S(2)}) collective-permute-start(bf16[184,1024]{1,0:T(8,128)(2,1)S(1)} %get-tuple-element.55), channel_id=1, source_target_pairs={{2,4},{4,2},{6,8},{8,6},{10,12},{12,10},{14,16},{16,14},{18,20},{2... | collective-permute-start | bytes 1130504 | tf_op jit(solution)/shard_map/ppermute | solution.py:471
  51.8 0.0 collective-permute-done.6.h1
  51.8 0.0 collective-permute-done.7.h0
  51.8 3.1 %shard_map.80 = (f32[720,1024]{1,0:T(8,128)S(1)}, bf16[720,384]{1,0:T(8,128)(2,1)S(1)}) custom-call(s32[2]{0:T(128)S(1)} %pad_add_fusion.ids, f32[2,2,184,128]{3,2,1,0:T(8,128)S(1)} %get-tuple-element.35.courant, f32[2,1024]{1,0:T(2,128)S(1)} %copy-done.6, s32[2,1024]{1,0:T(2,128)S(1)} %copy-done.5, f32[184,1024]{1,0:T(8,128)S(1)} %get-tuple-element.59.u0, ...), custom_call_target="tpu_custom_call" | custom-call | flops 3300000000 | tf_op jit(solution)/shard_map/pallas_call | solution.py:171
  54.9 7.6 %collective-permute-done.5.h0 = bf16[184,1024]{1,0:T(8,128)(2,1)S(1)} collective-permute-done((bf16[184,1024]{1,0:T(8,128)(2,1)S(1)}, bf16[184,1024]{1,0:T(8,128)(2,1)S(1)}, u32[]{:S(2)}, u32[]{:S(2)}) %collective-permute-start.5) | collective-permute-done | bytes 376864 | tf_op jit(solution)/shard_map/ppermute | solution.py:471
  62.5 4.3 %shard_map.81 = bf16[360,2,1024]{2,1,0:T(2,128)(2,1)} custom-call(s32[2]{0:T(128)S(1)} %pad_add_fusion.ids, f32[2,2,184,128]{3,2,1,0:T(8,128)S(1)} %get-tuple-element.35.courant, f32[2,1024]{1,0:T(2,128)S(1)} %copy-done.6, s32[2,1024]{1,0:T(2,128)S(1)} %copy-done.5, f32[184,1024]{1,0:T(8,128)S(1)} %get-tuple-element.49.u0, ...), custom_call_target="tpu_custom_call" | custom-call | flops 4400000000 | tf_op jit(solution)/shard_map/pallas_call | solution.py:171
  (13 shorter events, 0.0 us)
Async XLA Ops:
  0.1 1.4 %copy-start = (bf16[360,2,1024]{2,1,0:T(2,128)(2,1)S(1)}, bf16[360,2,1024]{2,1,0:T(2,128)(2,1)}, u32[]{:S(2)}) copy-start(bf16[360,2,1024]{2,1,0:T(2,128)(2,1)} %energy.1) | copy-start | bytes 4423684
  1.4 0.7 %copy-start.4 = (s32[2,1024]{1,0:T(2,128)S(1)}, s32[2,1024]{1,0:T(2,128)}, u32[]{:S(2)}) copy-start(s32[2,1024]{1,0:T(2,128)} %mask.13) | copy-start | bytes 24580
  2.1 6.0 %copy-start.6 = (f32[2,1024]{1,0:T(2,128)S(1)}, f32[2,1024]{1,0:T(2,128)}, u32[]{:S(2)}) copy-start(f32[2,1024]{1,0:T(2,128)} %depth.7) | copy-start | bytes 24580
  4.4 3.8 %collective-permute-start = (bf16[2,184,1024]{2,1,0:T(8,128)(2,1)S(1)}, bf16[2,184,1024]{2,1,0:T(8,128)(2,1)S(1)}, u32[]{:S(2)}, u32[]{:S(2)}) collective-permute-start(bf16[2,184,1024]{2,1,0:T(8,128)(2,1)S(1)} %get-tuple-element.41.field), channel_id=1, source_target_pairs={{0,2},{2,0},{4,6},{6,4},{8,10},{10,8},{12,14},{14,12},{16,18},{18,... | collective-permute-start | bytes 2261000 | tf_op jit(solution)/shard_map/ppermute | solution.py:426
  5.1 21.3 %collective-permute-start.2 = (bf16[2,184,1024]{2,1,0:T(8,128)(2,1)S(1)}, bf16[2,184,1024]{2,1,0:T(8,128)(2,1)S(1)}, u32[]{:S(2)}, u32[]{:S(2)}) collective-permute-start(bf16[2,184,1024]{2,1,0:T(8,128)(2,1)S(1)} %get-tuple-element.40.field), channel_id=1, source_target_pairs={{2,4},{4,2},{6,8},{8,6},{10,12},{12,10},{14,16},{16,14},{18,20},{2... | collective-permute-start | bytes 2261000 | tf_op jit(solution)/shard_map/ppermute | solution.py:427
  8.2 3.6 %copy-start.7 = (f32[720]{0:T(1024)S(1)}, f32[720]{0:T(1024)}, u32[]{:S(2)}) copy-start(f32[720]{0:T(1024)} %param.13) | copy-start | bytes 8644
  8.2 3.6 %copy-start.1 = (bf16[720,720]{1,0:T(8,128)(2,1)S(1)}, bf16[720,720]{1,0:T(8,128)(2,1)}, u32[]{:S(2)}) copy-start(bf16[720,720]{1,0:T(8,128)(2,1)} %first.1) | copy-start | bytes 3110404
  8.2 3.6 %copy-start.2 = (bf16[720,720]{1,0:T(8,128)(2,1)S(1)}, bf16[720,720]{1,0:T(8,128)(2,1)}, u32[]{:S(2)}) copy-start(bf16[720,720]{1,0:T(8,128)(2,1)} %second.1) | copy-start | bytes 3110404
  8.2 3.6 %copy-start.3 = (bf16[720,720]{1,0:T(8,128)(2,1)S(1)}, bf16[720,720]{1,0:T(8,128)(2,1)}, u32[]{:S(2)}) copy-start(bf16[720,720]{1,0:T(8,128)(2,1)} %transfer.1) | copy-start | bytes 3110404
  10.5 19.8 %collective-permute-start.1 = (bf16[2,184,1024]{2,1,0:T(8,128)(2,1)S(1)}, bf16[2,184,1024]{2,1,0:T(8,128)(2,1)S(1)}, u32[]{:S(2)}, u32[]{:S(2)}) collective-permute-start(bf16[2,184,1024]{2,1,0:T(8,128)(2,1)S(1)} %get-tuple-element.42.own0.rest_2_), channel_id=1, source_target_pairs={{0,1},{1,0},{2,3},{3,2},{4,5},{5,4},{6,7},{7,6},{8,9},{9,8},{10,11... | collective-permute-start | bytes 2261000 | tf_op jit(solution)/shard_map/ppermute | solution.py:435
  11.8 14.6 %copy-start.5 = (s32[2,1024]{1,0:T(2,128)S(1)}, s32[2,1024]{1,0:T(2,128)}, u32[]{:S(2)}) copy-start(s32[2,1024]{1,0:T(2,128)} %mask.13) | copy-start | bytes 24580
  28.7 10.9 %collective-permute-start.4 = (bf16[184,1024]{1,0:T(8,128)(2,1)S(1)}, bf16[184,1024]{1,0:T(8,128)(2,1)S(1)}, u32[]{:S(2)}, u32[]{:S(2)}) collective-permute-start(bf16[184,1024]{1,0:T(8,128)(2,1)S(1)} %get-tuple-element.44.own1_1.rest_3_), channel_id=1, source_target_pairs={{0,1},{1,0},{2,3},{3,2},{4,5},{5,4},{6,7},{7,6},{8,9},{9,8},{10,11... | collective-permute-start | bytes 1130504 | tf_op jit(solution)/shard_map/ppermute | solution.py:447
  30.0 16.2 %collective-permute-start.3 = (bf16[184,1024]{1,0:T(8,128)(2,1)S(1)}, bf16[184,1024]{1,0:T(8,128)(2,1)S(1)}, u32[]{:S(2)}, u32[]{:S(2)}) collective-permute-start(bf16[184,1024]{1,0:T(8,128)(2,1)S(1)} %get-tuple-element.43.own1_0.rest_3_), channel_id=1, source_target_pairs={{0,1},{1,0},{2,3},{3,2},{4,5},{5,4},{6,7},{7,6},{8,9},{9,8},{10,11... | collective-permute-start | bytes 1130504 | tf_op jit(solution)/shard_map/ppermute | solution.py:448
  42.3 9.4 %collective-permute-start.6 = (bf16[184,1024]{1,0:T(8,128)(2,1)S(1)}, bf16[184,1024]{1,0:T(8,128)(2,1)S(1)}, u32[]{:S(2)}, u32[]{:S(2)}) collective-permute-start(bf16[184,1024]{1,0:T(8,128)(2,1)S(1)} %get-tuple-element.57), channel_id=1, source_target_pairs={{2,4},{4,2},{6,8},{8,6},{10,12},{12,10},{14,16},{16,14},{18,20},{2... | collective-permute-start | bytes 1130504 | tf_op jit(solution)/shard_map/ppermute | solution.py:471
  46.1 5.7 %collective-permute-start.7 = (bf16[184,1024]{1,0:T(8,128)(2,1)S(1)}, bf16[184,1024]{1,0:T(8,128)(2,1)S(1)}, u32[]{:S(2)}, u32[]{:S(2)}) collective-permute-start(bf16[184,1024]{1,0:T(8,128)(2,1)S(1)} %get-tuple-element.61), channel_id=1, source_target_pairs={{0,2},{2,0},{4,6},{6,4},{8,10},{10,8},{12,14},{14,12},{16,18},{18,... | collective-permute-start | bytes 1130504 | tf_op jit(solution)/shard_map/ppermute | solution.py:472
  49.0 2.8 %collective-permute-start.8 = (bf16[184,1024]{1,0:T(8,128)(2,1)S(1)}, bf16[184,1024]{1,0:T(8,128)(2,1)S(1)}, u32[]{:S(2)}, u32[]{:S(2)}) collective-permute-start(bf16[184,1024]{1,0:T(8,128)(2,1)S(1)} %get-tuple-element.62), channel_id=1, source_target_pairs={{0,2},{2,0},{4,6},{6,4},{8,10},{10,8},{12,14},{14,12},{16,18},{18,... | collective-permute-start | bytes 1130504 | tf_op jit(solution)/shard_map/ppermute | solution.py:472
  49.6 12.9 %collective-permute-start.5 = (bf16[184,1024]{1,0:T(8,128)(2,1)S(1)}, bf16[184,1024]{1,0:T(8,128)(2,1)S(1)}, u32[]{:S(2)}, u32[]{:S(2)}) collective-permute-start(bf16[184,1024]{1,0:T(8,128)(2,1)S(1)} %get-tuple-element.55), channel_id=1, source_target_pairs={{2,4},{4,2},{6,8},{8,6},{10,12},{12,10},{14,16},{16,14},{18,20},{2... | collective-permute-start | bytes 1130504 | tf_op jit(solution)/shard_map/ppermute | solution.py:471

commit v3 on v2

--- a/solution.py
+++ b/solution.py
@@ -268,12 +268,17 @@
         block(full * 16, plan.rows % 16, -1)
 
 
+def within(ids, group, rows):
+    return rows if group == 0 else [jnp.where(ids[2] == 1, row, 0.0) for row in rows]
+
+
 def first_body(plan, group, ids, courant, depth, mask, field, halo, *rest):
     half, spectra, (depth8, ocean8) = rest[:2], rest[2:-2], rest[-2:]
 
     def load(start, rows):
         at = pl.ds(start, rows)
-        return tuple(ref[r, at].astype(F32) for ref, r in ((field, 0), (field, 1), (halo, 1), (halo, 0)))
+        values = [ref[r, at].astype(F32) for ref, r in ((field, 0), (field, 1), (halo, 1), (halo, 0))]
+        return values[:2] + within(ids, group, values[2:])
 
     def store(start, rows, new0, new1):
         at = pl.ds(start, rows)
@@ -293,7 +298,8 @@
 
     def load(start, rows):
         at = pl.ds(start, rows)
-        return tuple(ref[at].astype(F32) for ref in (u0, u1, h0, h1))
+        values = [ref[at].astype(F32) for ref in (u0, u1, h0, h1)]
+        return values[:2] + within(ids, group, values[2:])
 
     def store(start, rows, new0, new1):
         for r, new in enumerate((new0, new1)):
@@ -404,10 +410,12 @@
     size, rows, pitch, total = plan.columns, plan.rows, plan.pitch, plan.total
     bands = lax.axis_size("band")
     parity = lax.axis_index("band") % 2
-    ids = jnp.stack([parity, 2 * lax.axis_index("comp") + parity]).astype(jnp.int32)
+    band = lax.axis_index("band")
+    inside = jnp.logical_and(band > 0, band < bands - 1)
+    ids = jnp.stack([parity, 2 * lax.axis_index("comp") + parity, inside.astype(jnp.int32)]).astype(jnp.int32)
 
     inner = [(i, i ^ 1) for i in range(bands)]
-    outer = [(i, j) for i in range(1, bands - 1) for j in [i + 1 if i % 2 else i - 1]]
+    outer = [(i, (i + 1 if i % 2 else i - 1) % bands) for i in range(bands)]
     peers = [(0, 1), (1, 0)]
 
     def shape(*dims, kind=BF16):

time: 67.1 us -> 64.3 us (0.958)
  the two profiles are of different devices: /device:TPU:9 before, /device:TPU:1 now
where the time goes in v3:
time: 64.3 us; the launch traced here: 64.1 us
  Pallas kernels  28.3 us (44%)
  waiting for transfers between devices  22.9 us (36%)
  starting transfers between devices  10.5 us (16%)
  local copies, waits for them, and re-layouts  2.11 us (3%)
    pallas_call x9, Pallas kernels, call(): pl.pallas_call(body, in_specs=[SMEM] + [VMEM] * len(operands), out_specs=...  28.3 us
    ppermute x1, waiting for transfers between devices, paired_shards(): halo1 = lax.ppermute(field0, 'band', outer)  10.3 us
    ppermute x2, waiting for transfers between devices, paired_shards(): rim1 = [lax.ppermute(x, 'band', outer) for x in sent0]  6.85 us
    ppermute x1, waiting for transfers between devices, paired_shards(): peer1[1] = lax.ppermute(own1[1], 'comp', peers)  3.98 us
    ppermute x2, starting transfers between devices, paired_shards(): rim1 = [lax.ppermute(x, 'band', outer) for x in sent0]  3.77 us
    ppermute x1, starting transfers between devices, paired_shards(): halo1 = lax.ppermute(field0, 'band', outer)  2.61 us
    unnamed x16, local copies, waits for them, and re-layouts  2.1 us
    ppermute x1, starting transfers between devices, paired_shards(): peer0 = lax.ppermute(own0, 'comp', peers)  1.98 us
  transfers between devices with their start and end apart: 9, of which 5 were waited for; matrix products, arithmetic and copies ran while one was open for 0% of the time, Pallas kernels for 34%

profile of v3, /device:TPU:1, one launch (start us, length us, event | category | flops | bytes accessed | tf_op | source)
XLA Modules:
  0.0 64.1 jit_solution(13186121371539812144)
XLA Ops:
  0.0 0.1 pad_add_fusion.ids
  0.1 1.4 %copy-done = bf16[360,2,1024]{2,1,0:T(2,128)(2,1)S(1)} copy-done((bf16[360,2,1024]{2,1,0:T(2,128)(2,1)S(1)}, bf16[360,2,1024]{2,1,0:T(2,128)(2,1)}, u32[]{:S(2)}) %copy-start) | copy-done | bytes 1474584
  1.5 0.7 %copy-done.4 = s32[2,1024]{1,0:T(2,128)S(1)} copy-done((s32[2,1024]{1,0:T(2,128)S(1)}, s32[2,1024]{1,0:T(2,128)}, u32[]{:S(2)}) %copy-start.4) | copy-done | bytes 8216
  2.2 2.2 %shard_map.73 = (bf16[2,184,1024]{2,1,0:T(8,128)(2,1)S(1)}, bf16[2,184,1024]{2,1,0:T(8,128)(2,1)S(1)}, f32[2,2,184,128]{3,2,1,0:T(8,128)S(1)}) custom-call(s32[3]{0:T(128)S(1)} %pad_add_fusion.ids, bf16[360,2,1024]{2,1,0:T(2,128)(2,1)S(1)} %copy-done, s32[2,1024]{1,0:T(2,128)S(1)} %copy-done.4), custom_call_target="tpu_custom_call" | custom-call | flops 2200000000 | tf_op jit(solution)/shard_map/pallas_call | solution.py:171
  4.4 0.1 collective-permute-start
  4.5 2.6 %collective-permute-start.2 = (bf16[2,184,1024]{2,1,0:T(8,128)(2,1)S(1)}, bf16[2,184,1024]{2,1,0:T(8,128)(2,1)S(1)}, u32[]{:S(2)}, u32[]{:S(2)}) collective-permute-start(bf16[2,184,1024]{2,1,0:T(8,128)(2,1)S(1)} %get-tuple-element.40.field), channel_id=1, source_target_pairs={{0,30},{2,4},{4,2},{6,8},{8,6},{10,12},{12,10},{14,16},{16,14},{18... | collective-permute-start | bytes 2261000 | tf_op jit(solution)/shard_map/ppermute | solution.py:435
  7.1 0.0 collective-permute-done.halo
  7.1 0.0 copy-start.7
  7.1 0.0 copy-start.1
  7.1 0.0 copy-start.2
  7.2 0.0 copy-start.3
  7.2 2.2 %shard_map.75 = (f32[184,1024]{1,0:T(8,128)S(1)}, f32[184,1024]{1,0:T(8,128)S(1)}, bf16[2,184,1024]{2,1,0:T(8,128)(2,1)S(1)}) custom-call(s32[3]{0:T(128)S(1)} %pad_add_fusion.ids, f32[2,2,184,128]{3,2,1,0:T(8,128)S(1)} %get-tuple-element.35.courant, f32[2,1024]{1,0:T(2,128)S(1)} %copy-done.6, s32[2,1024]{1,0:T(2,128)S(1)} %copy-done.5, ...), custom_call_target="tpu_custom_call" | custom-call | flops 2200000000 | tf_op jit(solution)/shard_map/pallas_call | solution.py:171
  9.4 2.0 %collective-permute-start.1 = (bf16[2,184,1024]{2,1,0:T(8,128)(2,1)S(1)}, bf16[2,184,1024]{2,1,0:T(8,128)(2,1)S(1)}, u32[]{:S(2)}, u32[]{:S(2)}) collective-permute-start(bf16[2,184,1024]{2,1,0:T(8,128)(2,1)S(1)} %get-tuple-element.42.own0.rest_2_), channel_id=1, source_target_pairs={{0,1},{1,0},{2,3},{3,2},{4,5},{5,4},{6,7},{7,6},{8,9},{9,8},{10,11... | collective-permute-start | bytes 2261000 | tf_op jit(solution)/shard_map/ppermute | solution.py:443
  11.4 3.1 %shard_map.74 = (bf16[736,768]{1,0:T(8,128)(2,1)S(1)}, bf16[720,768]{1,0:T(8,128)(2,1)S(1)}, bf16[384,720]{1,0:T(8,128)(2,1)S(1)}, f32[384,128]{1,0:T(8,128)S(1)}) custom-call(s32[3]{0:T(128)S(1)} %pad_add_fusion.ids, bf16[720,720]{1,0:T(8,128)(2,1)S(1)} %copy-done.1, bf16[720,720]{1,0:T(8,128)(2,1)S(1)} %copy-done.2, bf16[720,720]{1,0:T(8,128)(2,1)S(1)} %copy-done.3, ...), custom_call_target="tpu_custom_call" | custom-call | flops 3300000000 | tf_op jit(solution)/shard_map/pallas_call | solution.py:171
  14.5 10.3 %collective-permute-done.2.halo = bf16[2,184,1024]{2,1,0:T(8,128)(2,1)S(1)} collective-permute-done((bf16[2,184,1024]{2,1,0:T(8,128)(2,1)S(1)}, bf16[2,184,1024]{2,1,0:T(8,128)(2,1)S(1)}, u32[]{:S(2)}, u32[]{:S(2)}) %collective-permute-start.2) | collective-permute-done | bytes 753696 | tf_op jit(solution)/shard_map/ppermute | solution.py:435
  24.8 2.3 %shard_map.76 = (f32[184,1024]{1,0:T(8,128)S(1)}, f32[184,1024]{1,0:T(8,128)S(1)}, bf16[184,1024]{1,0:T(8,128)(2,1)S(1)}, bf16[184,1024]{1,0:T(8,128)(2,1)S(1)}) custom-call(s32[3]{0:T(128)S(1)} %pad_add_fusion.ids, f32[2,2,184,128]{3,2,1,0:T(8,128)S(1)} %get-tuple-element.35.courant, f32[2,1024]{1,0:T(2,128)S(1)} %copy-done.6, s32[2,1024]{1,0:T(2,128)S(1)} %copy-done.5, ...), custom_call_target="tpu_custom_call" | custom-call | flops 2200000000 | tf_op jit(solution)/shard_map/pallas_call | solution.py:171
  27.1 1.9 %collective-permute-start.4 = (bf16[184,1024]{1,0:T(8,128)(2,1)S(1)}, bf16[184,1024]{1,0:T(8,128)(2,1)S(1)}, u32[]{:S(2)}, u32[]{:S(2)}) collective-permute-start(bf16[184,1024]{1,0:T(8,128)(2,1)S(1)} %get-tuple-element.44.own1_1.rest_3_), channel_id=1, source_target_pairs={{0,1},{1,0},{2,3},{3,2},{4,5},{5,4},{6,7},{7,6},{8,9},{9,8},{10,11... | collective-permute-start | bytes 1130504 | tf_op jit(solution)/shard_map/ppermute | solution.py:455
  29.0 0.1 collective-permute-start.3
  29.1 0.0 collective-permute-done.1.peer0
  29.1 5.3 %shard_map.77 = (f32[736,1024]{1,0:T(8,128)S(1)}, f32[720,1024]{1,0:T(8,128)S(1)}, f32[736,1024]{1,0:T(8,128)S(1)}, f32[720,1024]{1,0:T(8,128)S(1)}) custom-call(s32[3]{0:T(128)S(1)} %pad_add_fusion.ids, bf16[736,768]{1,0:T(8,128)(2,1)S(1)} %get-tuple-element.36.first, bf16[720,768]{1,0:T(8,128)(2,1)S(1)} %get-tuple-element.37.second, ...), custom_call_target="tpu_custom_call" | custom-call | flops 4400000000 | tf_op jit(solution)/shard_map/pallas_call | solution.py:171
  34.4 4.0 %collective-permute-done.4.rest_4_ = bf16[184,1024]{1,0:T(8,128)(2,1)S(1)} collective-permute-done((bf16[184,1024]{1,0:T(8,128)(2,1)S(1)}, bf16[184,1024]{1,0:T(8,128)(2,1)S(1)}, u32[]{:S(2)}, u32[]{:S(2)}) %collective-permute-start.4) | collective-permute-done | bytes 376864 | tf_op jit(solution)/shard_map/ppermute | solution.py:455
  38.4 2.8 %shard_map.79 = (f32[184,1024]{1,0:T(8,128)S(1)}, bf16[184,1024]{1,0:T(8,128)(2,1)S(1)}, f32[184,1024]{1,0:T(8,128)S(1)}, bf16[184,1024]{1,0:T(8,128)(2,1)S(1)}) custom-call(s32[3]{0:T(128)S(1)} %pad_add_fusion.ids, bf16[736,768]{1,0:T(8,128)(2,1)S(1)} %get-tuple-element.36.first, bf16[720,768]{1,0:T(8,128)(2,1)S(1)} %get-tuple-element.37.second, ...), custom_call_target="tpu_custom_call" | custom-call | flops 4400000000 | tf_op jit(solution)/shard_map/pallas_call | solution.py:171
  41.1 2.0 %collective-permute-start.6 = (bf16[184,1024]{1,0:T(8,128)(2,1)S(1)}, bf16[184,1024]{1,0:T(8,128)(2,1)S(1)}, u32[]{:S(2)}, u32[]{:S(2)}) collective-permute-start(bf16[184,1024]{1,0:T(8,128)(2,1)S(1)} %get-tuple-element.57), channel_id=1, source_target_pairs={{0,30},{2,4},{4,2},{6,8},{8,6},{10,12},{12,10},{14,16},{16,14},{18... | collective-permute-start | bytes 1130504 | tf_op jit(solution)/shard_map/ppermute | solution.py:479
  43.1 1.8 %collective-permute-done.3.rest_4_ = bf16[184,1024]{1,0:T(8,128)(2,1)S(1)} collective-permute-done((bf16[184,1024]{1,0:T(8,128)(2,1)S(1)}, bf16[184,1024]{1,0:T(8,128)(2,1)S(1)}, u32[]{:S(2)}, u32[]{:S(2)}) %collective-permute-start.3) | collective-permute-done | bytes 376864 | tf_op jit(solution)/shard_map/ppermute | solution.py:456
  44.9 2.8 %shard_map.78 = (f32[184,1024]{1,0:T(8,128)S(1)}, bf16[184,1024]{1,0:T(8,128)(2,1)S(1)}, f32[184,1024]{1,0:T(8,128)S(1)}, bf16[184,1024]{1,0:T(8,128)(2,1)S(1)}) custom-call(s32[3]{0:T(128)S(1)} %pad_add_fusion.ids, bf16[736,768]{1,0:T(8,128)(2,1)S(1)} %get-tuple-element.36.first, bf16[720,768]{1,0:T(8,128)(2,1)S(1)} %get-tuple-element.37.second, ...), custom_call_target="tpu_custom_call" | custom-call | flops 4400000000 | tf_op jit(solution)/shard_map/pallas_call | solution.py:171
  47.7 0.1 collective-permute-start.8
  47.8 1.8 %collective-permute-start.5 = (bf16[184,1024]{1,0:T(8,128)(2,1)S(1)}, bf16[184,1024]{1,0:T(8,128)(2,1)S(1)}, u32[]{:S(2)}, u32[]{:S(2)}) collective-permute-start(bf16[184,1024]{1,0:T(8,128)(2,1)S(1)} %get-tuple-element.55), channel_id=1, source_target_pairs={{0,30},{2,4},{4,2},{6,8},{8,6},{10,12},{12,10},{14,16},{16,14},{18... | collective-permute-start | bytes 1130504 | tf_op jit(solution)/shard_map/ppermute | solution.py:479
  49.6 2.1 %collective-permute-done.6.h1 = bf16[184,1024]{1,0:T(8,128)(2,1)S(1)} collective-permute-done((bf16[184,1024]{1,0:T(8,128)(2,1)S(1)}, bf16[184,1024]{1,0:T(8,128)(2,1)S(1)}, u32[]{:S(2)}, u32[]{:S(2)}) %collective-permute-start.6) | collective-permute-done | bytes 376864 | tf_op jit(solution)/shard_map/ppermute | solution.py:479
  51.7 0.0 collective-permute-done.8.h1
  51.7 3.3 %shard_map.80 = (f32[720,1024]{1,0:T(8,128)S(1)}, bf16[720,384]{1,0:T(8,128)(2,1)S(1)}) custom-call(s32[3]{0:T(128)S(1)} %pad_add_fusion.ids, f32[2,2,184,128]{3,2,1,0:T(8,128)S(1)} %get-tuple-element.35.courant, f32[2,1024]{1,0:T(2,128)S(1)} %copy-done.6, s32[2,1024]{1,0:T(2,128)S(1)} %copy-done.5, f32[184,1024]{1,0:T(8,128)S(1)} %get-tuple-element.59.u0, ...), custom_call_target="tpu_custom_call" | custom-call | flops 3300000000 | tf_op jit(solution)/shard_map/pallas_call | solution.py:171
  55.0 4.8 %collective-permute-done.5.h0 = bf16[184,1024]{1,0:T(8,128)(2,1)S(1)} collective-permute-done((bf16[184,1024]{1,0:T(8,128)(2,1)S(1)}, bf16[184,1024]{1,0:T(8,128)(2,1)S(1)}, u32[]{:S(2)}, u32[]{:S(2)}) %collective-permute-start.5) | collective-permute-done | bytes 376864 | tf_op jit(solution)/shard_map/ppermute | solution.py:479
  59.7 4.3 %shard_map.81 = bf16[360,2,1024]{2,1,0:T(2,128)(2,1)} custom-call(s32[3]{0:T(128)S(1)} %pad_add_fusion.ids, f32[2,2,184,128]{3,2,1,0:T(8,128)S(1)} %get-tuple-element.35.courant, f32[2,1024]{1,0:T(2,128)S(1)} %copy-done.6, s32[2,1024]{1,0:T(2,128)S(1)} %copy-done.5, f32[184,1024]{1,0:T(8,128)S(1)} %get-tuple-element.49.u0, ...), custom_call_target="tpu_custom_call" | custom-call | flops 4400000000 | tf_op jit(solution)/shard_map/pallas_call | solution.py:171
  (13 shorter events, 0.0 us)
Async XLA Ops:
  0.1 1.4 %copy-start = (bf16[360,2,1024]{2,1,0:T(2,128)(2,1)S(1)}, bf16[360,2,1024]{2,1,0:T(2,128)(2,1)}, u32[]{:S(2)}) copy-start(bf16[360,2,1024]{2,1,0:T(2,128)(2,1)} %energy.1) | copy-start | bytes 4423684
  1.5 0.7 %copy-start.4 = (s32[2,1024]{1,0:T(2,128)S(1)}, s32[2,1024]{1,0:T(2,128)}, u32[]{:S(2)}) copy-start(s32[2,1024]{1,0:T(2,128)} %mask.13) | copy-start | bytes 24580
  2.1 5.0 %copy-start.5 = (s32[2,1024]{1,0:T(2,128)S(1)}, s32[2,1024]{1,0:T(2,128)}, u32[]{:S(2)}) copy-start(s32[2,1024]{1,0:T(2,128)} %mask.13) | copy-start | bytes 24580
  2.2 5.0 %copy-start.6 = (f32[2,1024]{1,0:T(2,128)S(1)}, f32[2,1024]{1,0:T(2,128)}, u32[]{:S(2)}) copy-start(f32[2,1024]{1,0:T(2,128)} %depth.7) | copy-start | bytes 24580
  4.4 2.7 %collective-permute-start = (bf16[2,184,1024]{2,1,0:T(8,128)(2,1)S(1)}, bf16[2,184,1024]{2,1,0:T(8,128)(2,1)S(1)}, u32[]{:S(2)}, u32[]{:S(2)}) collective-permute-start(bf16[2,184,1024]{2,1,0:T(8,128)(2,1)S(1)} %get-tuple-element.41.field), channel_id=1, source_target_pairs={{0,2},{2,0},{4,6},{6,4},{8,10},{10,8},{12,14},{14,12},{16,18},{18,... | collective-permute-start | bytes 2261000 | tf_op jit(solution)/shard_map/ppermute | solution.py:434
  4.5 20.3 %collective-permute-start.2 = (bf16[2,184,1024]{2,1,0:T(8,128)(2,1)S(1)}, bf16[2,184,1024]{2,1,0:T(8,128)(2,1)S(1)}, u32[]{:S(2)}, u32[]{:S(2)}) collective-permute-start(bf16[2,184,1024]{2,1,0:T(8,128)(2,1)S(1)} %get-tuple-element.40.field), channel_id=1, source_target_pairs={{0,30},{2,4},{4,2},{6,8},{8,6},{10,12},{12,10},{14,16},{16,14},{18... | collective-permute-start | bytes 2261000 | tf_op jit(solution)/shard_map/ppermute | solution.py:435
  7.1 4.3 %copy-start.7 = (f32[720]{0:T(1024)S(1)}, f32[720]{0:T(1024)}, u32[]{:S(2)}) copy-start(f32[720]{0:T(1024)} %param.13) | copy-start | bytes 8644
  7.1 4.3 %copy-start.1 = (bf16[720,720]{1,0:T(8,128)(2,1)S(1)}, bf16[720,720]{1,0:T(8,128)(2,1)}, u32[]{:S(2)}) copy-start(bf16[720,720]{1,0:T(8,128)(2,1)} %first.1) | copy-start | bytes 3110404
  7.1 4.3 %copy-start.2 = (bf16[720,720]{1,0:T(8,128)(2,1)S(1)}, bf16[720,720]{1,0:T(8,128)(2,1)}, u32[]{:S(2)}) copy-start(bf16[720,720]{1,0:T(8,128)(2,1)} %second.1) | copy-start | bytes 3110404
  7.2 4.3 %copy-start.3 = (bf16[720,720]{1,0:T(8,128)(2,1)S(1)}, bf16[720,720]{1,0:T(8,128)(2,1)}, u32[]{:S(2)}) copy-start(bf16[720,720]{1,0:T(8,128)(2,1)} %transfer.1) | copy-start | bytes 3110404
  9.4 19.7 %collective-permute-start.1 = (bf16[2,184,1024]{2,1,0:T(8,128)(2,1)S(1)}, bf16[2,184,1024]{2,1,0:T(8,128)(2,1)S(1)}, u32[]{:S(2)}, u32[]{:S(2)}) collective-permute-start(bf16[2,184,1024]{2,1,0:T(8,128)(2,1)S(1)} %get-tuple-element.42.own0.rest_2_), channel_id=1, source_target_pairs={{0,1},{1,0},{2,3},{3,2},{4,5},{5,4},{6,7},{7,6},{8,9},{9,8},{10,11... | collective-permute-start | bytes 2261000 | tf_op jit(solution)/shard_map/ppermute | solution.py:443
  27.1 11.3 %collective-permute-start.4 = (bf16[184,1024]{1,0:T(8,128)(2,1)S(1)}, bf16[184,1024]{1,0:T(8,128)(2,1)S(1)}, u32[]{:S(2)}, u32[]{:S(2)}) collective-permute-start(bf16[184,1024]{1,0:T(8,128)(2,1)S(1)} %get-tuple-element.44.own1_1.rest_3_), channel_id=1, source_target_pairs={{0,1},{1,0},{2,3},{3,2},{4,5},{5,4},{6,7},{7,6},{8,9},{9,8},{10,11... | collective-permute-start | bytes 1130504 | tf_op jit(solution)/shard_map/ppermute | solution.py:455
  29.0 16.0 %collective-permute-start.3 = (bf16[184,1024]{1,0:T(8,128)(2,1)S(1)}, bf16[184,1024]{1,0:T(8,128)(2,1)S(1)}, u32[]{:S(2)}, u32[]{:S(2)}) collective-permute-start(bf16[184,1024]{1,0:T(8,128)(2,1)S(1)} %get-tuple-element.43.own1_0.rest_3_), channel_id=1, source_target_pairs={{0,1},{1,0},{2,3},{3,2},{4,5},{5,4},{6,7},{7,6},{8,9},{9,8},{10,11... | collective-permute-start | bytes 1130504 | tf_op jit(solution)/shard_map/ppermute | solution.py:456
  41.1 10.5 %collective-permute-start.6 = (bf16[184,1024]{1,0:T(8,128)(2,1)S(1)}, bf16[184,1024]{1,0:T(8,128)(2,1)S(1)}, u32[]{:S(2)}, u32[]{:S(2)}) collective-permute-start(bf16[184,1024]{1,0:T(8,128)(2,1)S(1)} %get-tuple-element.57), channel_id=1, source_target_pairs={{0,30},{2,4},{4,2},{6,8},{8,6},{10,12},{12,10},{14,16},{16,14},{18... | collective-permute-start | bytes 1130504 | tf_op jit(solution)/shard_map/ppermute | solution.py:479
  43.1 8.5 %collective-permute-start.7 = (bf16[184,1024]{1,0:T(8,128)(2,1)S(1)}, bf16[184,1024]{1,0:T(8,128)(2,1)S(1)}, u32[]{:S(2)}, u32[]{:S(2)}) collective-permute-start(bf16[184,1024]{1,0:T(8,128)(2,1)S(1)} %get-tuple-element.61), channel_id=1, source_target_pairs={{0,2},{2,0},{4,6},{6,4},{8,10},{10,8},{12,14},{14,12},{16,18},{18,... | collective-permute-start | bytes 1130504 | tf_op jit(solution)/shard_map/ppermute | solution.py:480
  47.7 3.9 %collective-permute-start.8 = (bf16[184,1024]{1,0:T(8,128)(2,1)S(1)}, bf16[184,1024]{1,0:T(8,128)(2,1)S(1)}, u32[]{:S(2)}, u32[]{:S(2)}) collective-permute-start(bf16[184,1024]{1,0:T(8,128)(2,1)S(1)} %get-tuple-element.62), channel_id=1, source_target_pairs={{0,2},{2,0},{4,6},{6,4},{8,10},{10,8},{12,14},{14,12},{16,18},{18,... | collective-permute-start | bytes 1130504 | tf_op jit(solution)/shard_map/ppermute | solution.py:480
  47.8 11.9 %collective-permute-start.5 = (bf16[184,1024]{1,0:T(8,128)(2,1)S(1)}, bf16[184,1024]{1,0:T(8,128)(2,1)S(1)}, u32[]{:S(2)}, u32[]{:S(2)}) collective-permute-start(bf16[184,1024]{1,0:T(8,128)(2,1)S(1)} %get-tuple-element.55), channel_id=1, source_target_pairs={{0,30},{2,4},{4,2},{6,8},{8,6},{10,12},{12,10},{14,16},{16,14},{18... | collective-permute-start | bytes 1130504 | tf_op jit(solution)/shard_map/ppermute | solution.py:479

commit v4 on v3

--- a/solution.py
+++ b/solution.py
@@ -117,6 +117,12 @@
         self.rows = -(-self.slots // 8) * 8
         self.pitch = -(-self.slots // 16) * 16
         self.out_rows = -(-(self.total + 1) // 16) * 16
+        self.side = columns // 2
+        self.cap = 3 * columns // 4
+
+    def pieces(self):
+        ends = [0, self.cap, (self.cap + 2 * self.columns) // 2, 2 * self.columns]
+        return list(zip(ends[:-1], ends[1:]))
 
     def slot_parts(self, slot):
         east = slot < self.half
@@ -203,7 +209,12 @@
         rows = in_order(ids, ocean, group)
         for r in range(2):
             at = (2 * group + r) * pitch
-            field[r] = (moved[at : at + plan.rows] * rows[r]).astype(BF16)
+            start = moved[at : at + plan.rows] * rows[r]
+            if group == 0:
+                place = lax.broadcasted_iota(jnp.int32, (8, plan.columns), 0) + (plan.rows - 8)
+                tail = jnp.where(place == plan.slots, rows[r], start[-8:])
+                start = jnp.concatenate([start[:-8], tail], axis=0)
+            field[r] = start.astype(BF16)
 
 
 def sweep(u, p, q, a):
@@ -272,8 +283,36 @@
     return rows if group == 0 else [jnp.where(ids[2] == 1, row, 0.0) for row in rows]
 
 
-def first_body(plan, group, ids, courant, depth, mask, field, halo, *rest):
-    half, spectra, (depth8, ocean8) = rest[:2], rest[2:-2], rest[-2:]
+def place_body(plan, neighbour, ids, mask, *placed):
+    side = plan.side
+    if neighbour:
+        tail = slice(plan.slots // 8 * 8, plan.rows)
+        at = plan.slots % 8
+        rows = [mask[r, tail].astype(F32)[at : at + 1] for r in range(2)]
+    else:
+        rows = in_order(ids, mask[...].astype(F32), 0)
+    parts = [row[:, b * side : (b + 1) * side] for b in range(2) for row in rows]
+    stacked = jnp.concatenate(parts + [jnp.zeros((12, side), F32)], axis=0).astype(BF16)
+    at = [lax.broadcasted_iota(jnp.int32, (side, side), axis) for axis in range(2)]
+    ahead = jnp.dot(stacked, one_hot(at[0] < at[1]), preferred_element_type=F32)
+    target = lax.broadcasted_iota(jnp.int32, (plan.cap, side), 0)
+    for b in range(2):
+        begin = jnp.zeros((1, 1), F32)
+        for r in range(2):
+            part = parts[2 * b + r]
+            place = jnp.where(part > 0, ahead[2 * b + r : 2 * b + r + 1] + begin, -1.0).astype(jnp.int32)
+            placed[b][:, r * side : (r + 1) * side] = one_hot(target == place)
+            begin = begin + jnp.sum(part, axis=1, keepdims=True)
+
+
+def gather_cells(cells, placed):
+    dims = (((1,), (1,)), ((), ()))
+    return lax.dot_general(cells, placed, dims, preferred_element_type=F32).astype(BF16)
+
+
+def first_body(plan, group, ids, courant, depth, mask, field, halo, placed0, placed1, *rest):
+    half, spectra, (depth8, ocean8, cells) = rest[:2], rest[2:-3], rest[-3:]
+    side = plan.side
 
     def load(start, rows):
         at = pl.ds(start, rows)
@@ -284,33 +323,53 @@
         at = pl.ds(start, rows)
         for r, new in enumerate((new0, new1)):
             half[r][at] = new
-            if len(spectra) == 1:
-                spectra[0][r, at] = new.astype(BF16)
-            else:
-                spectra[r][at] = new.astype(BF16)
+            begin = (r if group == 0 else 1 - r) * side
+            for b in range(2):
+                cells[b, at, begin : begin + side] = new[:, b * side : (b + 1) * side].astype(BF16)
 
     half_steps(plan, group, ids, courant, depth, mask, depth8, ocean8, load, store)
-
-
-def last_body(plan, group, ids, courant, depth, mask, u0, u1, h0, h1, *rest):
+    for b, placed in enumerate((placed0, placed1)):
+        gathered = gather_cells(cells[b], placed[...])
+        if group == 0:
+            spectra[0][:, b * plan.cap : (b + 1) * plan.cap] = gathered
+        else:
+            spectra[b][...] = gathered
+
+
+def last_body(plan, group, ids, courant, depth, mask, full0, full1, *rest):
     *rest, done, depth8, ocean8 = rest
-    width, pitch = 2 * plan.local, plan.pitch
-
-    def load(start, rows):
-        at = pl.ds(start, rows)
-        values = [ref[at].astype(F32) for ref in (u0, u1, h0, h1)]
-        return values[:2] + within(ids, group, values[2:])
-
-    def store(start, rows, new0, new1):
+    width, pitch, rows, side = 2 * plan.local, plan.pitch, plan.rows, plan.side
+
+    def scatter(cells, placed):
+        return jnp.dot(cells[...], placed[...], preferred_element_type=F32)[:rows].astype(BF16)
+
+    def both(a, b, at):
+        return jnp.concatenate([a[at], b[at]], axis=1).astype(F32)
+
+    def load(start, count):
+        at = pl.ds(start, count)
+        values = [both(full0.at[r], full1.at[r], at) for r in range(2)]
+        if group == 0:
+            rows_in = jnp.concatenate([piece[at] for piece in pieces], axis=1).astype(F32)
+            return values + [rows_in[:, plan.columns :], rows_in[:, : plan.columns]]
+        slots = [slice(slot * side, (slot + 1) * side) for slot in (1, 0)]
+        return values + within(ids, group, [both(rim0.at[:, slot], rim1.at[:, slot], at) for slot in slots])
+
+    def store(start, count, new0, new1):
         for r, new in enumerate((new0, new1)):
             at = r * pitch + start
-            if rows < 16:
-                new = jnp.concatenate([new, jnp.zeros((16 - rows, plan.columns), F32)], axis=0)
+            if count < 16:
+                new = jnp.concatenate([new, jnp.zeros((16 - count, plan.columns), F32)], axis=0)
             done[pl.ds(pl.multiple_of(at, 16), 16)] = new.astype(BF16)
 
+    if group == 0:
+        *pieces, partial, restore = rest
+    else:
+        cells0, cells1, placed0, placed1, partial, restore, out, rim0, rim1 = rest
+        rim0[...] = scatter(cells0, placed0)
+        rim1[...] = scatter(cells1, placed1)
     half_steps(plan, group, ids, courant, depth, mask, depth8, ocean8, load, store)
     if group == 0:
-        partial, restore = rest
         tables = []
         for g in range(2):
             lane = lax.broadcasted_iota(jnp.int32, (8, 2 * pitch), 1)
@@ -322,7 +381,6 @@
         restore[...] = tables[1]
         partial[...] = jnp.dot(tables[0], done[...], preferred_element_type=F32)
     else:
-        partial, restore, out = rest
         flat = partial[...] + jnp.dot(restore[...], done[...], preferred_element_type=F32)
         out[...] = flat.astype(BF16).reshape(plan.local, 2, plan.columns)
 
@@ -364,29 +422,30 @@
         cells[i * pitch : i * pitch + whole_rows] = block[:whole_rows]
         if whole_rows < pitch:
             tail = block[whole_rows:].astype(F32)
-            tail = jnp.concatenate([tail, jnp.zeros((pitch - rows, plan.columns), F32)], axis=0)
+            tail = jnp.concatenate([tail, jnp.zeros((pitch - rows, tail.shape[1]), F32)], axis=0)
             cells[i * pitch + whole_rows : (i + 1) * pitch] = tail.astype(BF16)
 
 
 def early_body(plan, ids, first, second, own0, peer0, own1_0, own1_1, *rest):
     outs, cells = rest[:4], rest[4]
-    own1 = (own1_0, own1_1)
     known = 3 * plan.pitch
-    for turn in range(2):
-        fill_cells(plan, cells, (own0[turn], peer0[turn], own1[1 - turn][...]))
-        for c in range(0, plan.columns, TILE):
+    for b, own1 in enumerate((own1_0, own1_1)):
+        block = slice(b * plan.cap, (b + 1) * plan.cap)
+        fill_cells(plan, cells, (own0[:, block], peer0[:, block], own1[...]))
+        for c in range(0, plan.cap, TILE):
             at = slice(c, c + TILE)
-            outs[2 * turn][:, at] = jnp.dot(first[:, :known], cells[:, at], preferred_element_type=F32)
-            outs[2 * turn + 1][:, at] = jnp.dot(second[:, :known], cells[:, at], preferred_element_type=F32)
-
-
-def source_body(plan, turn, ids, first, second, transfer, growth, mask, *rest):
-    (early_first, early_second, own0, own1, peer1, half0, half1, full0, sent0, full1, sent1, cells) = rest
-    total, rows, pitch = plan.total, plan.rows, plan.pitch
+            outs[2 * b][:, at] = jnp.dot(first[:, :known], cells[:, at], preferred_element_type=F32)
+            outs[2 * b + 1][:, at] = jnp.dot(second[:, :known], cells[:, at], preferred_element_type=F32)
+
+
+def source_body(plan, b, ids, first, second, transfer, growth, placed, *rest):
+    (early_first, early_second, own0, own1, peer1, half00, half01, half10, half11) = rest[:9]
+    *outs, cells, sources, leaving = rest[9:]
+    full0, sent0, full1 = outs[-6:-3] if b else outs
+    total, rows, pitch, cap, side = plan.total, plan.rows, plan.pitch, plan.cap, plan.side
     known = 3 * pitch
     fill_cells(plan, cells, (peer1[...],))
-    ocean = in_order(ids, mask[...].astype(F32), 0)[turn]
-    for c in range(0, plan.columns, TILE):
+    for c in range(0, cap, TILE):
         at = slice(c, c + TILE)
         piece = cells[:, at]
         forward = early_first[:, at] + jnp.dot(first[:, known:], piece, preferred_element_type=F32)
@@ -395,14 +454,27 @@
         nonlinear = jnp.dot(transfer[...], product, preferred_element_type=F32)
         level = forward[total : total + 1] / total
         damping = level * level / (1.0 + level * level)
-        for group, (own, half, full, sent) in enumerate(((own0, half0, full0, sent0), (own1, half1, full1, sent1))):
+        for group in range(2):
             begin = group * pitch
-            rate = spread(growth[begin : begin + rows], TILE)
-            spectra = (own[turn, :, at] if group == 0 else own[:, at]).astype(F32)
-            source = SOURCE_STEP * (nonlinear[begin : begin + rows] + (rate - damping) * spectra)
-            updated = ocean[:, at] * (half[:, at] + source.astype(BF16).astype(F32))
-            full[:, at] = updated
-            sent[:, at] = updated.astype(BF16)
+            spectra = (own1[:, at] if group else own0[:, b * cap + c : b * cap + c + TILE]).astype(F32)
+            spectra = jnp.concatenate([spectra, jnp.zeros((pitch - rows, TILE), F32)], axis=0)
+            rate = spread(growth[begin : begin + pitch], TILE)
+            source = SOURCE_STEP * (nonlinear[begin : begin + pitch] + (rate - damping) * spectra)
+            sources[begin : begin + pitch, at] = source.astype(BF16)
+    block = slice(b * side, (b + 1) * side)
+    for slot in range(2):
+        here = placed[:, slot * side : (slot + 1) * side]
+        spread_out = jnp.dot(sources[...], here, preferred_element_type=F32)
+        full0[slot] = (half00, half01)[slot][:, block] + spread_out[:rows]
+        leaving[:, slot * side : (slot + 1) * side] = full0[slot].astype(BF16)
+        full1[1 - slot] = (half10, half11)[1 - slot][:, block] + spread_out[pitch : pitch + rows]
+    gathered = gather_cells(leaving[...], placed[...]).astype(F32)
+    sent0[...] = jnp.concatenate([gathered, jnp.zeros((sent0.shape[0] - rows, cap), F32)], axis=0).astype(BF16)
+    if b:
+        parts = [full[r].astype(BF16) for r in range(2) for full in (outs[0], full1)]
+        for piece, (begin, end) in zip(outs[-3:], plan.pieces()):
+            ends = [(max(begin - i * side, 0), min(end - i * side, side)) for i in range(4)]
+            piece[...] = jnp.concatenate([parts[i][:, x:y] for i, (x, y) in enumerate(ends) if x < y], axis=1)
 
 
 def paired_shards(energy, depth_speed, ocean_mask, interp_first, interp_second, transfer_matrix, growth):
@@ -416,6 +488,8 @@
 
     inner = [(i, i ^ 1) for i in range(bands)]
     outer = [(i, (i + 1 if i % 2 else i - 1) % bands) for i in range(bands)]
+    outer_beside = [(2 * i + c, 2 * j + c) for i, j in outer if 0 < i < bands - 1 for c in range(2)]
+    outer_beside += [(2 * i + c, 2 * i + 1 - c) for i in (0, bands - 1) for c in range(2)]
     peers = [(0, 1), (1, 0)]
 
     def shape(*dims, kind=BF16):
@@ -434,12 +508,20 @@
     halo0 = lax.ppermute(field1, "band", inner)
     halo1 = lax.ppermute(field0, "band", outer)
 
+    cap, side = plan.cap, plan.side
+    def place(mask, neighbour, cost):
+        return call(functools.partial(place_body, plan, neighbour), ids, (mask,), [shape(cap, size)] * 2, cost=cost)
+
+    placed = place(ocean_mask, False, 2)
+    outer_placed = place(halo1, True, 0.01)
+
     def first_step(group, field, halo, spectra):
-        operands = (courant, depth_speed, ocean_mask, field, halo)
+        operands = (courant, depth_speed, ocean_mask, field, halo, *placed)
         outs = [shape(rows, size, kind=F32)] * 2 + spectra
-        return call(functools.partial(first_body, plan, group), ids, operands, outs, rims, limit=20, cost=2)
-
-    *half0, own0 = first_step(0, field0, halo0, [shape(2, rows, size)])
+        scratch = rims + [pltpu.VMEM((2, rows, size), BF16)]
+        return call(functools.partial(first_body, plan, group), ids, operands, outs, scratch, limit=20, cost=2)
+
+    *half0, own0 = first_step(0, field0, halo0, [shape(rows, 2 * cap)])
     peer0 = lax.ppermute(own0, "comp", peers)
     first, second, transfer, rate = call(
         functools.partial(weights_body, plan),
@@ -449,52 +531,65 @@
         [pltpu.VMEM((total, 4 * pitch), BF16)],
         cost=3,
     )
-    *half1, own1_0, own1_1 = first_step(1, field1, halo1, [shape(rows, size)] * 2)
+    *half1, own1_0, own1_1 = first_step(1, field1, halo1, [shape(rows, cap)] * 2)
     own1 = (own1_0, own1_1)
-    peer1 = [None, None]
-    peer1[1] = lax.ppermute(own1[1], "comp", peers)
-    peer1[0] = lax.ppermute(own1[0], "comp", peers)
+    peer1 = [lax.ppermute(own, "comp", peers) for own in own1]
     early = call(
         functools.partial(early_body, plan),
         ids,
         (first, second, own0, peer0, own1_0, own1_1),
-        [shape(plan.out_rows, size, kind=F32), shape(total, size, kind=F32)] * 2,
-        [pltpu.VMEM((3 * pitch, size), BF16)],
+        [shape(plan.out_rows, cap, kind=F32), shape(total, cap, kind=F32)] * 2,
+        [pltpu.VMEM((3 * pitch, cap), BF16)],
         limit=30,
         cost=4,
     )
 
-    full0, sent0, full1, sent1 = [None] * 2, [None] * 2, [None] * 2, [None] * 2
-    for turn in range(2):
-        full0[turn], sent0[turn], full1[1 - turn], sent1[1 - turn] = call(
-            functools.partial(source_body, plan, turn),
+    full0, sent0, full1 = [], [], []
+    for b in range(2):
+        own = call(
+            functools.partial(source_body, plan, b),
             ids,
-            (first, second, transfer, rate, ocean_mask, early[2 * turn], early[2 * turn + 1])
-            + (own0, own1[1 - turn], peer1[1 - turn], half0[turn], half1[1 - turn]),
-            [shape(rows, size, kind=F32), shape(rows, size)] * 2,
-            [pltpu.VMEM((pitch, size), BF16)],
+            (first, second, transfer, rate, placed[b], early[2 * b], early[2 * b + 1], own0, own1[b], peer1[b])
+            + (*half0, *half1, *full1),
+            [shape(2, rows, side, kind=F32), shape(rows + (24, 8)[b], cap), shape(2, rows, side, kind=F32)]
+            + [shape(rows, end - begin) for begin, end in plan.pieces()] * b,
+            [pltpu.VMEM((pitch, cap), BF16), pltpu.VMEM((2 * pitch, cap), BF16), pltpu.VMEM((rows, size), BF16)],
             limit=30,
             cost=4,
         )
-    rim1 = [lax.ppermute(x, "band", outer) for x in sent0]
-    rim0 = [lax.ppermute(x, "band", inner) for x in sent1]
-
-    def last_step(group, full, rim, more, outs, cost):
-        operands = (courant, depth_speed, ocean_mask, full[0], full[1], rim[1], rim[0]) + more
-        scratch = [pltpu.VMEM((2 * pitch, size), BF16)] + rims
-        return call(functools.partial(last_body, plan, group), ids, operands, outs, scratch, limit=30, cost=cost)
+        full0.append(own[0])
+        sent0.append(own[1])
+        full1.append(own[2])
+    rim1 = [lax.ppermute(sent0[0], "band", outer), lax.ppermute(sent0[1], ("band", "comp"), outer_beside)]
+    rim0 = [lax.ppermute(x, "band", inner) for x in own[3:]]
 
     width = 2 * plan.local
-    full0[0], rim1[0] = lax.optimization_barrier((full0[0], rim1[0]))
-    more = last_step(0, full0, rim0, (), [shape(width, size, kind=F32), shape(width, 2 * pitch)], 3)
-    (out,) = last_step(1, full1, rim1, tuple(more), [shape(*energy.shape)], 4)
+    done = pltpu.VMEM((2 * pitch, size), BF16)
+    partial, restore = call(
+        functools.partial(last_body, plan, 0),
+        ids,
+        (courant, depth_speed, ocean_mask, *full0, *rim0),
+        [shape(width, size, kind=F32), shape(width, 2 * pitch)],
+        [done] + rims,
+        limit=30,
+        cost=0.01,
+    )
+    (out,) = call(
+        functools.partial(last_body, plan, 1),
+        ids,
+        (courant, depth_speed, ocean_mask, *full1, *rim1, *outer_placed, partial, restore),
+        [shape(*energy.shape)],
+        [pltpu.VMEM((rows, size), BF16)] * 2 + [done] + rims,
+        limit=30,
+        cost=4,
+    )
     return out
 
 
 def solution(mesh):
     def shards(energy, *others):
         paired = lax.axis_size("comp") == 2 and lax.axis_size("band") % 2 == 0
-        if paired and energy.shape[0] % ND == 0 and energy.shape[1] == 2 and energy.shape[2] % TILE == 0:
+        if paired and energy.shape[0] % ND == 0 and energy.shape[1] == 2 and energy.shape[2] % (4 * TILE) == 0 and energy.shape[0] // 2 % 8:
             return paired_shards(energy, *others)
         return general_shards(energy, *others)
 

time: 64.3 us -> 56.7 us (0.88)
  waiting for transfers between devices: 22.9 us -> 10.3 us
  Pallas kernels: 28.3 us -> 35 us
  starting transfers between devices: 10.5 us -> 8.38 us
    ppermute x6 -> x7, waiting for transfers between devices: 12.6 us -> 2.46 us  [the longest x2 1.8 us: paired_shards(): peer1 = [lax.ppermute(own, 'comp', peers) for own in own1]]
    pallas_call x9 -> x11, Pallas kernels: 28.3 us -> 35 us  [call(): pl.pallas_call(body, in_specs=[SMEM] + [VMEM] * len(operands), out_specs=...]
    ppermute x1, waiting for transfers between devices: 10.3 us -> 7.88 us  [paired_shards(): halo1 = lax.ppermute(field0, 'band', outer)]
    ppermute x6 -> x7, starting transfers between devices: 5.81 us -> 4.33 us  [the longest x2 1.94 us: paired_shards(): peer1 = [lax.ppermute(own, 'comp', peers) for own in own1]]
    ppermute x1, starting transfers between devices: 1.98 us -> 1.3 us  [paired_shards(): peer0 = lax.ppermute(own0, 'comp', peers)]
  transfers between devices with their start and end apart: 9 -> 10, of which waited for: 5 -> 3; matrix products, arithmetic and copies ran while one was open for 0% -> 0% of each run, Pallas kernels for 34% -> 49%
where the time goes in v4:
time: 56.7 us; the launch traced here: 56.1 us
  Pallas kernels  35 us (62%)
  waiting for transfers between devices  10.3 us (18%)
  starting transfers between devices  8.38 us (15%)
  local copies, waits for them, and re-layouts  2.11 us (4%)
    pallas_call x11, Pallas kernels, call(): pl.pallas_call(body, in_specs=[SMEM] + [VMEM] * len(operands), out_specs=...  35 us
    ppermute x1, waiting for transfers between devices, paired_shards(): halo1 = lax.ppermute(field0, 'band', outer)  7.88 us
    ppermute x1, starting transfers between devices, paired_shards(): halo1 = lax.ppermute(field0, 'band', outer)  2.63 us
    unnamed x16, local copies, waits for them, and re-layouts  2.1 us
    ppermute x2, starting transfers between devices, paired_shards(): peer1 = [lax.ppermute(own, 'comp', peers) for own in own1]  1.94 us
    ppermute x2, waiting for transfers between devices, paired_shards(): peer1 = [lax.ppermute(own, 'comp', peers) for own in own1]  1.8 us
    ppermute x1, starting transfers between devices, paired_shards(): peer0 = lax.ppermute(own0, 'comp', peers)  1.3 us
    ppermute x1, starting transfers between devices, paired_shards(): lax.ppermute(sent0[0], 'band', outer)  1.24 us
  transfers between devices with their start and end apart: 10, of which 3 were waited for; matrix products, arithmetic and copies ran while one was open for 0% of the time, Pallas kernels for 49%

profile of v4, /device:TPU:1, one launch (start us, length us, event | category | flops | bytes accessed | tf_op | source)
XLA Modules:
  0.0 56.1 jit_solution(17897888816602951845)
XLA Ops:
  0.0 0.1 pad_add_fusion.ids
  0.1 0.7 %copy-done = s32[2,1024]{1,0:T(2,128)S(1)} copy-done((s32[2,1024]{1,0:T(2,128)S(1)}, s32[2,1024]{1,0:T(2,128)}, u32[]{:S(2)}) %copy-start) | copy-done | bytes 8216
  0.8 1.4 %copy-done.3 = bf16[360,2,1024]{2,1,0:T(2,128)(2,1)S(1)} copy-done((bf16[360,2,1024]{2,1,0:T(2,128)(2,1)S(1)}, bf16[360,2,1024]{2,1,0:T(2,128)(2,1)}, u32[]{:S(2)}) %copy-start.3) | copy-done | bytes 1474584
  2.2 2.2 %shard_map.73 = (bf16[2,184,1024]{2,1,0:T(8,128)(2,1)S(1)}, bf16[2,184,1024]{2,1,0:T(8,128)(2,1)S(1)}, f32[2,2,184,128]{3,2,1,0:T(8,128)S(1)}) custom-call(s32[3]{0:T(128)S(1)} %pad_add_fusion.ids, bf16[360,2,1024]{2,1,0:T(2,128)(2,1)S(1)} %copy-done.3, s32[2,1024]{1,0:T(2,128)S(1)} %copy-done), custom_call_target="tpu_custom_call" | custom-call | flops 2200000000 | tf_op jit(solution)/shard_map/pallas_call | solution.py:177
  4.4 0.1 collective-permute-start
  4.5 2.6 %collective-permute-start.2 = (bf16[2,184,1024]{2,1,0:T(8,128)(2,1)S(1)}, bf16[2,184,1024]{2,1,0:T(8,128)(2,1)S(1)}, u32[]{:S(2)}, u32[]{:S(2)}) collective-permute-start(bf16[2,184,1024]{2,1,0:T(8,128)(2,1)S(1)} %get-tuple-element.44.field), channel_id=1, source_target_pairs={{0,30},{2,4},{4,2},{6,8},{8,6},{10,12},{12,10},{14,16},{16,14},{18... | collective-permute-start | bytes 2261000 | tf_op jit(solution)/shard_map/ppermute | solution.py:509
  7.1 2.0 %shard_map.75 = (bf16[768,1024]{1,0:T(8,128)(2,1)S(1)}, bf16[768,1024]{1,0:T(8,128)(2,1)S(1)}) custom-call(s32[3]{0:T(128)S(1)} %pad_add_fusion.ids, s32[2,1024]{1,0:T(2,128)S(1)} %copy-done.1), custom_call_target="tpu_custom_call" | custom-call | flops 2200000000 | tf_op jit(solution)/shard_map/pallas_call | solution.py:177
  9.2 0.0 collective-permute-done.halo
  9.2 0.0 copy-start.7
  9.2 0.0 copy-start.4
  9.2 0.0 copy-start.5
  9.2 0.0 copy-start.6
  9.3 3.3 %shard_map.76 = (f32[184,1024]{1,0:T(8,128)S(1)}, f32[184,1024]{1,0:T(8,128)S(1)}, bf16[184,1536]{1,0:T(8,128)(2,1)S(1)}) custom-call(s32[3]{0:T(128)S(1)} %pad_add_fusion.ids, f32[2,2,184,128]{3,2,1,0:T(8,128)S(1)} %get-tuple-element.38.courant, f32[2,1024]{1,0:T(2,128)S(1)} %copy-done.2, s32[2,1024]{1,0:T(2,128)S(1)} %copy-done.1, ...), custom_call_target="tpu_custom_call" | custom-call | flops 2200000000 | tf_op jit(solution)/shard_map/pallas_call | solution.py:177
  12.5 1.3 %collective-permute-start.1 = (bf16[184,1536]{1,0:T(8,128)(2,1)S(1)}, bf16[184,1536]{1,0:T(8,128)(2,1)S(1)}, u32[]{:S(2)}, u32[]{:S(2)}) collective-permute-start(bf16[184,1536]{1,0:T(8,128)(2,1)S(1)} %get-tuple-element.47.own0.rest_2_), channel_id=1, source_target_pairs={{0,1},{1,0},{2,3},{3,2},{4,5},{5,4},{6,7},{7,6},{8,9},{9,8},{10,11... | collective-permute-start | bytes 1695752 | tf_op jit(solution)/shard_map/ppermute | solution.py:525
  13.9 3.1 %shard_map.74 = (bf16[736,768]{1,0:T(8,128)(2,1)S(1)}, bf16[720,768]{1,0:T(8,128)(2,1)S(1)}, bf16[384,720]{1,0:T(8,128)(2,1)S(1)}, f32[384,128]{1,0:T(8,128)S(1)}) custom-call(s32[3]{0:T(128)S(1)} %pad_add_fusion.ids, bf16[720,720]{1,0:T(8,128)(2,1)S(1)} %copy-done.4, bf16[720,720]{1,0:T(8,128)(2,1)S(1)} %copy-done.5, bf16[720,720]{1,0:T(8,128)(2,1)S(1)} %copy-done.6, ...), custom_call_target="tpu_custom_call" | custom-call | flops 3300000000 | tf_op jit(solution)/shard_map/pallas_call | solution.py:177
  16.9 7.9 %collective-permute-done.2.halo.mask = bf16[2,184,1024]{2,1,0:T(8,128)(2,1)S(1)} collective-permute-done((bf16[2,184,1024]{2,1,0:T(8,128)(2,1)S(1)}, bf16[2,184,1024]{2,1,0:T(8,128)(2,1)S(1)}, u32[]{:S(2)}, u32[]{:S(2)}) %collective-permute-start.2) | collective-permute-done | bytes 753696 | tf_op jit(solution)/shard_map/ppermute | solution.py:509
  24.8 3.5 %shard_map.77 = (f32[184,1024]{1,0:T(8,128)S(1)}, f32[184,1024]{1,0:T(8,128)S(1)}, bf16[184,768]{1,0:T(8,128)(2,1)S(1)}, bf16[184,768]{1,0:T(8,128)(2,1)S(1)}) custom-call(s32[3]{0:T(128)S(1)} %pad_add_fusion.ids, f32[2,2,184,128]{3,2,1,0:T(8,128)S(1)} %get-tuple-element.38.courant, f32[2,1024]{1,0:T(2,128)S(1)} %copy-done.2, s32[2,1024]{1,0:T(2,128)S(1)} %copy-done.1, ...), custom_call_target="tpu_custom_call" | custom-call | flops 2200000000 | tf_op jit(solution)/shard_map/pallas_call | solution.py:177
  28.3 1.9 %collective-permute-start.3 = (bf16[184,768]{1,0:T(8,128)(2,1)S(1)}, bf16[184,768]{1,0:T(8,128)(2,1)S(1)}, u32[]{:S(2)}, u32[]{:S(2)}) collective-permute-start(bf16[184,768]{1,0:T(8,128)(2,1)S(1)} %get-tuple-element.48.own1_0.rest_3_), channel_id=1, source_target_pairs={{0,1},{1,0},{2,3},{3,2},{4,5},{5,4},{6,7},{7,6},{8,9},{9,8},{10,11... | collective-permute-start | bytes 847880 | tf_op jit(solution)/shard_map/ppermute | solution.py:536
  30.2 0.1 collective-permute-start.4
  30.3 0.0 collective-permute-done.1.peer0
  30.3 4.2 %shard_map.78 = (f32[736,768]{1,0:T(8,128)S(1)}, f32[720,768]{1,0:T(8,128)S(1)}, f32[736,768]{1,0:T(8,128)S(1)}, f32[720,768]{1,0:T(8,128)S(1)}) custom-call(s32[3]{0:T(128)S(1)} %pad_add_fusion.ids, bf16[736,768]{1,0:T(8,128)(2,1)S(1)} %get-tuple-element.39.first, bf16[720,768]{1,0:T(8,128)(2,1)S(1)} %get-tuple-element.40.second, ...), custom_call_target="tpu_custom_call" | custom-call | flops 4400000000 | tf_op jit(solution)/shard_map/pallas_call | solution.py:177
  34.4 1.8 %collective-permute-done.3.rest_4_ = bf16[184,768]{1,0:T(8,128)(2,1)S(1)} collective-permute-done((bf16[184,768]{1,0:T(8,128)(2,1)S(1)}, bf16[184,768]{1,0:T(8,128)(2,1)S(1)}, u32[]{:S(2)}, u32[]{:S(2)}) %collective-permute-start.3) | collective-permute-done | bytes 282656 | tf_op jit(solution)/shard_map/ppermute | solution.py:536
  36.2 3.1 %shard_map.79 = (f32[2,184,512]{2,1,0:T(8,128)S(1)}, bf16[208,768]{1,0:T(8,128)(2,1)S(1)}, f32[2,184,512]{2,1,0:T(8,128)S(1)}) custom-call(s32[3]{0:T(128)S(1)} %pad_add_fusion.ids, bf16[736,768]{1,0:T(8,128)(2,1)S(1)} %get-tuple-element.39.first, bf16[720,768]{1,0:T(8,128)(2,1)S(1)} %get-tuple-element.40.second, ...), custom_call_target="tpu_custom_call" | custom-call | flops 4400000000 | tf_op jit(solution)/shard_map/pallas_call | solution.py:177
  39.4 1.2 %collective-permute-start.5 = (bf16[208,768]{1,0:T(8,128)(2,1)S(1)}, bf16[208,768]{1,0:T(8,128)(2,1)S(1)}, u32[]{:S(2)}, u32[]{:S(2)}) collective-permute-start(bf16[208,768]{1,0:T(8,128)(2,1)S(1)} %get-tuple-element.60), channel_id=1, source_target_pairs={{0,30},{2,4},{4,2},{6,8},{8,6},{10,12},{12,10},{14,16},{16,14},{18... | collective-permute-start | bytes 958472 | tf_op jit(solution)/shard_map/ppermute | solution.py:563
  40.6 0.0 collective-permute-done.4.rest_4_
  40.6 3.1 %shard_map.80 = (f32[2,184,512]{2,1,0:T(8,128)S(1)}, bf16[192,768]{1,0:T(8,128)(2,1)S(1)}, f32[2,184,512]{2,1,0:T(8,128)S(1)}, bf16[184,768]{1,0:T(8,128)(2,1)S(...) custom-call(s32[3]{0:T(128)S(1)} %pad_add_fusion.ids, bf16[736,768]{1,0:T(8,128)(2,1)S(1)} %get-tuple-element.39.first, ...), custom_call_target="tpu_custom_call" | custom-call | flops 4400000000 | tf_op jit(solution)/shard_map/pallas_call | solution.py:177
  43.8 0.6 %collective-permute-start.6 = (bf16[192,768]{1,0:T(8,128)(2,1)S(1)}, bf16[192,768]{1,0:T(8,128)(2,1)S(1)}, u32[]{:S(2)}, u32[]{:S(2)}) collective-permute-start(bf16[192,768]{1,0:T(8,128)(2,1)S(1)} %get-tuple-element.61), channel_id=1, source_target_pairs={{2,4},{3,5},{4,2},{5,3},{6,8},{7,9},{8,6},{9,7},{10,12},{11,13},{1... | collective-permute-start | bytes 884744 | tf_op jit(solution)/shard_map/ppermute | solution.py:563
  44.4 0.5 collective-permute-start.8
  44.9 2.1 %shard_map.81 = (bf16[768,1024]{1,0:T(8,128)(2,1)S(1)}, bf16[768,1024]{1,0:T(8,128)(2,1)S(1)}) custom-call(s32[3]{0:T(128)S(1)} %pad_add_fusion.ids, bf16[2,184,1024]{2,1,0:T(8,128)(2,1)S(1)} %collective-permute-done.2.halo.mask), custom_call_target="tpu_custom_call" | custom-call | flops 11000000 | tf_op jit(solution)/shard_map/pallas_call | solution.py:177
  47.1 3.1 %shard_map.82 = (f32[720,1024]{1,0:T(8,128)S(1)}, bf16[720,384]{1,0:T(8,128)(2,1)S(1)}) custom-call(s32[3]{0:T(128)S(1)} %pad_add_fusion.ids, f32[2,2,184,128]{3,2,1,0:T(8,128)S(1)} %get-tuple-element.38.courant, f32[2,1024]{1,0:T(2,128)S(1)} %copy-done.2, s32[2,1024]{1,0:T(2,128)S(1)} %copy-done.1, f32[2,184,512]{2,1,0:T(8,128)S(1)} %get-tuple-element.64.full0, ...), custom_call_target="tpu_custom_call" | custom-call | flops 11000000 | tf_op jit(solution)/shard_map/pallas_call | solution.py:177
  50.2 0.6 %collective-permute-done.6.rest_1_ = bf16[192,768]{1,0:T(8,128)(2,1)S(1)} collective-permute-done((bf16[192,768]{1,0:T(8,128)(2,1)S(1)}, bf16[192,768]{1,0:T(8,128)(2,1)S(1)}, u32[]{:S(2)}, u32[]{:S(2)}) %collective-permute-start.6) | collective-permute-done | bytes 294944 | tf_op jit(solution)/shard_map/ppermute | solution.py:563
  50.9 5.2 %shard_map.83 = bf16[360,2,1024]{2,1,0:T(2,128)(2,1)} custom-call(s32[3]{0:T(128)S(1)} %pad_add_fusion.ids, f32[2,2,184,128]{3,2,1,0:T(8,128)S(1)} %get-tuple-element.38.courant, f32[2,1024]{1,0:T(2,128)S(1)} %copy-done.2, s32[2,1024]{1,0:T(2,128)S(1)} %copy-done.1, f32[2,184,512]{2,1,0:T(8,128)S(1)} %get-tuple-element.56.rest_9_.full0, ...), custom_call_target="tpu_custom_call" | custom-call | flops 4400000000 | tf_op jit(solution)/shard_map/pallas_call | solution.py:177
  (17 shorter events, 0.0 us)
Async XLA Ops:
  0.1 0.7 %copy-start = (s32[2,1024]{1,0:T(2,128)S(1)}, s32[2,1024]{1,0:T(2,128)}, u32[]{:S(2)}) copy-start(s32[2,1024]{1,0:T(2,128)} %mask.11) | copy-start | bytes 24580
  0.8 1.4 %copy-start.3 = (bf16[360,2,1024]{2,1,0:T(2,128)(2,1)S(1)}, bf16[360,2,1024]{2,1,0:T(2,128)(2,1)}, u32[]{:S(2)}) copy-start(bf16[360,2,1024]{2,1,0:T(2,128)(2,1)} %energy.1) | copy-start | bytes 4423684
  2.1 5.0 %copy-start.1 = (s32[2,1024]{1,0:T(2,128)S(1)}, s32[2,1024]{1,0:T(2,128)}, u32[]{:S(2)}) copy-start(s32[2,1024]{1,0:T(2,128)} %mask.11) | copy-start | bytes 24580
  4.4 4.8 %collective-permute-start = (bf16[2,184,1024]{2,1,0:T(8,128)(2,1)S(1)}, bf16[2,184,1024]{2,1,0:T(8,128)(2,1)S(1)}, u32[]{:S(2)}, u32[]{:S(2)}) collective-permute-start(bf16[2,184,1024]{2,1,0:T(8,128)(2,1)S(1)} %get-tuple-element.45.field), channel_id=1, source_target_pairs={{0,2},{2,0},{4,6},{6,4},{8,10},{10,8},{12,14},{14,12},{16,18},{18,... | collective-permute-start | bytes 2261000 | tf_op jit(solution)/shard_map/ppermute | solution.py:508
  4.5 4.7 %copy-start.2 = (f32[2,1024]{1,0:T(2,128)S(1)}, f32[2,1024]{1,0:T(2,128)}, u32[]{:S(2)}) copy-start(f32[2,1024]{1,0:T(2,128)} %depth.7) | copy-start | bytes 24580
  4.5 20.3 %collective-permute-start.2 = (bf16[2,184,1024]{2,1,0:T(8,128)(2,1)S(1)}, bf16[2,184,1024]{2,1,0:T(8,128)(2,1)S(1)}, u32[]{:S(2)}, u32[]{:S(2)}) collective-permute-start(bf16[2,184,1024]{2,1,0:T(8,128)(2,1)S(1)} %get-tuple-element.44.field), channel_id=1, source_target_pairs={{0,30},{2,4},{4,2},{6,8},{8,6},{10,12},{12,10},{14,16},{16,14},{18... | collective-permute-start | bytes 2261000 | tf_op jit(solution)/shard_map/ppermute | solution.py:509
  9.2 4.6 %copy-start.7 = (f32[720]{0:T(1024)S(1)}, f32[720]{0:T(1024)}, u32[]{:S(2)}) copy-start(f32[720]{0:T(1024)} %param.13) | copy-start | bytes 8644
  9.2 4.6 %copy-start.4 = (bf16[720,720]{1,0:T(8,128)(2,1)S(1)}, bf16[720,720]{1,0:T(8,128)(2,1)}, u32[]{:S(2)}) copy-start(bf16[720,720]{1,0:T(8,128)(2,1)} %first.1) | copy-start | bytes 3110404
  9.2 4.6 %copy-start.5 = (bf16[720,720]{1,0:T(8,128)(2,1)S(1)}, bf16[720,720]{1,0:T(8,128)(2,1)}, u32[]{:S(2)}) copy-start(bf16[720,720]{1,0:T(8,128)(2,1)} %second.1) | copy-start | bytes 3110404
  9.2 4.6 %copy-start.6 = (bf16[720,720]{1,0:T(8,128)(2,1)S(1)}, bf16[720,720]{1,0:T(8,128)(2,1)}, u32[]{:S(2)}) copy-start(bf16[720,720]{1,0:T(8,128)(2,1)} %transfer.1) | copy-start | bytes 3110404
  12.5 17.8 %collective-permute-start.1 = (bf16[184,1536]{1,0:T(8,128)(2,1)S(1)}, bf16[184,1536]{1,0:T(8,128)(2,1)S(1)}, u32[]{:S(2)}, u32[]{:S(2)}) collective-permute-start(bf16[184,1536]{1,0:T(8,128)(2,1)S(1)} %get-tuple-element.47.own0.rest_2_), channel_id=1, source_target_pairs={{0,1},{1,0},{2,3},{3,2},{4,5},{5,4},{6,7},{7,6},{8,9},{9,8},{10,11... | collective-permute-start | bytes 1695752 | tf_op jit(solution)/shard_map/ppermute | solution.py:525
  28.3 7.9 %collective-permute-start.3 = (bf16[184,768]{1,0:T(8,128)(2,1)S(1)}, bf16[184,768]{1,0:T(8,128)(2,1)S(1)}, u32[]{:S(2)}, u32[]{:S(2)}) collective-permute-start(bf16[184,768]{1,0:T(8,128)(2,1)S(1)} %get-tuple-element.48.own1_0.rest_3_), channel_id=1, source_target_pairs={{0,1},{1,0},{2,3},{3,2},{4,5},{5,4},{6,7},{7,6},{8,9},{9,8},{10,11... | collective-permute-start | bytes 847880 | tf_op jit(solution)/shard_map/ppermute | solution.py:536
  30.2 10.4 %collective-permute-start.4 = (bf16[184,768]{1,0:T(8,128)(2,1)S(1)}, bf16[184,768]{1,0:T(8,128)(2,1)S(1)}, u32[]{:S(2)}, u32[]{:S(2)}) collective-permute-start(bf16[184,768]{1,0:T(8,128)(2,1)S(1)} %get-tuple-element.49.own1_1.rest_3_), channel_id=1, source_target_pairs={{0,1},{1,0},{2,3},{3,2},{4,5},{5,4},{6,7},{7,6},{8,9},{9,8},{10,11... | collective-permute-start | bytes 847880 | tf_op jit(solution)/shard_map/ppermute | solution.py:536
  39.4 11.5 %collective-permute-start.5 = (bf16[208,768]{1,0:T(8,128)(2,1)S(1)}, bf16[208,768]{1,0:T(8,128)(2,1)S(1)}, u32[]{:S(2)}, u32[]{:S(2)}) collective-permute-start(bf16[208,768]{1,0:T(8,128)(2,1)S(1)} %get-tuple-element.60), channel_id=1, source_target_pairs={{0,30},{2,4},{4,2},{6,8},{8,6},{10,12},{12,10},{14,16},{16,14},{18... | collective-permute-start | bytes 958472 | tf_op jit(solution)/shard_map/ppermute | solution.py:563
  43.8 7.1 %collective-permute-start.6 = (bf16[192,768]{1,0:T(8,128)(2,1)S(1)}, bf16[192,768]{1,0:T(8,128)(2,1)S(1)}, u32[]{:S(2)}, u32[]{:S(2)}) collective-permute-start(bf16[192,768]{1,0:T(8,128)(2,1)S(1)} %get-tuple-element.61), channel_id=1, source_target_pairs={{2,4},{3,5},{4,2},{5,3},{6,8},{7,9},{8,6},{9,7},{10,12},{11,13},{1... | collective-permute-start | bytes 884744 | tf_op jit(solution)/shard_map/ppermute | solution.py:563
  44.4 2.6 %collective-permute-start.7 = (bf16[184,768]{1,0:T(8,128)(2,1)S(1)}, bf16[184,768]{1,0:T(8,128)(2,1)S(1)}, u32[]{:S(2)}, u32[]{:S(2)}) collective-permute-start(bf16[184,768]{1,0:T(8,128)(2,1)S(1)} %get-tuple-element.66), channel_id=1, source_target_pairs={{0,2},{2,0},{4,6},{6,4},{8,10},{10,8},{12,14},{14,12},{16,18},{18,... | collective-permute-start | bytes 847880 | tf_op jit(solution)/shard_map/ppermute | solution.py:564
  44.4 2.6 %collective-permute-start.8 = (bf16[184,640]{1,0:T(8,128)(2,1)S(1)}, bf16[184,640]{1,0:T(8,128)(2,1)S(1)}, u32[]{:S(2)}, u32[]{:S(2)}) collective-permute-start(bf16[184,640]{1,0:T(8,128)(2,1)S(1)} %get-tuple-element.67), channel_id=1, source_target_pairs={{0,2},{2,0},{4,6},{6,4},{8,10},{10,8},{12,14},{14,12},{16,18},{18,... | collective-permute-start | bytes 706568 | tf_op jit(solution)/shard_map/ppermute | solution.py:564
  44.9 2.1 %collective-permute-start.9 = (bf16[184,640]{1,0:T(8,128)(2,1)S(1)}, bf16[184,640]{1,0:T(8,128)(2,1)S(1)}, u32[]{:S(2)}, u32[]{:S(2)}) collective-permute-start(bf16[184,640]{1,0:T(8,128)(2,1)S(1)} %get-tuple-element.68), channel_id=1, source_target_pairs={{0,2},{2,0},{4,6},{6,4},{8,10},{10,8},{12,14},{14,12},{16,18},{18,... | collective-permute-start | bytes 706568 | tf_op jit(solution)/shard_map/ppermute | solution.py:564

commit v5 on v4

--- a/solution.py
+++ b/solution.py
@@ -402,7 +402,11 @@
         chosen.append(spread(comp, total) == lax.broadcasted_iota(jnp.int32, (pitch, total), 1))
     first_out[:total] = jnp.dot(first[...], columns[...], preferred_element_type=F32).astype(BF16)
     extra = plan.out_rows - total
-    first_out[total:] = one_hot(lax.broadcasted_iota(jnp.int32, (extra, 4 * pitch), 0) == 0)
+    place = lax.broadcasted_iota(jnp.int32, (extra, 4 * pitch), 1)
+    for i in range(1, 4):
+        place = jnp.where(place >= pitch, place - pitch, place)
+    top = lax.broadcasted_iota(jnp.int32, (extra, 4 * pitch), 0) == 0
+    first_out[total:] = one_hot(jnp.logical_and(top, place < plan.slots))
     second_out[...] = jnp.dot(second[...], columns[...], preferred_element_type=F32).astype(BF16)
     for group in range(2):
         at = slice(group * pitch, (group + 1) * pitch)

time: 56.7 us -> 56.7 us (level)
  no operation moved by 1% of the time
where the time goes in v5:
time: 56.7 us; the launch traced here: 56.1 us
  Pallas kernels  35 us (62%)
  waiting for transfers between devices  10.3 us (18%)
  starting transfers between devices  8.38 us (15%)
  local copies, waits for them, and re-layouts  2.11 us (4%)
    pallas_call x11, Pallas kernels, call(): pl.pallas_call(body, in_specs=[SMEM] + [VMEM] * len(operands), out_specs=...  35 us
    ppermute x1, waiting for transfers between devices, paired_shards(): halo1 = lax.ppermute(field0, 'band', outer)  7.88 us
    ppermute x1, starting transfers between devices, paired_shards(): halo1 = lax.ppermute(field0, 'band', outer)  2.63 us
    unnamed x16, local copies, waits for them, and re-layouts  2.1 us
    ppermute x2, starting transfers between devices, paired_shards(): peer1 = [lax.ppermute(own, 'comp', peers) for own in own1]  1.94 us
    ppermute x2, waiting for transfers between devices, paired_shards(): peer1 = [lax.ppermute(own, 'comp', peers) for own in own1]  1.8 us
    ppermute x1, starting transfers between devices, paired_shards(): peer0 = lax.ppermute(own0, 'comp', peers)  1.3 us
    ppermute x1, starting transfers between devices, paired_shards(): lax.ppermute(sent0[0], 'band', outer)  1.24 us
  transfers between devices with their start and end apart: 10, of which 3 were waited for; matrix products, arithmetic and copies ran while one was open for 0% of the time, Pallas kernels for 49%

profile of v5, /device:TPU:1, one launch (start us, length us, event | category | flops | bytes accessed | tf_op | source)
XLA Modules:
  0.0 56.1 jit_solution(6642846608402980470)
XLA Ops:
  0.0 0.1 pad_add_fusion.ids
  0.1 0.7 %copy-done = s32[2,1024]{1,0:T(2,128)S(1)} copy-done((s32[2,1024]{1,0:T(2,128)S(1)}, s32[2,1024]{1,0:T(2,128)}, u32[]{:S(2)}) %copy-start) | copy-done | bytes 8216
  0.8 1.4 %copy-done.3 = bf16[360,2,1024]{2,1,0:T(2,128)(2,1)S(1)} copy-done((bf16[360,2,1024]{2,1,0:T(2,128)(2,1)S(1)}, bf16[360,2,1024]{2,1,0:T(2,128)(2,1)}, u32[]{:S(2)}) %copy-start.3) | copy-done | bytes 1474584
  2.2 2.2 %shard_map.73 = (bf16[2,184,1024]{2,1,0:T(8,128)(2,1)S(1)}, bf16[2,184,1024]{2,1,0:T(8,128)(2,1)S(1)}, f32[2,2,184,128]{3,2,1,0:T(8,128)S(1)}) custom-call(s32[3]{0:T(128)S(1)} %pad_add_fusion.ids, bf16[360,2,1024]{2,1,0:T(2,128)(2,1)S(1)} %copy-done.3, s32[2,1024]{1,0:T(2,128)S(1)} %copy-done), custom_call_target="tpu_custom_call" | custom-call | flops 2200000000 | tf_op jit(solution)/shard_map/pallas_call | solution.py:177
  4.4 0.1 collective-permute-start
  4.5 2.6 %collective-permute-start.2 = (bf16[2,184,1024]{2,1,0:T(8,128)(2,1)S(1)}, bf16[2,184,1024]{2,1,0:T(8,128)(2,1)S(1)}, u32[]{:S(2)}, u32[]{:S(2)}) collective-permute-start(bf16[2,184,1024]{2,1,0:T(8,128)(2,1)S(1)} %get-tuple-element.44.field), channel_id=1, source_target_pairs={{0,30},{2,4},{4,2},{6,8},{8,6},{10,12},{12,10},{14,16},{16,14},{18... | collective-permute-start | bytes 2261000 | tf_op jit(solution)/shard_map/ppermute | solution.py:513
  7.1 2.0 %shard_map.75 = (bf16[768,1024]{1,0:T(8,128)(2,1)S(1)}, bf16[768,1024]{1,0:T(8,128)(2,1)S(1)}) custom-call(s32[3]{0:T(128)S(1)} %pad_add_fusion.ids, s32[2,1024]{1,0:T(2,128)S(1)} %copy-done.1), custom_call_target="tpu_custom_call" | custom-call | flops 2200000000 | tf_op jit(solution)/shard_map/pallas_call | solution.py:177
  9.2 0.0 collective-permute-done.halo
  9.2 0.0 copy-start.7
  9.2 0.0 copy-start.4
  9.2 0.0 copy-start.5
  9.2 0.0 copy-start.6
  9.3 3.3 %shard_map.76 = (f32[184,1024]{1,0:T(8,128)S(1)}, f32[184,1024]{1,0:T(8,128)S(1)}, bf16[184,1536]{1,0:T(8,128)(2,1)S(1)}) custom-call(s32[3]{0:T(128)S(1)} %pad_add_fusion.ids, f32[2,2,184,128]{3,2,1,0:T(8,128)S(1)} %get-tuple-element.38.courant, f32[2,1024]{1,0:T(2,128)S(1)} %copy-done.2, s32[2,1024]{1,0:T(2,128)S(1)} %copy-done.1, ...), custom_call_target="tpu_custom_call" | custom-call | flops 2200000000 | tf_op jit(solution)/shard_map/pallas_call | solution.py:177
  12.5 1.3 %collective-permute-start.1 = (bf16[184,1536]{1,0:T(8,128)(2,1)S(1)}, bf16[184,1536]{1,0:T(8,128)(2,1)S(1)}, u32[]{:S(2)}, u32[]{:S(2)}) collective-permute-start(bf16[184,1536]{1,0:T(8,128)(2,1)S(1)} %get-tuple-element.47.own0.rest_2_), channel_id=1, source_target_pairs={{0,1},{1,0},{2,3},{3,2},{4,5},{5,4},{6,7},{7,6},{8,9},{9,8},{10,11... | collective-permute-start | bytes 1695752 | tf_op jit(solution)/shard_map/ppermute | solution.py:529
  13.9 3.1 %shard_map.74 = (bf16[736,768]{1,0:T(8,128)(2,1)S(1)}, bf16[720,768]{1,0:T(8,128)(2,1)S(1)}, bf16[384,720]{1,0:T(8,128)(2,1)S(1)}, f32[384,128]{1,0:T(8,128)S(1)}) custom-call(s32[3]{0:T(128)S(1)} %pad_add_fusion.ids, bf16[720,720]{1,0:T(8,128)(2,1)S(1)} %copy-done.4, bf16[720,720]{1,0:T(8,128)(2,1)S(1)} %copy-done.5, bf16[720,720]{1,0:T(8,128)(2,1)S(1)} %copy-done.6, ...), custom_call_target="tpu_custom_call" | custom-call | flops 3300000000 | tf_op jit(solution)/shard_map/pallas_call | solution.py:177
  16.9 7.9 %collective-permute-done.2.halo.mask = bf16[2,184,1024]{2,1,0:T(8,128)(2,1)S(1)} collective-permute-done((bf16[2,184,1024]{2,1,0:T(8,128)(2,1)S(1)}, bf16[2,184,1024]{2,1,0:T(8,128)(2,1)S(1)}, u32[]{:S(2)}, u32[]{:S(2)}) %collective-permute-start.2) | collective-permute-done | bytes 753696 | tf_op jit(solution)/shard_map/ppermute | solution.py:513
  24.8 3.5 %shard_map.77 = (f32[184,1024]{1,0:T(8,128)S(1)}, f32[184,1024]{1,0:T(8,128)S(1)}, bf16[184,768]{1,0:T(8,128)(2,1)S(1)}, bf16[184,768]{1,0:T(8,128)(2,1)S(1)}) custom-call(s32[3]{0:T(128)S(1)} %pad_add_fusion.ids, f32[2,2,184,128]{3,2,1,0:T(8,128)S(1)} %get-tuple-element.38.courant, f32[2,1024]{1,0:T(2,128)S(1)} %copy-done.2, s32[2,1024]{1,0:T(2,128)S(1)} %copy-done.1, ...), custom_call_target="tpu_custom_call" | custom-call | flops 2200000000 | tf_op jit(solution)/shard_map/pallas_call | solution.py:177
  28.3 1.9 %collective-permute-start.3 = (bf16[184,768]{1,0:T(8,128)(2,1)S(1)}, bf16[184,768]{1,0:T(8,128)(2,1)S(1)}, u32[]{:S(2)}, u32[]{:S(2)}) collective-permute-start(bf16[184,768]{1,0:T(8,128)(2,1)S(1)} %get-tuple-element.48.own1_0.rest_3_), channel_id=1, source_target_pairs={{0,1},{1,0},{2,3},{3,2},{4,5},{5,4},{6,7},{7,6},{8,9},{9,8},{10,11... | collective-permute-start | bytes 847880 | tf_op jit(solution)/shard_map/ppermute | solution.py:540
  30.2 0.1 collective-permute-start.4
  30.3 0.0 collective-permute-done.1.peer0
  30.3 4.2 %shard_map.78 = (f32[736,768]{1,0:T(8,128)S(1)}, f32[720,768]{1,0:T(8,128)S(1)}, f32[736,768]{1,0:T(8,128)S(1)}, f32[720,768]{1,0:T(8,128)S(1)}) custom-call(s32[3]{0:T(128)S(1)} %pad_add_fusion.ids, bf16[736,768]{1,0:T(8,128)(2,1)S(1)} %get-tuple-element.39.first, bf16[720,768]{1,0:T(8,128)(2,1)S(1)} %get-tuple-element.40.second, ...), custom_call_target="tpu_custom_call" | custom-call | flops 4400000000 | tf_op jit(solution)/shard_map/pallas_call | solution.py:177
  34.4 1.8 %collective-permute-done.3.rest_4_ = bf16[184,768]{1,0:T(8,128)(2,1)S(1)} collective-permute-done((bf16[184,768]{1,0:T(8,128)(2,1)S(1)}, bf16[184,768]{1,0:T(8,128)(2,1)S(1)}, u32[]{:S(2)}, u32[]{:S(2)}) %collective-permute-start.3) | collective-permute-done | bytes 282656 | tf_op jit(solution)/shard_map/ppermute | solution.py:540
  36.2 3.1 %shard_map.79 = (f32[2,184,512]{2,1,0:T(8,128)S(1)}, bf16[208,768]{1,0:T(8,128)(2,1)S(1)}, f32[2,184,512]{2,1,0:T(8,128)S(1)}) custom-call(s32[3]{0:T(128)S(1)} %pad_add_fusion.ids, bf16[736,768]{1,0:T(8,128)(2,1)S(1)} %get-tuple-element.39.first, bf16[720,768]{1,0:T(8,128)(2,1)S(1)} %get-tuple-element.40.second, ...), custom_call_target="tpu_custom_call" | custom-call | flops 4400000000 | tf_op jit(solution)/shard_map/pallas_call | solution.py:177
  39.4 1.2 %collective-permute-start.5 = (bf16[208,768]{1,0:T(8,128)(2,1)S(1)}, bf16[208,768]{1,0:T(8,128)(2,1)S(1)}, u32[]{:S(2)}, u32[]{:S(2)}) collective-permute-start(bf16[208,768]{1,0:T(8,128)(2,1)S(1)} %get-tuple-element.60), channel_id=1, source_target_pairs={{0,30},{2,4},{4,2},{6,8},{8,6},{10,12},{12,10},{14,16},{16,14},{18... | collective-permute-start | bytes 958472 | tf_op jit(solution)/shard_map/ppermute | solution.py:567
  40.6 0.0 collective-permute-done.4.rest_4_
  40.6 3.1 %shard_map.80 = (f32[2,184,512]{2,1,0:T(8,128)S(1)}, bf16[192,768]{1,0:T(8,128)(2,1)S(1)}, f32[2,184,512]{2,1,0:T(8,128)S(1)}, bf16[184,768]{1,0:T(8,128)(2,1)S(...) custom-call(s32[3]{0:T(128)S(1)} %pad_add_fusion.ids, bf16[736,768]{1,0:T(8,128)(2,1)S(1)} %get-tuple-element.39.first, ...), custom_call_target="tpu_custom_call" | custom-call | flops 4400000000 | tf_op jit(solution)/shard_map/pallas_call | solution.py:177
  43.8 0.6 %collective-permute-start.6 = (bf16[192,768]{1,0:T(8,128)(2,1)S(1)}, bf16[192,768]{1,0:T(8,128)(2,1)S(1)}, u32[]{:S(2)}, u32[]{:S(2)}) collective-permute-start(bf16[192,768]{1,0:T(8,128)(2,1)S(1)} %get-tuple-element.61), channel_id=1, source_target_pairs={{2,4},{3,5},{4,2},{5,3},{6,8},{7,9},{8,6},{9,7},{10,12},{11,13},{1... | collective-permute-start | bytes 884744 | tf_op jit(solution)/shard_map/ppermute | solution.py:567
  44.4 0.5 collective-permute-start.8
  44.9 2.1 %shard_map.81 = (bf16[768,1024]{1,0:T(8,128)(2,1)S(1)}, bf16[768,1024]{1,0:T(8,128)(2,1)S(1)}) custom-call(s32[3]{0:T(128)S(1)} %pad_add_fusion.ids, bf16[2,184,1024]{2,1,0:T(8,128)(2,1)S(1)} %collective-permute-done.2.halo.mask), custom_call_target="tpu_custom_call" | custom-call | flops 11000000 | tf_op jit(solution)/shard_map/pallas_call | solution.py:177
  47.1 3.1 %shard_map.82 = (f32[720,1024]{1,0:T(8,128)S(1)}, bf16[720,384]{1,0:T(8,128)(2,1)S(1)}) custom-call(s32[3]{0:T(128)S(1)} %pad_add_fusion.ids, f32[2,2,184,128]{3,2,1,0:T(8,128)S(1)} %get-tuple-element.38.courant, f32[2,1024]{1,0:T(2,128)S(1)} %copy-done.2, s32[2,1024]{1,0:T(2,128)S(1)} %copy-done.1, f32[2,184,512]{2,1,0:T(8,128)S(1)} %get-tuple-element.64.full0, ...), custom_call_target="tpu_custom_call" | custom-call | flops 11000000 | tf_op jit(solution)/shard_map/pallas_call | solution.py:177
  50.2 0.6 %collective-permute-done.6.rest_1_ = bf16[192,768]{1,0:T(8,128)(2,1)S(1)} collective-permute-done((bf16[192,768]{1,0:T(8,128)(2,1)S(1)}, bf16[192,768]{1,0:T(8,128)(2,1)S(1)}, u32[]{:S(2)}, u32[]{:S(2)}) %collective-permute-start.6) | collective-permute-done | bytes 294944 | tf_op jit(solution)/shard_map/ppermute | solution.py:567
  50.9 5.2 %shard_map.83 = bf16[360,2,1024]{2,1,0:T(2,128)(2,1)} custom-call(s32[3]{0:T(128)S(1)} %pad_add_fusion.ids, f32[2,2,184,128]{3,2,1,0:T(8,128)S(1)} %get-tuple-element.38.courant, f32[2,1024]{1,0:T(2,128)S(1)} %copy-done.2, s32[2,1024]{1,0:T(2,128)S(1)} %copy-done.1, f32[2,184,512]{2,1,0:T(8,128)S(1)} %get-tuple-element.56.rest_9_.full0, ...), custom_call_target="tpu_custom_call" | custom-call | flops 4400000000 | tf_op jit(solution)/shard_map/pallas_call | solution.py:177
  (17 shorter events, 0.0 us)
Async XLA Ops:
  0.1 0.7 %copy-start = (s32[2,1024]{1,0:T(2,128)S(1)}, s32[2,1024]{1,0:T(2,128)}, u32[]{:S(2)}) copy-start(s32[2,1024]{1,0:T(2,128)} %mask.11) | copy-start | bytes 24580
  0.8 1.4 %copy-start.3 = (bf16[360,2,1024]{2,1,0:T(2,128)(2,1)S(1)}, bf16[360,2,1024]{2,1,0:T(2,128)(2,1)}, u32[]{:S(2)}) copy-start(bf16[360,2,1024]{2,1,0:T(2,128)(2,1)} %energy.1) | copy-start | bytes 4423684
  2.1 5.0 %copy-start.1 = (s32[2,1024]{1,0:T(2,128)S(1)}, s32[2,1024]{1,0:T(2,128)}, u32[]{:S(2)}) copy-start(s32[2,1024]{1,0:T(2,128)} %mask.11) | copy-start | bytes 24580
  4.4 4.8 %collective-permute-start = (bf16[2,184,1024]{2,1,0:T(8,128)(2,1)S(1)}, bf16[2,184,1024]{2,1,0:T(8,128)(2,1)S(1)}, u32[]{:S(2)}, u32[]{:S(2)}) collective-permute-start(bf16[2,184,1024]{2,1,0:T(8,128)(2,1)S(1)} %get-tuple-element.45.field), channel_id=1, source_target_pairs={{0,2},{2,0},{4,6},{6,4},{8,10},{10,8},{12,14},{14,12},{16,18},{18,... | collective-permute-start | bytes 2261000 | tf_op jit(solution)/shard_map/ppermute | solution.py:512
  4.5 4.7 %copy-start.2 = (f32[2,1024]{1,0:T(2,128)S(1)}, f32[2,1024]{1,0:T(2,128)}, u32[]{:S(2)}) copy-start(f32[2,1024]{1,0:T(2,128)} %depth.7) | copy-start | bytes 24580
  4.5 20.3 %collective-permute-start.2 = (bf16[2,184,1024]{2,1,0:T(8,128)(2,1)S(1)}, bf16[2,184,1024]{2,1,0:T(8,128)(2,1)S(1)}, u32[]{:S(2)}, u32[]{:S(2)}) collective-permute-start(bf16[2,184,1024]{2,1,0:T(8,128)(2,1)S(1)} %get-tuple-element.44.field), channel_id=1, source_target_pairs={{0,30},{2,4},{4,2},{6,8},{8,6},{10,12},{12,10},{14,16},{16,14},{18... | collective-permute-start | bytes 2261000 | tf_op jit(solution)/shard_map/ppermute | solution.py:513
  9.2 4.6 %copy-start.7 = (f32[720]{0:T(1024)S(1)}, f32[720]{0:T(1024)}, u32[]{:S(2)}) copy-start(f32[720]{0:T(1024)} %param.13) | copy-start | bytes 8644
  9.2 4.6 %copy-start.4 = (bf16[720,720]{1,0:T(8,128)(2,1)S(1)}, bf16[720,720]{1,0:T(8,128)(2,1)}, u32[]{:S(2)}) copy-start(bf16[720,720]{1,0:T(8,128)(2,1)} %first.1) | copy-start | bytes 3110404
  9.2 4.6 %copy-start.5 = (bf16[720,720]{1,0:T(8,128)(2,1)S(1)}, bf16[720,720]{1,0:T(8,128)(2,1)}, u32[]{:S(2)}) copy-start(bf16[720,720]{1,0:T(8,128)(2,1)} %second.1) | copy-start | bytes 3110404
  9.2 4.6 %copy-start.6 = (bf16[720,720]{1,0:T(8,128)(2,1)S(1)}, bf16[720,720]{1,0:T(8,128)(2,1)}, u32[]{:S(2)}) copy-start(bf16[720,720]{1,0:T(8,128)(2,1)} %transfer.1) | copy-start | bytes 3110404
  12.5 17.8 %collective-permute-start.1 = (bf16[184,1536]{1,0:T(8,128)(2,1)S(1)}, bf16[184,1536]{1,0:T(8,128)(2,1)S(1)}, u32[]{:S(2)}, u32[]{:S(2)}) collective-permute-start(bf16[184,1536]{1,0:T(8,128)(2,1)S(1)} %get-tuple-element.47.own0.rest_2_), channel_id=1, source_target_pairs={{0,1},{1,0},{2,3},{3,2},{4,5},{5,4},{6,7},{7,6},{8,9},{9,8},{10,11... | collective-permute-start | bytes 1695752 | tf_op jit(solution)/shard_map/ppermute | solution.py:529
  28.3 7.9 %collective-permute-start.3 = (bf16[184,768]{1,0:T(8,128)(2,1)S(1)}, bf16[184,768]{1,0:T(8,128)(2,1)S(1)}, u32[]{:S(2)}, u32[]{:S(2)}) collective-permute-start(bf16[184,768]{1,0:T(8,128)(2,1)S(1)} %get-tuple-element.48.own1_0.rest_3_), channel_id=1, source_target_pairs={{0,1},{1,0},{2,3},{3,2},{4,5},{5,4},{6,7},{7,6},{8,9},{9,8},{10,11... | collective-permute-start | bytes 847880 | tf_op jit(solution)/shard_map/ppermute | solution.py:540
  30.2 10.4 %collective-permute-start.4 = (bf16[184,768]{1,0:T(8,128)(2,1)S(1)}, bf16[184,768]{1,0:T(8,128)(2,1)S(1)}, u32[]{:S(2)}, u32[]{:S(2)}) collective-permute-start(bf16[184,768]{1,0:T(8,128)(2,1)S(1)} %get-tuple-element.49.own1_1.rest_3_), channel_id=1, source_target_pairs={{0,1},{1,0},{2,3},{3,2},{4,5},{5,4},{6,7},{7,6},{8,9},{9,8},{10,11... | collective-permute-start | bytes 847880 | tf_op jit(solution)/shard_map/ppermute | solution.py:540
  39.4 11.5 %collective-permute-start.5 = (bf16[208,768]{1,0:T(8,128)(2,1)S(1)}, bf16[208,768]{1,0:T(8,128)(2,1)S(1)}, u32[]{:S(2)}, u32[]{:S(2)}) collective-permute-start(bf16[208,768]{1,0:T(8,128)(2,1)S(1)} %get-tuple-element.60), channel_id=1, source_target_pairs={{0,30},{2,4},{4,2},{6,8},{8,6},{10,12},{12,10},{14,16},{16,14},{18... | collective-permute-start | bytes 958472 | tf_op jit(solution)/shard_map/ppermute | solution.py:567
  43.8 7.1 %collective-permute-start.6 = (bf16[192,768]{1,0:T(8,128)(2,1)S(1)}, bf16[192,768]{1,0:T(8,128)(2,1)S(1)}, u32[]{:S(2)}, u32[]{:S(2)}) collective-permute-start(bf16[192,768]{1,0:T(8,128)(2,1)S(1)} %get-tuple-element.61), channel_id=1, source_target_pairs={{2,4},{3,5},{4,2},{5,3},{6,8},{7,9},{8,6},{9,7},{10,12},{11,13},{1... | collective-permute-start | bytes 884744 | tf_op jit(solution)/shard_map/ppermute | solution.py:567
  44.4 2.6 %collective-permute-start.7 = (bf16[184,768]{1,0:T(8,128)(2,1)S(1)}, bf16[184,768]{1,0:T(8,128)(2,1)S(1)}, u32[]{:S(2)}, u32[]{:S(2)}) collective-permute-start(bf16[184,768]{1,0:T(8,128)(2,1)S(1)} %get-tuple-element.66), channel_id=1, source_target_pairs={{0,2},{2,0},{4,6},{6,4},{8,10},{10,8},{12,14},{14,12},{16,18},{18,... | collective-permute-start | bytes 847880 | tf_op jit(solution)/shard_map/ppermute | solution.py:568
  44.4 2.6 %collective-permute-start.8 = (bf16[184,640]{1,0:T(8,128)(2,1)S(1)}, bf16[184,640]{1,0:T(8,128)(2,1)S(1)}, u32[]{:S(2)}, u32[]{:S(2)}) collective-permute-start(bf16[184,640]{1,0:T(8,128)(2,1)S(1)} %get-tuple-element.67), channel_id=1, source_target_pairs={{0,2},{2,0},{4,6},{6,4},{8,10},{10,8},{12,14},{14,12},{16,18},{18,... | collective-permute-start | bytes 706568 | tf_op jit(solution)/shard_map/ppermute | solution.py:568
  44.9 2.1 %collective-permute-start.9 = (bf16[184,640]{1,0:T(8,128)(2,1)S(1)}, bf16[184,640]{1,0:T(8,128)(2,1)S(1)}, u32[]{:S(2)}, u32[]{:S(2)}) collective-permute-start(bf16[184,640]{1,0:T(8,128)(2,1)S(1)} %get-tuple-element.68), channel_id=1, source_target_pairs={{0,2},{2,0},{4,6},{6,4},{8,10},{10,8},{12,14},{14,12},{16,18},{18,... | collective-permute-start | bytes 706568 | tf_op jit(solution)/shard_map/ppermute | solution.py:568

commit v6 on v5

--- a/solution.py
+++ b/solution.py
@@ -202,7 +202,7 @@
         for r in range(2):
             begin = (2 * group + r) * pitch
             regroup[begin : begin + pitch] = one_hot(spread(2 * comp + actual_row(r, south), width) == column)
-    ocean = mask[...].astype(F32)
+    ocean = mask[...]
     flat = energy[...].reshape(width, plan.columns)
     moved = jnp.dot(regroup[...], flat, preferred_element_type=F32)
     for group, field in enumerate((field0, field1)):
@@ -224,19 +224,15 @@
 
 
 def lon_sweep(u, a, shift, size):
-    def back(x):
-        return pltpu.roll(x, shift % size, 1)
-
-    d = back(u) - u
-    e = back(d) - d
-    return u + a * (d + (0.5 * a - 0.5) * e)
+    p, q = pltpu.roll(u, shift % size, 1), pltpu.roll(u, 2 * shift % size, 1)
+    return sweep(u, p, q, a)
 
 
 def half_steps(plan, group, ids, courant, depth, mask, depth8, ocean8, load, store):
     size = plan.columns
     for r, row in enumerate(in_order(ids, depth[...], group)):
         depth8[r] = jnp.broadcast_to(row, (8, size))
-    for r, row in enumerate(in_order(ids, mask[...].astype(F32), group)):
+    for r, row in enumerate(in_order(ids, mask[...], group)):
         ocean8[r] = jnp.broadcast_to(row, (8, size))
 
     def block(start, rows, side):
@@ -264,14 +260,14 @@
     west = -(-plan.half // 16)
     full = plan.rows // 16
 
-    @pl.loop(0, east, unroll=2)
+    @pl.loop(0, east, unroll=5)
     def _(i):
         block(pl.multiple_of(i * 16, 16), 16, 1)
 
     for i in range(east, west):
         block(i * 16, 16, 0)
 
-    @pl.loop(west, full, unroll=2)
+    @pl.loop(west, full, unroll=5)
     def _(i):
         block(pl.multiple_of(i * 16, 16), 16, -1)
 
@@ -290,18 +286,20 @@
         at = plan.slots % 8
         rows = [mask[r, tail].astype(F32)[at : at + 1] for r in range(2)]
     else:
-        rows = in_order(ids, mask[...].astype(F32), 0)
+        rows = in_order(ids, mask[...], 0)
     parts = [row[:, b * side : (b + 1) * side] for b in range(2) for row in rows]
     stacked = jnp.concatenate(parts + [jnp.zeros((12, side), F32)], axis=0).astype(BF16)
     at = [lax.broadcasted_iota(jnp.int32, (side, side), axis) for axis in range(2)]
     ahead = jnp.dot(stacked, one_hot(at[0] < at[1]), preferred_element_type=F32)
-    target = lax.broadcasted_iota(jnp.int32, (plan.cap, side), 0)
+    target = lax.broadcasted_iota(jnp.int32, (16, side), 0)
     for b in range(2):
         begin = jnp.zeros((1, 1), F32)
         for r in range(2):
             part = parts[2 * b + r]
             place = jnp.where(part > 0, ahead[2 * b + r : 2 * b + r + 1] + begin, -1.0).astype(jnp.int32)
-            placed[b][:, r * side : (r + 1) * side] = one_hot(target == place)
+            beyond = jnp.broadcast_to(place, target.shape) - target
+            for t in range(0, plan.cap, 16):
+                placed[b][t : t + 16, r * side : (r + 1) * side] = one_hot(beyond == t)
             begin = begin + jnp.sum(part, axis=1, keepdims=True)
 
 
@@ -391,15 +389,18 @@
     chosen = []
     for group in range(2):
         south = southward(ids, group)
+        comp = plan.slot_comp(lax.broadcasted_iota(jnp.int32, (pitch, 128), 0), south) + local * comp_index
+        chosen.append(spread(comp, total) == lax.broadcasted_iota(jnp.int32, (pitch, total), 1))
+    for owner in (comp_index, 1 - comp_index):
         lane = lax.broadcasted_iota(jnp.int32, (8, 2 * pitch), 1)
-        other = jnp.where(lane >= pitch, 1, 0)
-        owner = jnp.where(other == 0, comp_index, 1 - comp_index)
-        source = plan.slot_comp(lane - pitch * other, south) + local * owner
+        group = jnp.where(lane >= pitch, 1, 0)
+        source = plan.slot_comp(lane - pitch * group, ids[0] == group) + local * owner
         source = jnp.concatenate([source] * (total // 8), axis=0)
         hot = one_hot(source == lax.broadcasted_iota(jnp.int32, (total, 2 * pitch), 0))
-        columns[:, 2 * group * pitch : 2 * (group + 1) * pitch] = hot
-        comp = plan.slot_comp(lax.broadcasted_iota(jnp.int32, (pitch, 128), 0), south) + local * comp_index
-        chosen.append(spread(comp, total) == lax.broadcasted_iota(jnp.int32, (pitch, total), 1))
+        if owner is comp_index:
+            columns[:, : 2 * pitch] = hot
+        else:
+            columns[:, 2 * pitch :] = hot
     first_out[:total] = jnp.dot(first[...], columns[...], preferred_element_type=F32).astype(BF16)
     extra = plan.out_rows - total
     place = lax.broadcasted_iota(jnp.int32, (extra, 4 * pitch), 1)
@@ -430,25 +431,37 @@
             cells[i * pitch + whole_rows : (i + 1) * pitch] = tail.astype(BF16)
 
 
-def early_body(plan, ids, first, second, own0, peer0, own1_0, own1_1, *rest):
+def early_body(plan, ids, first, second, own0, own1_0, own1_1, *rest):
     outs, cells = rest[:4], rest[4]
-    known = 3 * plan.pitch
+    pitch = plan.pitch
     for b, own1 in enumerate((own1_0, own1_1)):
-        block = slice(b * plan.cap, (b + 1) * plan.cap)
-        fill_cells(plan, cells, (own0[:, block], peer0[:, block], own1[...]))
+        fill_cells(plan, cells, (own0[:, b * plan.cap : (b + 1) * plan.cap], own1[...]))
         for c in range(0, plan.cap, TILE):
             at = slice(c, c + TILE)
-            outs[2 * b][:, at] = jnp.dot(first[:, :known], cells[:, at], preferred_element_type=F32)
-            outs[2 * b + 1][:, at] = jnp.dot(second[:, :known], cells[:, at], preferred_element_type=F32)
+            for weights, out in ((first, outs[2 * b]), (second, outs[2 * b + 1])):
+                out[:, at] = jnp.dot(weights[:, : 2 * pitch], cells[:, at], preferred_element_type=F32)
+
+
+def middle_body(plan, ids, first, second, peer0, *rest):
+    partial, outs, cells = rest[:4], rest[4:8], rest[8]
+    known = slice(2 * plan.pitch, 3 * plan.pitch)
+    for b in range(2):
+        fill_cells(plan, cells, (peer0[:, b * plan.cap : (b + 1) * plan.cap],))
+        for c in range(0, plan.cap, TILE):
+            at = slice(c, c + TILE)
+            for i, weights in ((2 * b, first), (2 * b + 1, second)):
+                more = jnp.dot(weights[:, known], cells[:, at], preferred_element_type=F32)
+                outs[i][:, at] = partial[i][:, at] + more
 
 
 def source_body(plan, b, ids, first, second, transfer, growth, placed, *rest):
     (early_first, early_second, own0, own1, peer1, half00, half01, half10, half11) = rest[:9]
-    *outs, cells, sources, leaving = rest[9:]
+    *outs, cells, sources = rest[9:]
     full0, sent0, full1 = outs[-6:-3] if b else outs
     total, rows, pitch, cap, side = plan.total, plan.rows, plan.pitch, plan.cap, plan.side
     known = 3 * pitch
     fill_cells(plan, cells, (peer1[...],))
+    spare = [jnp.zeros((sent0.shape[0] - pitch, TILE), F32)] if sent0.shape[0] > pitch else []
     for c in range(0, cap, TILE):
         at = slice(c, c + TILE)
         piece = cells[:, at]
@@ -465,15 +478,15 @@
             rate = spread(growth[begin : begin + pitch], TILE)
             source = SOURCE_STEP * (nonlinear[begin : begin + pitch] + (rate - damping) * spectra)
             sources[begin : begin + pitch, at] = source.astype(BF16)
+            if group == 0:
+                sum_here = spectra + source.astype(BF16).astype(F32)
+                sent0[:, at] = jnp.concatenate([sum_here] + spare, axis=0)[: sent0.shape[0]].astype(BF16)
     block = slice(b * side, (b + 1) * side)
     for slot in range(2):
         here = placed[:, slot * side : (slot + 1) * side]
         spread_out = jnp.dot(sources[...], here, preferred_element_type=F32)
         full0[slot] = (half00, half01)[slot][:, block] + spread_out[:rows]
-        leaving[:, slot * side : (slot + 1) * side] = full0[slot].astype(BF16)
         full1[1 - slot] = (half10, half11)[1 - slot][:, block] + spread_out[pitch : pitch + rows]
-    gathered = gather_cells(leaving[...], placed[...]).astype(F32)
-    sent0[...] = jnp.concatenate([gathered, jnp.zeros((sent0.shape[0] - rows, cap), F32)], axis=0).astype(BF16)
     if b:
         parts = [full[r].astype(BF16) for r in range(2) for full in (outs[0], full1)]
         for piece, (begin, end) in zip(outs[-3:], plan.pieces()):
@@ -500,11 +513,12 @@
         return jax.ShapeDtypeStruct(dims, kind)
 
     rims = [pltpu.VMEM((2, 8, size), F32)] * 2
+    ocean = ocean_mask.astype(F32)
 
     field0, field1, courant = call(
         functools.partial(prep_body, plan),
         ids,
-        (energy, ocean_mask),
+        (energy, ocean),
         [shape(2, rows, size)] * 2 + [shape(2, 2, rows, 128, kind=F32)],
         [pltpu.VMEM((4 * pitch, 2 * plan.local), BF16)],
         cost=2,
@@ -516,11 +530,11 @@
     def place(mask, neighbour, cost):
         return call(functools.partial(place_body, plan, neighbour), ids, (mask,), [shape(cap, size)] * 2, cost=cost)
 
-    placed = place(ocean_mask, False, 2)
+    placed = place(ocean, False, 2)
     outer_placed = place(halo1, True, 0.01)
 
     def first_step(group, field, halo, spectra):
-        operands = (courant, depth_speed, ocean_mask, field, halo, *placed)
+        operands = (courant, depth_speed, ocean, field, halo, *placed)
         outs = [shape(rows, size, kind=F32)] * 2 + spectra
         scratch = rims + [pltpu.VMEM((2, rows, size), BF16)]
         return call(functools.partial(first_body, plan, group), ids, operands, outs, scratch, limit=20, cost=2)
@@ -541,11 +555,20 @@
     early = call(
         functools.partial(early_body, plan),
         ids,
-        (first, second, own0, peer0, own1_0, own1_1),
+        (first, second, own0, own1_0, own1_1),
         [shape(plan.out_rows, cap, kind=F32), shape(total, cap, kind=F32)] * 2,
-        [pltpu.VMEM((3 * pitch, cap), BF16)],
-        limit=30,
-        cost=4,
+        [pltpu.VMEM((2 * pitch, cap), BF16)],
+        limit=20,
+        cost=3,
+    )
+    early = call(
+        functools.partial(middle_body, plan),
+        ids,
+        (first, second, peer0, *early),
+        [shape(plan.out_rows, cap, kind=F32), shape(total, cap, kind=F32)] * 2,
+        [pltpu.VMEM((pitch, cap), BF16)],
+        limit=20,
+        cost=2,
     )
 
     full0, sent0, full1 = [], [], []
@@ -557,7 +580,7 @@
             + (*half0, *half1, *full1),
             [shape(2, rows, side, kind=F32), shape(rows + (24, 8)[b], cap), shape(2, rows, side, kind=F32)]
             + [shape(rows, end - begin) for begin, end in plan.pieces()] * b,
-            [pltpu.VMEM((pitch, cap), BF16), pltpu.VMEM((2 * pitch, cap), BF16), pltpu.VMEM((rows, size), BF16)],
+            [pltpu.VMEM((pitch, cap), BF16), pltpu.VMEM((2 * pitch, cap), BF16)],
             limit=30,
             cost=4,
         )
@@ -572,7 +595,7 @@
     partial, restore = call(
         functools.partial(last_body, plan, 0),
         ids,
-        (courant, depth_speed, ocean_mask, *full0, *rim0),
+        (courant, depth_speed, ocean, *full0, *rim0),
         [shape(width, size, kind=F32), shape(width, 2 * pitch)],
         [done] + rims,
         limit=30,
@@ -581,7 +604,7 @@
     (out,) = call(
         functools.partial(last_body, plan, 1),
         ids,
-        (courant, depth_speed, ocean_mask, *full1, *rim1, *outer_placed, partial, restore),
+        (courant, depth_speed, ocean, *full1, *rim1, *outer_placed, partial, restore),
         [shape(*energy.shape)],
         [pltpu.VMEM((rows, size), BF16)] * 2 + [done] + rims,
         limit=30,

time: 56.7 us -> 54.1 us (0.954)
  Pallas kernels: 35 us -> 30.7 us
  waiting for transfers between devices: 10.3 us -> 12.2 us
  other arithmetic: 0.08 us -> 0.78 us
  local copies, waits for them, and re-layouts: 2.11 us -> 1.42 us
    pallas_call x11 -> x12, Pallas kernels: 35 us -> 30.7 us  [call(): pl.pallas_call(body, in_specs=[SMEM] + [VMEM] * len(operands), out_specs=...]
    ppermute x1, waiting for transfers between devices: 7.88 us -> 9.47 us  [paired_shards(): halo1 = lax.ppermute(field0, 'band', outer)]
    ppermute x1, waiting for transfers between devices: 0.65 us -> 2.12 us  [paired_shards(): lax.ppermute(sent0[1], ('band', 'comp'), outer_beside)]
    ppermute x2, waiting for transfers between devices: 1.8 us -> 0.33 us  [paired_shards(): peer1 = [lax.ppermute(own, 'comp', peers) for own in own1]]
    convert_element_type x0 -> x1, other arithmetic: none -> 0.7 us  [paired_shards(): ocean = ocean_mask.astype(F32)]
    unnamed x16, local copies, waits for them, and re-layouts: 2.1 us -> 1.41 us
    ppermute x1, starting transfers between devices: 1.24 us -> 1.9 us  [paired_shards(): lax.ppermute(sent0[0], 'band', outer)]
  transfers between devices with their start and end apart: 10 -> 10, of which waited for: 3 -> 4; matrix products, arithmetic and copies ran while one was open for 0% -> 0% of each run, Pallas kernels for 49% -> 45%
where the time goes in v6:
time: 54.1 us; the launch traced here: 53.9 us
  Pallas kernels  30.7 us (57%)
  waiting for transfers between devices  12.2 us (23%)
  starting transfers between devices  8.62 us (16%)
  local copies, waits for them, and re-layouts  1.42 us (3%)
  other arithmetic  0.78 us (1%)
    pallas_call x12, Pallas kernels, call(): pl.pallas_call(body, in_specs=[SMEM] + [VMEM] * len(operands), out_specs=...  30.7 us
    ppermute x1, waiting for transfers between devices, paired_shards(): halo1 = lax.ppermute(field0, 'band', outer)  9.47 us
    ppermute x1, starting transfers between devices, paired_shards(): halo1 = lax.ppermute(field0, 'band', outer)  2.62 us
    ppermute x1, waiting for transfers between devices, paired_shards(): lax.ppermute(sent0[1], ('band', 'comp'), outer_beside)  2.12 us
    ppermute x2, starting transfers between devices, paired_shards(): peer1 = [lax.ppermute(own, 'comp', peers) for own in own1]  1.95 us
    ppermute x1, starting transfers between devices, paired_shards(): lax.ppermute(sent0[0], 'band', outer)  1.9 us
    unnamed x16, local copies, waits for them, and re-layouts  1.41 us
    ppermute x1, starting transfers between devices, paired_shards(): peer0 = lax.ppermute(own0, 'comp', peers)  1.31 us
  transfers between devices with their start and end apart: 10, of which 4 were waited for; matrix products, arithmetic and copies ran while one was open for 0% of the time, Pallas kernels for 45%

profile of v6, /device:TPU:1, one launch (start us, length us, event | category | flops | bytes accessed | tf_op | source)
XLA Modules:
  0.0 53.9 jit_solution(166844525538663693)
XLA Ops:
  0.0 0.7 %convert_element_type.4.mask = f32[2,1024]{1,0:T(2,128)S(1)} convert(s32[2,1024]{1,0:T(2,128)} %param.9) | non-fusion elementwise | flops 2048 | bytes 16384 | tf_op jit(solution)/shard_map/convert_element_type | solution.py:516
  0.7 0.1 pad_add_fusion.ids
  0.8 1.4 %copy-done.1 = bf16[360,2,1024]{2,1,0:T(2,128)(2,1)S(1)} copy-done((bf16[360,2,1024]{2,1,0:T(2,128)(2,1)S(1)}, bf16[360,2,1024]{2,1,0:T(2,128)(2,1)}, u32[]{:S(2)}) %copy-start.1) | copy-done | bytes 1474584
  2.2 2.2 %shard_map.73 = (bf16[2,184,1024]{2,1,0:T(8,128)(2,1)S(1)}, bf16[2,184,1024]{2,1,0:T(8,128)(2,1)S(1)}, f32[2,2,184,128]{3,2,1,0:T(8,128)S(1)}) custom-call(s32[3]{0:T(128)S(1)} %pad_add_fusion.ids, bf16[360,2,1024]{2,1,0:T(2,128)(2,1)S(1)} %copy-done.1, f32[2,1024]{1,0:T(2,128)S(1)} %convert_element_type.4.mask), custom_call_target="tpu_custom_call" | custom-call | flops 2200000000 | tf_op jit(solution)/shard_map/pallas_call | solution.py:177
  4.4 0.1 collective-permute-start
  4.5 2.6 %collective-permute-start.2 = (bf16[2,184,1024]{2,1,0:T(8,128)(2,1)S(1)}, bf16[2,184,1024]{2,1,0:T(8,128)(2,1)S(1)}, u32[]{:S(2)}, u32[]{:S(2)}) collective-permute-start(bf16[2,184,1024]{2,1,0:T(8,128)(2,1)S(1)} %get-tuple-element.48.field), channel_id=1, source_target_pairs={{0,30},{2,4},{4,2},{6,8},{8,6},{10,12},{12,10},{14,16},{16,14},{18... | collective-permute-start | bytes 2261000 | tf_op jit(solution)/shard_map/ppermute | solution.py:527
  7.1 1.3 %shard_map.75 = (bf16[768,1024]{1,0:T(8,128)(2,1)S(1)}, bf16[768,1024]{1,0:T(8,128)(2,1)S(1)}) custom-call(s32[3]{0:T(128)S(1)} %pad_add_fusion.ids, f32[2,1024]{1,0:T(2,128)S(1)} %convert_element_type.4.mask), custom_call_target="tpu_custom_call" | custom-call | flops 2200000000 | tf_op jit(solution)/shard_map/pallas_call | solution.py:177
  8.4 0.0 copy-start.2
  8.4 0.0 copy-start.3
  8.5 2.5 %shard_map.76 = (f32[184,1024]{1,0:T(8,128)S(1)}, f32[184,1024]{1,0:T(8,128)S(1)}, bf16[184,1536]{1,0:T(8,128)(2,1)S(1)}) custom-call(s32[3]{0:T(128)S(1)} %pad_add_fusion.ids, f32[2,2,184,128]{3,2,1,0:T(8,128)S(1)} %get-tuple-element.42.courant, f32[2,1024]{1,0:T(2,128)S(1)} %copy-done, f32[2,1024]{1,0:T(2,128)S(1)} %convert_element_type.4.mask, ...), custom_call_target="tpu_custom_call" | custom-call | flops 2200000000 | tf_op jit(solution)/shard_map/pallas_call | solution.py:177
  10.9 1.3 %collective-permute-start.1 = (bf16[184,1536]{1,0:T(8,128)(2,1)S(1)}, bf16[184,1536]{1,0:T(8,128)(2,1)S(1)}, u32[]{:S(2)}, u32[]{:S(2)}) collective-permute-start(bf16[184,1536]{1,0:T(8,128)(2,1)S(1)} %get-tuple-element.51.own0.rest_2_), channel_id=1, source_target_pairs={{0,1},{1,0},{2,3},{3,2},{4,5},{5,4},{6,7},{7,6},{8,9},{9,8},{10,11... | collective-permute-start | bytes 1695752 | tf_op jit(solution)/shard_map/ppermute | solution.py:543
  12.3 3.1 %shard_map.74 = (bf16[736,768]{1,0:T(8,128)(2,1)S(1)}, bf16[720,768]{1,0:T(8,128)(2,1)S(1)}, bf16[384,720]{1,0:T(8,128)(2,1)S(1)}, f32[384,128]{1,0:T(8,128)S(1)}) custom-call(s32[3]{0:T(128)S(1)} %pad_add_fusion.ids, bf16[720,720]{1,0:T(8,128)(2,1)S(1)} %copy-done.2, bf16[720,720]{1,0:T(8,128)(2,1)S(1)} %copy-done.3, bf16[720,720]{1,0:T(8,128)(2,1)S(1)} %copy-done.4, ...), custom_call_target="tpu_custom_call" | custom-call | flops 3300000000 | tf_op jit(solution)/shard_map/pallas_call | solution.py:177
  15.3 9.5 %collective-permute-done.2.halo.mask = bf16[2,184,1024]{2,1,0:T(8,128)(2,1)S(1)} collective-permute-done((bf16[2,184,1024]{2,1,0:T(8,128)(2,1)S(1)}, bf16[2,184,1024]{2,1,0:T(8,128)(2,1)S(1)}, u32[]{:S(2)}, u32[]{:S(2)}) %collective-permute-start.2) | collective-permute-done | bytes 753696 | tf_op jit(solution)/shard_map/ppermute | solution.py:527
  24.8 2.5 %shard_map.77 = (f32[184,1024]{1,0:T(8,128)S(1)}, f32[184,1024]{1,0:T(8,128)S(1)}, bf16[184,768]{1,0:T(8,128)(2,1)S(1)}, bf16[184,768]{1,0:T(8,128)(2,1)S(1)}) custom-call(s32[3]{0:T(128)S(1)} %pad_add_fusion.ids, f32[2,2,184,128]{3,2,1,0:T(8,128)S(1)} %get-tuple-element.42.courant, f32[2,1024]{1,0:T(2,128)S(1)} %copy-done, ...), custom_call_target="tpu_custom_call" | custom-call | flops 2200000000 | tf_op jit(solution)/shard_map/pallas_call | solution.py:177
  27.3 1.9 %collective-permute-start.3 = (bf16[184,768]{1,0:T(8,128)(2,1)S(1)}, bf16[184,768]{1,0:T(8,128)(2,1)S(1)}, u32[]{:S(2)}, u32[]{:S(2)}) collective-permute-start(bf16[184,768]{1,0:T(8,128)(2,1)S(1)} %get-tuple-element.52.own1_0.rest_3_), channel_id=1, source_target_pairs={{0,1},{1,0},{2,3},{3,2},{4,5},{5,4},{6,7},{7,6},{8,9},{9,8},{10,11... | collective-permute-start | bytes 847880 | tf_op jit(solution)/shard_map/ppermute | solution.py:554
  29.2 0.1 collective-permute-start.4
  29.3 3.0 %shard_map.78 = (f32[736,768]{1,0:T(8,128)S(1)}, f32[720,768]{1,0:T(8,128)S(1)}, f32[736,768]{1,0:T(8,128)S(1)}, f32[720,768]{1,0:T(8,128)S(1)}) custom-call(s32[3]{0:T(128)S(1)} %pad_add_fusion.ids, bf16[736,768]{1,0:T(8,128)(2,1)S(1)} %get-tuple-element.43.first, bf16[720,768]{1,0:T(8,128)(2,1)S(1)} %get-tuple-element.44.second, ...), custom_call_target="tpu_custom_call" | custom-call | flops 3300000000 | tf_op jit(solution)/shard_map/pallas_call | solution.py:177
  32.3 0.0 copy-start.6
  32.3 2.0 %shard_map.79 = (f32[736,768]{1,0:T(8,128)S(1)}, f32[720,768]{1,0:T(8,128)S(1)}, f32[736,768]{1,0:T(8,128)S(1)}, f32[720,768]{1,0:T(8,128)S(1)}) custom-call(s32[3]{0:T(128)S(1)} %pad_add_fusion.ids, bf16[736,768]{1,0:T(8,128)(2,1)S(1)} %get-tuple-element.43.first, bf16[720,768]{1,0:T(8,128)(2,1)S(1)} %get-tuple-element.44.second, ...), custom_call_target="tpu_custom_call" | custom-call | flops 2200000000 | tf_op jit(solution)/shard_map/pallas_call | solution.py:177
  34.3 0.3 collective-permute-done.3.rest_4_
  34.6 3.2 %shard_map.80 = (f32[2,184,512]{2,1,0:T(8,128)S(1)}, bf16[208,768]{1,0:T(8,128)(2,1)S(1)}, f32[2,184,512]{2,1,0:T(8,128)S(1)}) custom-call(s32[3]{0:T(128)S(1)} %pad_add_fusion.ids, bf16[736,768]{1,0:T(8,128)(2,1)S(1)} %get-tuple-element.43.first, bf16[720,768]{1,0:T(8,128)(2,1)S(1)} %get-tuple-element.44.second, bf16[384,720]{1,0:T(8,128)(2,1)S(1)} %copy-done.6, ...), custom_call_target="tpu_custom_call" | custom-call | flops 4400000000 | tf_op jit(solution)/shard_map/pallas_call | solution.py:177
  37.8 1.9 %collective-permute-start.5 = (bf16[208,768]{1,0:T(8,128)(2,1)S(1)}, bf16[208,768]{1,0:T(8,128)(2,1)S(1)}, u32[]{:S(2)}, u32[]{:S(2)}) collective-permute-start(bf16[208,768]{1,0:T(8,128)(2,1)S(1)} %get-tuple-element.68), channel_id=1, source_target_pairs={{0,30},{2,4},{4,2},{6,8},{8,6},{10,12},{12,10},{14,16},{16,14},{18... | collective-permute-start | bytes 958472 | tf_op jit(solution)/shard_map/ppermute | solution.py:590
  39.7 3.0 %shard_map.81 = (f32[2,184,512]{2,1,0:T(8,128)S(1)}, bf16[192,768]{1,0:T(8,128)(2,1)S(1)}, f32[2,184,512]{2,1,0:T(8,128)S(1)}, bf16[184,768]{1,0:T(8,128)(2,1)S(...) custom-call(s32[3]{0:T(128)S(1)} %pad_add_fusion.ids, bf16[736,768]{1,0:T(8,128)(2,1)S(1)} %get-tuple-element.43.first, ...), custom_call_target="tpu_custom_call" | custom-call | flops 4400000000 | tf_op jit(solution)/shard_map/pallas_call | solution.py:177
  42.8 0.1 collective-permute-start.6
  42.8 0.1 collective-permute-start.7
  42.9 0.5 collective-permute-start.8
  43.4 0.1 collective-permute-start.9
  43.5 1.3 %shard_map.82 = (bf16[768,1024]{1,0:T(8,128)(2,1)S(1)}, bf16[768,1024]{1,0:T(8,128)(2,1)S(1)}) custom-call(s32[3]{0:T(128)S(1)} %pad_add_fusion.ids, bf16[2,184,1024]{2,1,0:T(8,128)(2,1)S(1)} %collective-permute-done.2.halo.mask), custom_call_target="tpu_custom_call" | custom-call | flops 11000000 | tf_op jit(solution)/shard_map/pallas_call | solution.py:177
  44.8 0.3 collective-permute-done.9.rest_2_
  45.1 2.4 %shard_map.83 = (f32[720,1024]{1,0:T(8,128)S(1)}, bf16[720,384]{1,0:T(8,128)(2,1)S(1)}) custom-call(s32[3]{0:T(128)S(1)} %pad_add_fusion.ids, f32[2,2,184,128]{3,2,1,0:T(8,128)S(1)} %get-tuple-element.42.courant, f32[2,1024]{1,0:T(2,128)S(1)} %copy-done, f32[2,1024]{1,0:T(2,128)S(1)} %convert_element_type.4.mask, ...), custom_call_target="tpu_custom_call" | custom-call | flops 11000000 | tf_op jit(solution)/shard_map/pallas_call | solution.py:177
  47.6 2.1 %collective-permute-done.6.rest_1_ = bf16[192,768]{1,0:T(8,128)(2,1)S(1)} collective-permute-done((bf16[192,768]{1,0:T(8,128)(2,1)S(1)}, bf16[192,768]{1,0:T(8,128)(2,1)S(1)}, u32[]{:S(2)}, u32[]{:S(2)}) %collective-permute-start.6) | collective-permute-done | bytes 294944 | tf_op jit(solution)/shard_map/ppermute | solution.py:590
  49.7 4.2 %shard_map.84 = bf16[360,2,1024]{2,1,0:T(2,128)(2,1)} custom-call(s32[3]{0:T(128)S(1)} %pad_add_fusion.ids, f32[2,2,184,128]{3,2,1,0:T(8,128)S(1)} %get-tuple-element.42.courant, f32[2,1024]{1,0:T(2,128)S(1)} %copy-done, f32[2,1024]{1,0:T(2,128)S(1)} %convert_element_type.4.mask, f32[2,184,512]{2,1,0:T(8,128)S(1)} %get-tuple-element.64.rest_9_.full0, ...), custom_call_target="tpu_custom_call" | custom-call | flops 4400000000 | tf_op jit(solution)/shard_map/pallas_call | solution.py:177
  (19 shorter events, 0.0 us)
Async XLA Ops:
  0.8 1.4 %copy-start.1 = (bf16[360,2,1024]{2,1,0:T(2,128)(2,1)S(1)}, bf16[360,2,1024]{2,1,0:T(2,128)(2,1)}, u32[]{:S(2)}) copy-start(bf16[360,2,1024]{2,1,0:T(2,128)(2,1)} %energy.1) | copy-start | bytes 4423684
  2.2 5.0 %copy-start.7 = (f32[720]{0:T(1024)S(1)}, f32[720]{0:T(1024)}, u32[]{:S(2)}) copy-start(f32[720]{0:T(1024)} %param.13) | copy-start | bytes 8644
  4.4 4.0 %collective-permute-start = (bf16[2,184,1024]{2,1,0:T(8,128)(2,1)S(1)}, bf16[2,184,1024]{2,1,0:T(8,128)(2,1)S(1)}, u32[]{:S(2)}, u32[]{:S(2)}) collective-permute-start(bf16[2,184,1024]{2,1,0:T(8,128)(2,1)S(1)} %get-tuple-element.49.field), channel_id=1, source_target_pairs={{0,2},{2,0},{4,6},{6,4},{8,10},{10,8},{12,14},{14,12},{16,18},{18,... | collective-permute-start | bytes 2261000 | tf_op jit(solution)/shard_map/ppermute | solution.py:526
  4.5 20.3 %collective-permute-start.2 = (bf16[2,184,1024]{2,1,0:T(8,128)(2,1)S(1)}, bf16[2,184,1024]{2,1,0:T(8,128)(2,1)S(1)}, u32[]{:S(2)}, u32[]{:S(2)}) collective-permute-start(bf16[2,184,1024]{2,1,0:T(8,128)(2,1)S(1)} %get-tuple-element.48.field), channel_id=1, source_target_pairs={{0,30},{2,4},{4,2},{6,8},{8,6},{10,12},{12,10},{14,16},{16,14},{18... | collective-permute-start | bytes 2261000 | tf_op jit(solution)/shard_map/ppermute | solution.py:527
  7.1 1.3 %copy-start = (f32[2,1024]{1,0:T(2,128)S(1)}, f32[2,1024]{1,0:T(2,128)}, u32[]{:S(2)}) copy-start(f32[2,1024]{1,0:T(2,128)} %depth.7) | copy-start | bytes 24580
  8.4 3.8 %copy-start.2 = (bf16[720,720]{1,0:T(8,128)(2,1)S(1)}, bf16[720,720]{1,0:T(8,128)(2,1)}, u32[]{:S(2)}) copy-start(bf16[720,720]{1,0:T(8,128)(2,1)} %first.1) | copy-start | bytes 3110404
  8.4 3.8 %copy-start.3 = (bf16[720,720]{1,0:T(8,128)(2,1)S(1)}, bf16[720,720]{1,0:T(8,128)(2,1)}, u32[]{:S(2)}) copy-start(bf16[720,720]{1,0:T(8,128)(2,1)} %second.1) | copy-start | bytes 3110404
  8.4 3.8 %copy-start.4 = (bf16[720,720]{1,0:T(8,128)(2,1)S(1)}, bf16[720,720]{1,0:T(8,128)(2,1)}, u32[]{:S(2)}) copy-start(bf16[720,720]{1,0:T(8,128)(2,1)} %transfer.1) | copy-start | bytes 3110404
  10.9 21.4 %collective-permute-start.1 = (bf16[184,1536]{1,0:T(8,128)(2,1)S(1)}, bf16[184,1536]{1,0:T(8,128)(2,1)S(1)}, u32[]{:S(2)}, u32[]{:S(2)}) collective-permute-start(bf16[184,1536]{1,0:T(8,128)(2,1)S(1)} %get-tuple-element.51.own0.rest_2_), channel_id=1, source_target_pairs={{0,1},{1,0},{2,3},{3,2},{4,5},{5,4},{6,7},{7,6},{8,9},{9,8},{10,11... | collective-permute-start | bytes 1695752 | tf_op jit(solution)/shard_map/ppermute | solution.py:543
  15.3 12.0 %copy-start.5 = (bf16[384,720]{1,0:T(8,128)(2,1)}, bf16[384,720]{1,0:T(8,128)(2,1)S(1)}, u32[]{:S(2)}) copy-start(bf16[384,720]{1,0:T(8,128)(2,1)S(1)} %get-tuple-element.45.transfer) | copy-start | bytes 1658884
  27.3 7.3 %collective-permute-start.3 = (bf16[184,768]{1,0:T(8,128)(2,1)S(1)}, bf16[184,768]{1,0:T(8,128)(2,1)S(1)}, u32[]{:S(2)}, u32[]{:S(2)}) collective-permute-start(bf16[184,768]{1,0:T(8,128)(2,1)S(1)} %get-tuple-element.52.own1_0.rest_3_), channel_id=1, source_target_pairs={{0,1},{1,0},{2,3},{3,2},{4,5},{5,4},{6,7},{7,6},{8,9},{9,8},{10,11... | collective-permute-start | bytes 847880 | tf_op jit(solution)/shard_map/ppermute | solution.py:554
  29.2 10.5 %collective-permute-start.4 = (bf16[184,768]{1,0:T(8,128)(2,1)S(1)}, bf16[184,768]{1,0:T(8,128)(2,1)S(1)}, u32[]{:S(2)}, u32[]{:S(2)}) collective-permute-start(bf16[184,768]{1,0:T(8,128)(2,1)S(1)} %get-tuple-element.53.own1_1.rest_3_), channel_id=1, source_target_pairs={{0,1},{1,0},{2,3},{3,2},{4,5},{5,4},{6,7},{7,6},{8,9},{9,8},{10,11... | collective-permute-start | bytes 847880 | tf_op jit(solution)/shard_map/ppermute | solution.py:554
  32.3 2.3 %copy-start.6 = (bf16[384,720]{1,0:T(8,128)(2,1)S(1)}, bf16[384,720]{1,0:T(8,128)(2,1)}, u32[]{:S(2)}) copy-start(bf16[384,720]{1,0:T(8,128)(2,1)} %copy-done.5) | copy-start | bytes 1658884
  37.8 11.9 %collective-permute-start.5 = (bf16[208,768]{1,0:T(8,128)(2,1)S(1)}, bf16[208,768]{1,0:T(8,128)(2,1)S(1)}, u32[]{:S(2)}, u32[]{:S(2)}) collective-permute-start(bf16[208,768]{1,0:T(8,128)(2,1)S(1)} %get-tuple-element.68), channel_id=1, source_target_pairs={{0,30},{2,4},{4,2},{6,8},{8,6},{10,12},{12,10},{14,16},{16,14},{18... | collective-permute-start | bytes 958472 | tf_op jit(solution)/shard_map/ppermute | solution.py:590
  42.8 7.0 %collective-permute-start.6 = (bf16[192,768]{1,0:T(8,128)(2,1)S(1)}, bf16[192,768]{1,0:T(8,128)(2,1)S(1)}, u32[]{:S(2)}, u32[]{:S(2)}) collective-permute-start(bf16[192,768]{1,0:T(8,128)(2,1)S(1)} %get-tuple-element.69), channel_id=1, source_target_pairs={{2,4},{3,5},{4,2},{5,3},{6,8},{7,9},{8,6},{9,7},{10,12},{11,13},{1... | collective-permute-start | bytes 884744 | tf_op jit(solution)/shard_map/ppermute | solution.py:590
  42.8 2.3 %collective-permute-start.7 = (bf16[184,768]{1,0:T(8,128)(2,1)S(1)}, bf16[184,768]{1,0:T(8,128)(2,1)S(1)}, u32[]{:S(2)}, u32[]{:S(2)}) collective-permute-start(bf16[184,768]{1,0:T(8,128)(2,1)S(1)} %get-tuple-element.74), channel_id=1, source_target_pairs={{0,2},{2,0},{4,6},{6,4},{8,10},{10,8},{12,14},{14,12},{16,18},{18,... | collective-permute-start | bytes 847880 | tf_op jit(solution)/shard_map/ppermute | solution.py:591
  42.9 1.9 %collective-permute-start.8 = (bf16[184,640]{1,0:T(8,128)(2,1)S(1)}, bf16[184,640]{1,0:T(8,128)(2,1)S(1)}, u32[]{:S(2)}, u32[]{:S(2)}) collective-permute-start(bf16[184,640]{1,0:T(8,128)(2,1)S(1)} %get-tuple-element.75), channel_id=1, source_target_pairs={{0,2},{2,0},{4,6},{6,4},{8,10},{10,8},{12,14},{14,12},{16,18},{18,... | collective-permute-start | bytes 706568 | tf_op jit(solution)/shard_map/ppermute | solution.py:591
  43.4 1.7 %collective-permute-start.9 = (bf16[184,640]{1,0:T(8,128)(2,1)S(1)}, bf16[184,640]{1,0:T(8,128)(2,1)S(1)}, u32[]{:S(2)}, u32[]{:S(2)}) collective-permute-start(bf16[184,640]{1,0:T(8,128)(2,1)S(1)} %get-tuple-element.76), channel_id=1, source_target_pairs={{0,2},{2,0},{4,6},{6,4},{8,10},{10,8},{12,14},{14,12},{16,18},{18,... | collective-permute-start | bytes 706568 | tf_op jit(solution)/shard_map/ppermute | solution.py:591

commit v7 on v6

--- a/solution.py
+++ b/solution.py
@@ -120,10 +120,6 @@
         self.side = columns // 2
         self.cap = 3 * columns // 4
 
-    def pieces(self):
-        ends = [0, self.cap, (self.cap + 2 * self.columns) // 2, 2 * self.columns]
-        return list(zip(ends[:-1], ends[1:]))
-
     def slot_parts(self, slot):
         east = slot < self.half
         j = jnp.where(east, slot, slot - self.half)
@@ -173,7 +169,7 @@
 SMEM = pl.BlockSpec(memory_space=pltpu.SMEM)
 
 
-def call(body, ids, operands, outs, scratch=(), limit=40, cost=1.0):
+def call(body, ids, operands, outs, scratch=(), limit=20, cost=1.0):
     return pl.pallas_call(
         body,
         in_specs=[SMEM] + [VMEM] * len(operands),
@@ -334,24 +330,21 @@
             spectra[b][...] = gathered
 
 
-def last_body(plan, group, ids, courant, depth, mask, full0, full1, *rest):
+def last_body(plan, group, ids, courant, depth, mask, full, *rest):
     *rest, done, depth8, ocean8 = rest
     width, pitch, rows, side = 2 * plan.local, plan.pitch, plan.rows, plan.side
 
     def scatter(cells, placed):
         return jnp.dot(cells[...], placed[...], preferred_element_type=F32)[:rows].astype(BF16)
 
-    def both(a, b, at):
-        return jnp.concatenate([a[at], b[at]], axis=1).astype(F32)
-
     def load(start, count):
         at = pl.ds(start, count)
-        values = [both(full0.at[r], full1.at[r], at) for r in range(2)]
+        values = [full[r, at] for r in range(2)]
         if group == 0:
-            rows_in = jnp.concatenate([piece[at] for piece in pieces], axis=1).astype(F32)
-            return values + [rows_in[:, plan.columns :], rows_in[:, : plan.columns]]
+            return values + [inner_rows[r, at].astype(F32) for r in (1, 0)]
         slots = [slice(slot * side, (slot + 1) * side) for slot in (1, 0)]
-        return values + within(ids, group, [both(rim0.at[:, slot], rim1.at[:, slot], at) for slot in slots])
+        outer = [jnp.concatenate([rim[at, slot] for rim in (rim0, rim1)], axis=1).astype(F32) for slot in slots]
+        return values + within(ids, group, outer)
 
     def store(start, count, new0, new1):
         for r, new in enumerate((new0, new1)):
@@ -361,26 +354,31 @@
             done[pl.ds(pl.multiple_of(at, 16), 16)] = new.astype(BF16)
 
     if group == 0:
-        *pieces, partial, restore = rest
+        *pieces, restore, partial, inner_rows = rest
+        for r in range(2):
+            inner_rows[r, :SPLIT] = pieces[r][...]
+            inner_rows[r, SPLIT:] = pieces[2][r * (pitch - SPLIT) : (r + 1) * (pitch - SPLIT)]
     else:
         cells0, cells1, placed0, placed1, partial, restore, out, rim0, rim1 = rest
         rim0[...] = scatter(cells0, placed0)
         rim1[...] = scatter(cells1, placed1)
     half_steps(plan, group, ids, courant, depth, mask, depth8, ocean8, load, store)
     if group == 0:
-        tables = []
-        for g in range(2):
-            lane = lax.broadcasted_iota(jnp.int32, (8, 2 * pitch), 1)
-            r = jnp.where(lane >= pitch, 1, 0)
-            south = southward(ids, g)
-            target = 2 * plan.slot_comp(lane - pitch * r, south) + actual_row(r, south)
-            target = jnp.concatenate([target] * (width // 8), axis=0)
-            tables.append(one_hot(target == lax.broadcasted_iota(jnp.int32, (width, 2 * pitch), 0)))
-        restore[...] = tables[1]
-        partial[...] = jnp.dot(tables[0], done[...], preferred_element_type=F32)
+        partial[...] = jnp.dot(restore[...], done[...], preferred_element_type=F32)
     else:
         flat = partial[...] + jnp.dot(restore[...], done[...], preferred_element_type=F32)
         out[...] = flat.astype(BF16).reshape(plan.local, 2, plan.columns)
+
+
+def restore_body(plan, ids, growth, *tables):
+    width, pitch = 2 * plan.local, plan.pitch
+    for group in range(2):
+        lane = lax.broadcasted_iota(jnp.int32, (8, 2 * pitch), 1)
+        r = jnp.where(lane >= pitch, 1, 0)
+        south = southward(ids, group)
+        target = 2 * plan.slot_comp(lane - pitch * r, south) + actual_row(r, south)
+        target = jnp.concatenate([target] * (width // 8), axis=0)
+        tables[group][...] = one_hot(target == lax.broadcasted_iota(jnp.int32, (width, 2 * pitch), 0))
 
 
 def weights_body(plan, ids, first, second, transfer, growth, first_out, second_out, transfer_out, growth_out, columns):
@@ -454,15 +452,13 @@
                 outs[i][:, at] = partial[i][:, at] + more
 
 
-def source_body(plan, b, ids, first, second, transfer, growth, placed, *rest):
-    (early_first, early_second, own0, own1, peer1, half00, half01, half10, half11) = rest[:9]
-    *outs, cells, sources = rest[9:]
-    full0, sent0, full1 = outs[-6:-3] if b else outs
-    total, rows, pitch, cap, side = plan.total, plan.rows, plan.pitch, plan.cap, plan.side
+def source_body(plan, b, ids, first, second, transfer, growth, *rest):
+    early_first, early_second, own0, own1, peer1, sources, sent0, cells = rest
+    total, rows, pitch = plan.total, plan.rows, plan.pitch
     known = 3 * pitch
     fill_cells(plan, cells, (peer1[...],))
-    spare = [jnp.zeros((sent0.shape[0] - pitch, TILE), F32)] if sent0.shape[0] > pitch else []
-    for c in range(0, cap, TILE):
+    extra = sent0.shape[0] - rows
+    for c in range(0, plan.cap, TILE):
         at = slice(c, c + TILE)
         piece = cells[:, at]
         forward = early_first[:, at] + jnp.dot(first[:, known:], piece, preferred_element_type=F32)
@@ -473,25 +469,36 @@
         damping = level * level / (1.0 + level * level)
         for group in range(2):
             begin = group * pitch
-            spectra = (own1[:, at] if group else own0[:, b * cap + c : b * cap + c + TILE]).astype(F32)
+            spectra = (own1[:, at] if group else own0[:, b * plan.cap + c : b * plan.cap + c + TILE]).astype(F32)
             spectra = jnp.concatenate([spectra, jnp.zeros((pitch - rows, TILE), F32)], axis=0)
             rate = spread(growth[begin : begin + pitch], TILE)
             source = SOURCE_STEP * (nonlinear[begin : begin + pitch] + (rate - damping) * spectra)
-            sources[begin : begin + pitch, at] = source.astype(BF16)
+            source = source.astype(BF16)
+            sources[begin : begin + pitch, at] = source
             if group == 0:
-                sum_here = spectra + source.astype(BF16).astype(F32)
-                sent0[:, at] = jnp.concatenate([sum_here] + spare, axis=0)[: sent0.shape[0]].astype(BF16)
-    block = slice(b * side, (b + 1) * side)
-    for slot in range(2):
-        here = placed[:, slot * side : (slot + 1) * side]
-        spread_out = jnp.dot(sources[...], here, preferred_element_type=F32)
-        full0[slot] = (half00, half01)[slot][:, block] + spread_out[:rows]
-        full1[1 - slot] = (half10, half11)[1 - slot][:, block] + spread_out[pitch : pitch + rows]
-    if b:
-        parts = [full[r].astype(BF16) for r in range(2) for full in (outs[0], full1)]
-        for piece, (begin, end) in zip(outs[-3:], plan.pieces()):
-            ends = [(max(begin - i * side, 0), min(end - i * side, side)) for i in range(4)]
-            piece[...] = jnp.concatenate([parts[i][:, x:y] for i, (x, y) in enumerate(ends) if x < y], axis=1)
+                sent0[:, at] = (spectra + source.astype(F32))[: rows + extra].astype(BF16)
+
+
+SPLIT = 128
+
+
+def spread_body(plan, ids, sources0, sources1, placed0, placed1, half00, half01, half10, half11, full0, full1, *pieces):
+    rows, pitch, side = plan.rows, plan.pitch, plan.side
+    halves, fulls = ((half00, half01), (half10, half11)), (full0, full1)
+    for b, (sources, placed) in enumerate(((sources0, placed0), (sources1, placed1))):
+        block = slice(b * side, (b + 1) * side)
+        for slot in range(2):
+            here = placed[:, slot * side : (slot + 1) * side]
+            spread_out = jnp.dot(sources[...], here, preferred_element_type=F32)
+            for group in range(2):
+                r = 1 - slot if group else slot
+                updated = halves[group][r][:, block] + spread_out[group * pitch : group * pitch + rows]
+                fulls[group][r, :, block] = updated
+                if group:
+                    spare = jnp.zeros((pitch - rows, side), F32)
+                    pieces[r][:, block] = updated[:SPLIT].astype(BF16)
+                    tail = jnp.concatenate([updated[SPLIT:], spare], axis=0).astype(BF16)
+                    pieces[2][r * (pitch - SPLIT) : (r + 1) * (pitch - SPLIT), block] = tail
 
 
 def paired_shards(energy, depth_speed, ocean_mask, interp_first, interp_second, transfer_matrix, growth):
@@ -541,6 +548,7 @@
 
     *half0, own0 = first_step(0, field0, halo0, [shape(rows, 2 * cap)])
     peer0 = lax.ppermute(own0, "comp", peers)
+    growth, own0 = lax.optimization_barrier((growth, own0))
     first, second, transfer, rate = call(
         functools.partial(weights_body, plan),
         ids,
@@ -549,6 +557,10 @@
         [pltpu.VMEM((total, 4 * pitch), BF16)],
         cost=3,
     )
+    restore = call(
+        functools.partial(restore_body, plan), ids, (rate,), [shape(2 * plan.local, 2 * pitch)] * 2, limit=14, cost=0.5
+    )
+    halo1, restore = lax.optimization_barrier((halo1, restore))
     *half1, own1_0, own1_1 = first_step(1, field1, halo1, [shape(rows, cap)] * 2)
     own1 = (own1_0, own1_1)
     peer1 = [lax.ppermute(own, "comp", peers) for own in own1]
@@ -571,43 +583,48 @@
         cost=2,
     )
 
-    full0, sent0, full1 = [], [], []
+    sources, sent0 = [], []
     for b in range(2):
-        own = call(
+        source, sent = call(
             functools.partial(source_body, plan, b),
             ids,
-            (first, second, transfer, rate, placed[b], early[2 * b], early[2 * b + 1], own0, own1[b], peer1[b])
-            + (*half0, *half1, *full1),
-            [shape(2, rows, side, kind=F32), shape(rows + (24, 8)[b], cap), shape(2, rows, side, kind=F32)]
-            + [shape(rows, end - begin) for begin, end in plan.pieces()] * b,
-            [pltpu.VMEM((pitch, cap), BF16), pltpu.VMEM((2 * pitch, cap), BF16)],
-            limit=30,
-            cost=4,
+            (first, second, transfer, rate, early[2 * b], early[2 * b + 1], own0, own1[b], peer1[b]),
+            [shape(2 * pitch, cap), shape((pitch, rows)[b], cap)],
+            [pltpu.VMEM((pitch, cap), BF16)],
+            limit=20,
+            cost=3,
         )
-        full0.append(own[0])
-        sent0.append(own[1])
-        full1.append(own[2])
+        sources.append(source)
+        sent0.append(sent)
     rim1 = [lax.ppermute(sent0[0], "band", outer), lax.ppermute(sent0[1], ("band", "comp"), outer_beside)]
-    rim0 = [lax.ppermute(x, "band", inner) for x in own[3:]]
+    full0, full1, *pieces = call(
+        functools.partial(spread_body, plan),
+        ids,
+        (*sources, *placed, *half0, *half1),
+        [shape(2, rows, size, kind=F32)] * 2 + [shape(SPLIT, size)] * 2 + [shape(2 * (pitch - SPLIT), size)],
+        limit=14,
+        cost=2,
+    )
+    rim0 = [lax.ppermute(x, "band", inner) for x in pieces]
 
     width = 2 * plan.local
     done = pltpu.VMEM((2 * pitch, size), BF16)
-    partial, restore = call(
+    (partial,) = call(
         functools.partial(last_body, plan, 0),
         ids,
-        (courant, depth_speed, ocean, *full0, *rim0),
-        [shape(width, size, kind=F32), shape(width, 2 * pitch)],
-        [done] + rims,
-        limit=30,
+        (courant, depth_speed, ocean, full0, *rim0, restore[0]),
+        [shape(width, size, kind=F32)],
+        [pltpu.VMEM((2, pitch, size), BF16), done] + rims,
+        limit=20,
         cost=0.01,
     )
     (out,) = call(
         functools.partial(last_body, plan, 1),
         ids,
-        (courant, depth_speed, ocean, *full1, *rim1, *outer_placed, partial, restore),
+        (courant, depth_speed, ocean, full1, *rim1, *outer_placed, partial, restore[1]),
         [shape(*energy.shape)],
         [pltpu.VMEM((rows, size), BF16)] * 2 + [done] + rims,
-        limit=30,
+        limit=20,
         cost=4,
     )
     return out

time: 54.1 us -> 53 us (0.980)
  waiting for transfers between devices: 12.2 us -> 9.32 us
  Pallas kernels: 30.7 us -> 32 us
    ppermute x1, waiting for transfers between devices: 2.12 us -> 0.01 us  [paired_shards(): lax.ppermute(sent0[1], ('band', 'comp'), outer_beside)]
    pallas_call x12 -> x14, Pallas kernels: 30.7 us -> 32 us  [call(): pl.pallas_call(body, in_specs=[SMEM] + [VMEM] * len(operands), out_specs=...]
    ppermute x1, waiting for transfers between devices: 9.47 us -> 8.66 us  [paired_shards(): halo1 = lax.ppermute(field0, 'band', outer)]
    unnamed x16 -> x12, local copies, waits for them, and re-layouts: 1.41 us -> 1.4 us
  transfers between devices with their start and end apart: 10 -> 10, of which waited for: 4 -> 3; matrix products, arithmetic and copies ran while one was open for 0% -> 0% of each run, Pallas kernels for 45% -> 49%
where the time goes in v7:
time: 53 us; the launch traced here: 52.7 us
  Pallas kernels  32 us (60%)
  waiting for transfers between devices  9.32 us (18%)
  starting transfers between devices  9.07 us (17%)
  local copies, waits for them, and re-layouts  1.41 us (3%)
  other arithmetic  0.78 us (1%)
    pallas_call x14, Pallas kernels, call(): pl.pallas_call(body, in_specs=[SMEM] + [VMEM] * len(operands), out_specs=...  32 us
    ppermute x1, waiting for transfers between devices, paired_shards(): halo1 = lax.ppermute(field0, 'band', outer)  8.66 us
    ppermute x1, starting transfers between devices, paired_shards(): halo1 = lax.ppermute(field0, 'band', outer)  2.63 us
    ppermute x2, starting transfers between devices, paired_shards(): peer1 = [lax.ppermute(own, 'comp', peers) for own in own1]  1.94 us
    ppermute x1, starting transfers between devices, paired_shards(): lax.ppermute(sent0[0], 'band', outer)  1.92 us
    unnamed x12, local copies, waits for them, and re-layouts  1.4 us
    ppermute x1, starting transfers between devices, paired_shards(): peer0 = lax.ppermute(own0, 'comp', peers)  1.31 us
  transfers between devices with their start and end apart: 10, of which 3 were waited for; matrix products, arithmetic and copies ran while one was open for 0% of the time, Pallas kernels for 49%

profile of v7, /device:TPU:1, one launch (start us, length us, event | category | flops | bytes accessed | tf_op | source)
XLA Modules:
  0.0 52.7 jit_solution(19951441670338202)
XLA Ops:
  0.0 0.7 %convert_element_type.4.mask = f32[2,1024]{1,0:T(2,128)S(1)} convert(s32[2,1024]{1,0:T(2,128)} %param.9) | non-fusion elementwise | flops 2048 | bytes 16384 | tf_op jit(solution)/shard_map/convert_element_type | solution.py:523
  0.7 0.1 pad_add_fusion.ids
  0.8 1.4 %copy-done.1 = bf16[360,2,1024]{2,1,0:T(2,128)(2,1)S(1)} copy-done((bf16[360,2,1024]{2,1,0:T(2,128)(2,1)S(1)}, bf16[360,2,1024]{2,1,0:T(2,128)(2,1)}, u32[]{:S(2)}) %copy-start.1) | copy-done | bytes 1474584
  2.2 2.2 %shard_map.73 = (bf16[2,184,1024]{2,1,0:T(8,128)(2,1)S(1)}, bf16[2,184,1024]{2,1,0:T(8,128)(2,1)S(1)}, f32[2,2,184,128]{3,2,1,0:T(8,128)S(1)}) custom-call(s32[3]{0:T(128)S(1)} %pad_add_fusion.ids, bf16[360,2,1024]{2,1,0:T(2,128)(2,1)S(1)} %copy-done.1, f32[2,1024]{1,0:T(2,128)S(1)} %convert_element_type.4.mask), custom_call_target="tpu_custom_call" | custom-call | flops 2200000000 | tf_op jit(solution)/shard_map/pallas_call | solution.py:173
  4.4 0.1 collective-permute-start
  4.5 2.6 %collective-permute-start.2 = (bf16[2,184,1024]{2,1,0:T(8,128)(2,1)S(1)}, bf16[2,184,1024]{2,1,0:T(8,128)(2,1)S(1)}, u32[]{:S(2)}, u32[]{:S(2)}) collective-permute-start(bf16[2,184,1024]{2,1,0:T(8,128)(2,1)S(1)} %get-tuple-element.48.field), channel_id=1, source_target_pairs={{0,30},{2,4},{4,2},{6,8},{8,6},{10,12},{12,10},{14,16},{16,14},{18... | collective-permute-start | bytes 2261000 | tf_op jit(solution)/shard_map/ppermute | solution.py:534
  7.1 1.3 %shard_map.74 = (bf16[768,1024]{1,0:T(8,128)(2,1)S(1)}, bf16[768,1024]{1,0:T(8,128)(2,1)S(1)}) custom-call(s32[3]{0:T(128)S(1)} %pad_add_fusion.ids, f32[2,1024]{1,0:T(2,128)S(1)} %convert_element_type.4.mask), custom_call_target="tpu_custom_call" | custom-call | flops 2200000000 | tf_op jit(solution)/shard_map/pallas_call | solution.py:173
  8.4 0.0 copy-start.5
  8.5 0.0 copy-start.4
  8.5 2.5 %shard_map.75 = (f32[184,1024]{1,0:T(8,128)S(1)}, f32[184,1024]{1,0:T(8,128)S(1)}, bf16[184,1536]{1,0:T(8,128)(2,1)S(1)}) custom-call(s32[3]{0:T(128)S(1)} %pad_add_fusion.ids, f32[2,2,184,128]{3,2,1,0:T(8,128)S(1)} %get-tuple-element.47.courant, f32[2,1024]{1,0:T(2,128)S(1)} %copy-done, f32[2,1024]{1,0:T(2,128)S(1)} %convert_element_type.4.mask, ...), custom_call_target="tpu_custom_call" | custom-call | flops 2200000000 | tf_op jit(solution)/shard_map/pallas_call | solution.py:173
  10.9 1.3 %collective-permute-start.1 = (bf16[184,1536]{1,0:T(8,128)(2,1)S(1)}, bf16[184,1536]{1,0:T(8,128)(2,1)S(1)}, u32[]{:S(2)}, u32[]{:S(2)}) collective-permute-start(bf16[184,1536]{1,0:T(8,128)(2,1)S(1)} %get-tuple-element.58.own0.rest_2_), channel_id=1, source_target_pairs={{0,1},{1,0},{2,3},{3,2},{4,5},{5,4},{6,7},{7,6},{8,9},{9,8},{10,11... | collective-permute-start | bytes 1695752 | tf_op jit(solution)/shard_map/ppermute | solution.py:550
  12.3 3.1 %shard_map.76 = (bf16[736,768]{1,0:T(8,128)(2,1)S(1)}, bf16[720,768]{1,0:T(8,128)(2,1)S(1)}, bf16[384,720]{1,0:T(8,128)(2,1)S(1)}, f32[384,128]{1,0:T(8,128)S(1)}) custom-call(s32[3]{0:T(128)S(1)} %pad_add_fusion.ids, bf16[720,720]{1,0:T(8,128)(2,1)S(1)} %copy-done.2, bf16[720,720]{1,0:T(8,128)(2,1)S(1)} %copy-done.3, bf16[720,720]{1,0:T(8,128)(2,1)S(1)} %copy-done.4, ...), custom_call_target="tpu_custom_call" | custom-call | flops 3300000000 | tf_op jit(solution)/shard_map/pallas_call | solution.py:173
  15.4 0.8 %shard_map.77 = (bf16[720,384]{1,0:T(8,128)(2,1)S(1)}, bf16[720,384]{1,0:T(8,128)(2,1)S(1)}) custom-call(s32[3]{0:T(128)S(1)} %pad_add_fusion.ids, f32[384,128]{1,0:T(8,128)S(1)} %get-tuple-element.57.growth), custom_call_target="tpu_custom_call" | custom-call | flops 550000000 | tf_op jit(solution)/shard_map/pallas_call | solution.py:173
  16.2 8.7 %collective-permute-done.2.halo.mask = bf16[2,184,1024]{2,1,0:T(8,128)(2,1)S(1)} collective-permute-done((bf16[2,184,1024]{2,1,0:T(8,128)(2,1)S(1)}, bf16[2,184,1024]{2,1,0:T(8,128)(2,1)S(1)}, u32[]{:S(2)}, u32[]{:S(2)}) %collective-permute-start.2) | collective-permute-done | bytes 753696 | tf_op jit(solution)/shard_map/ppermute | solution.py:534
  24.8 2.5 %shard_map.78 = (f32[184,1024]{1,0:T(8,128)S(1)}, f32[184,1024]{1,0:T(8,128)S(1)}, bf16[184,768]{1,0:T(8,128)(2,1)S(1)}, bf16[184,768]{1,0:T(8,128)(2,1)S(1)}) custom-call(s32[3]{0:T(128)S(1)} %pad_add_fusion.ids, f32[2,2,184,128]{3,2,1,0:T(8,128)S(1)} %get-tuple-element.47.courant, f32[2,1024]{1,0:T(2,128)S(1)} %copy-done, ...), custom_call_target="tpu_custom_call" | custom-call | flops 2200000000 | tf_op jit(solution)/shard_map/pallas_call | solution.py:173
  27.4 1.9 %collective-permute-start.3 = (bf16[184,768]{1,0:T(8,128)(2,1)S(1)}, bf16[184,768]{1,0:T(8,128)(2,1)S(1)}, u32[]{:S(2)}, u32[]{:S(2)}) collective-permute-start(bf16[184,768]{1,0:T(8,128)(2,1)S(1)} %get-tuple-element.62.own1_0.rest_3_), channel_id=1, source_target_pairs={{0,1},{1,0},{2,3},{3,2},{4,5},{5,4},{6,7},{7,6},{8,9},{9,8},{10,11... | collective-permute-start | bytes 847880 | tf_op jit(solution)/shard_map/ppermute | solution.py:566
  29.2 0.1 collective-permute-start.4
  29.3 3.0 %shard_map.79 = (f32[736,768]{1,0:T(8,128)S(1)}, f32[720,768]{1,0:T(8,128)S(1)}, f32[736,768]{1,0:T(8,128)S(1)}, f32[720,768]{1,0:T(8,128)S(1)}) custom-call(s32[3]{0:T(128)S(1)} %pad_add_fusion.ids, bf16[736,768]{1,0:T(8,128)(2,1)S(1)} %get-tuple-element.54.first, bf16[720,768]{1,0:T(8,128)(2,1)S(1)} %get-tuple-element.55.second, ...), custom_call_target="tpu_custom_call" | custom-call | flops 3300000000 | tf_op jit(solution)/shard_map/pallas_call | solution.py:173
  32.4 1.9 %shard_map.80 = (f32[736,768]{1,0:T(8,128)S(1)}, f32[720,768]{1,0:T(8,128)S(1)}, f32[736,768]{1,0:T(8,128)S(1)}, f32[720,768]{1,0:T(8,128)S(1)}) custom-call(s32[3]{0:T(128)S(1)} %pad_add_fusion.ids, bf16[736,768]{1,0:T(8,128)(2,1)S(1)} %get-tuple-element.54.first, bf16[720,768]{1,0:T(8,128)(2,1)S(1)} %get-tuple-element.55.second, ...), custom_call_target="tpu_custom_call" | custom-call | flops 2200000000 | tf_op jit(solution)/shard_map/pallas_call | solution.py:173
  34.3 0.3 collective-permute-done.3.rest_4_
  34.6 2.5 %shard_map.81 = (bf16[384,768]{1,0:T(8,128)(2,1)S(1)}, bf16[192,768]{1,0:T(8,128)(2,1)S(1)}) custom-call(s32[3]{0:T(128)S(1)} %pad_add_fusion.ids, bf16[736,768]{1,0:T(8,128)(2,1)S(1)} %get-tuple-element.54.first, bf16[720,768]{1,0:T(8,128)(2,1)S(1)} %get-tuple-element.55.second, bf16[384,720]{1,0:T(8,128)(2,1)S(1)} %get-tuple-element.56.transfer, ...), custom_call_target="tpu_custom_call" | custom-call | flops 3300000000 | tf_op jit(solution)/shard_map/pallas_call | solution.py:173
  37.1 1.9 %collective-permute-start.5 = (bf16[192,768]{1,0:T(8,128)(2,1)S(1)}, bf16[192,768]{1,0:T(8,128)(2,1)S(1)}, u32[]{:S(2)}, u32[]{:S(2)}) collective-permute-start(bf16[192,768]{1,0:T(8,128)(2,1)S(1)} %get-tuple-element.79), channel_id=1, source_target_pairs={{0,30},{2,4},{4,2},{6,8},{8,6},{10,12},{12,10},{14,16},{16,14},{18... | collective-permute-start | bytes 884744 | tf_op jit(solution)/shard_map/ppermute | solution.py:599
  39.1 2.3 %shard_map.82 = (bf16[384,768]{1,0:T(8,128)(2,1)S(1)}, bf16[184,768]{1,0:T(8,128)(2,1)S(1)}) custom-call(s32[3]{0:T(128)S(1)} %pad_add_fusion.ids, bf16[736,768]{1,0:T(8,128)(2,1)S(1)} %get-tuple-element.54.first, bf16[720,768]{1,0:T(8,128)(2,1)S(1)} %get-tuple-element.55.second, bf16[384,720]{1,0:T(8,128)(2,1)S(1)} %get-tuple-element.56.transfer, ...), custom_call_target="tpu_custom_call" | custom-call | flops 3300000000 | tf_op jit(solution)/shard_map/pallas_call | solution.py:173
  41.4 0.5 collective-permute-start.6
  41.9 2.0 %shard_map.83 = (f32[2,184,1024]{2,1,0:T(8,128)S(1)}, f32[2,184,1024]{2,1,0:T(8,128)S(1)}, bf16[128,1024]{1,0:T(8,128)(2,1)S(1)}, bf16[128,1024]{1,0:T(8,128)(2,1)S(1)}, bf16[128,1024]{1,0:T(8,128)(2,1)S(1)}) custom-call(s32[3]{0:T(128)S(1)} %pad_add_fusion.ids, bf16[384,768]{1,0:T(8,128)(2,1)S(1)} %get-tuple-element.70.sources0, ...), custom_call_target="tpu_custom_call" | custom-call | flops 2200000000 | tf_op jit(solution)/shard_map/pallas_call | solution.py:173
  43.9 0.1 collective-permute-start.7
  44.0 0.5 collective-permute-start.8
  44.5 0.1 collective-permute-start.9
  44.5 1.3 %shard_map.84 = (bf16[768,1024]{1,0:T(8,128)(2,1)S(1)}, bf16[768,1024]{1,0:T(8,128)(2,1)S(1)}) custom-call(s32[3]{0:T(128)S(1)} %pad_add_fusion.ids, bf16[2,184,1024]{2,1,0:T(8,128)(2,1)S(1)} %collective-permute-done.2.halo.mask), custom_call_target="tpu_custom_call" | custom-call | flops 11000000 | tf_op jit(solution)/shard_map/pallas_call | solution.py:173
  45.9 0.3 collective-permute-done.9.rest_2_
  46.2 2.3 %shard_map.85.rest_4_ = f32[720,1024]{1,0:T(8,128)S(1)} custom-call(s32[3]{0:T(128)S(1)} %pad_add_fusion.ids, f32[2,2,184,128]{3,2,1,0:T(8,128)S(1)} %get-tuple-element.47.courant, f32[2,1024]{1,0:T(2,128)S(1)} %copy-done, f32[2,1024]{1,0:T(2,128)S(1)} %convert_element_type.4.mask, f32[2,184,1024]{2,1,0:T(8,128)S(1)} %get-tuple-element.83.full, ...), custom_call_target="tpu_custom_call" | custom-call | flops 11000000 | tf_op jit(solution)/shard_map/pallas_call | solution.py:173
  48.6 4.2 %shard_map.86 = bf16[360,2,1024]{2,1,0:T(2,128)(2,1)} custom-call(s32[3]{0:T(128)S(1)} %pad_add_fusion.ids, f32[2,2,184,128]{3,2,1,0:T(8,128)S(1)} %get-tuple-element.47.courant, f32[2,1024]{1,0:T(2,128)S(1)} %copy-done, f32[2,1024]{1,0:T(2,128)S(1)} %convert_element_type.4.mask, f32[2,184,1024]{2,1,0:T(8,128)S(1)} %get-tuple-element.78.full, ...), custom_call_target="tpu_custom_call" | custom-call | flops 4400000000 | tf_op jit(solution)/shard_map/pallas_call | solution.py:173
  (17 shorter events, 0.0 us)
Async XLA Ops:
  0.8 1.4 %copy-start.1 = (bf16[360,2,1024]{2,1,0:T(2,128)(2,1)S(1)}, bf16[360,2,1024]{2,1,0:T(2,128)(2,1)}, u32[]{:S(2)}) copy-start(bf16[360,2,1024]{2,1,0:T(2,128)(2,1)} %energy.1) | copy-start | bytes 4423684
  4.4 4.0 %collective-permute-start = (bf16[2,184,1024]{2,1,0:T(8,128)(2,1)S(1)}, bf16[2,184,1024]{2,1,0:T(8,128)(2,1)S(1)}, u32[]{:S(2)}, u32[]{:S(2)}) collective-permute-start(bf16[2,184,1024]{2,1,0:T(8,128)(2,1)S(1)} %get-tuple-element.49.field), channel_id=1, source_target_pairs={{0,2},{2,0},{4,6},{6,4},{8,10},{10,8},{12,14},{14,12},{16,18},{18,... | collective-permute-start | bytes 2261000 | tf_op jit(solution)/shard_map/ppermute | solution.py:533
  4.5 3.9 %copy-start = (f32[2,1024]{1,0:T(2,128)S(1)}, f32[2,1024]{1,0:T(2,128)}, u32[]{:S(2)}) copy-start(f32[2,1024]{1,0:T(2,128)} %depth.7) | copy-start | bytes 24580
  4.5 20.3 %collective-permute-start.2 = (bf16[2,184,1024]{2,1,0:T(8,128)(2,1)S(1)}, bf16[2,184,1024]{2,1,0:T(8,128)(2,1)S(1)}, u32[]{:S(2)}, u32[]{:S(2)}) collective-permute-start(bf16[2,184,1024]{2,1,0:T(8,128)(2,1)S(1)} %get-tuple-element.48.field), channel_id=1, source_target_pairs={{0,30},{2,4},{4,2},{6,8},{8,6},{10,12},{12,10},{14,16},{16,14},{18... | collective-permute-start | bytes 2261000 | tf_op jit(solution)/shard_map/ppermute | solution.py:534
  8.4 3.8 %copy-start.5 = (f32[720]{0:T(1024)S(1)}, f32[720]{0:T(1024)}, u32[]{:S(2)}) copy-start(f32[720]{0:T(1024)} %param.13) | copy-start | bytes 8644
  8.4 3.8 %copy-start.2 = (bf16[720,720]{1,0:T(8,128)(2,1)S(1)}, bf16[720,720]{1,0:T(8,128)(2,1)}, u32[]{:S(2)}) copy-start(bf16[720,720]{1,0:T(8,128)(2,1)} %first.1) | copy-start | bytes 3110404
  8.4 3.8 %copy-start.3 = (bf16[720,720]{1,0:T(8,128)(2,1)S(1)}, bf16[720,720]{1,0:T(8,128)(2,1)}, u32[]{:S(2)}) copy-start(bf16[720,720]{1,0:T(8,128)(2,1)} %second.1) | copy-start | bytes 3110404
  8.5 3.8 %copy-start.4 = (bf16[720,720]{1,0:T(8,128)(2,1)S(1)}, bf16[720,720]{1,0:T(8,128)(2,1)}, u32[]{:S(2)}) copy-start(bf16[720,720]{1,0:T(8,128)(2,1)} %transfer.1) | copy-start | bytes 3110404
  10.9 21.4 %collective-permute-start.1 = (bf16[184,1536]{1,0:T(8,128)(2,1)S(1)}, bf16[184,1536]{1,0:T(8,128)(2,1)S(1)}, u32[]{:S(2)}, u32[]{:S(2)}) collective-permute-start(bf16[184,1536]{1,0:T(8,128)(2,1)S(1)} %get-tuple-element.58.own0.rest_2_), channel_id=1, source_target_pairs={{0,1},{1,0},{2,3},{3,2},{4,5},{5,4},{6,7},{7,6},{8,9},{9,8},{10,11... | collective-permute-start | bytes 1695752 | tf_op jit(solution)/shard_map/ppermute | solution.py:550
  27.4 7.3 %collective-permute-start.3 = (bf16[184,768]{1,0:T(8,128)(2,1)S(1)}, bf16[184,768]{1,0:T(8,128)(2,1)S(1)}, u32[]{:S(2)}, u32[]{:S(2)}) collective-permute-start(bf16[184,768]{1,0:T(8,128)(2,1)S(1)} %get-tuple-element.62.own1_0.rest_3_), channel_id=1, source_target_pairs={{0,1},{1,0},{2,3},{3,2},{4,5},{5,4},{6,7},{7,6},{8,9},{9,8},{10,11... | collective-permute-start | bytes 847880 | tf_op jit(solution)/shard_map/ppermute | solution.py:566
  29.2 9.8 %collective-permute-start.4 = (bf16[184,768]{1,0:T(8,128)(2,1)S(1)}, bf16[184,768]{1,0:T(8,128)(2,1)S(1)}, u32[]{:S(2)}, u32[]{:S(2)}) collective-permute-start(bf16[184,768]{1,0:T(8,128)(2,1)S(1)} %get-tuple-element.63.own1_1.rest_3_), channel_id=1, source_target_pairs={{0,1},{1,0},{2,3},{3,2},{4,5},{5,4},{6,7},{7,6},{8,9},{9,8},{10,11... | collective-permute-start | bytes 847880 | tf_op jit(solution)/shard_map/ppermute | solution.py:566
  37.1 11.4 %collective-permute-start.5 = (bf16[192,768]{1,0:T(8,128)(2,1)S(1)}, bf16[192,768]{1,0:T(8,128)(2,1)S(1)}, u32[]{:S(2)}, u32[]{:S(2)}) collective-permute-start(bf16[192,768]{1,0:T(8,128)(2,1)S(1)} %get-tuple-element.79), channel_id=1, source_target_pairs={{0,30},{2,4},{4,2},{6,8},{8,6},{10,12},{12,10},{14,16},{16,14},{18... | collective-permute-start | bytes 884744 | tf_op jit(solution)/shard_map/ppermute | solution.py:599
  41.4 7.1 %collective-permute-start.6 = (bf16[184,768]{1,0:T(8,128)(2,1)S(1)}, bf16[184,768]{1,0:T(8,128)(2,1)S(1)}, u32[]{:S(2)}, u32[]{:S(2)}) collective-permute-start(bf16[184,768]{1,0:T(8,128)(2,1)S(1)} %get-tuple-element.80), channel_id=1, source_target_pairs={{2,4},{3,5},{4,2},{5,3},{6,8},{7,9},{8,6},{9,7},{10,12},{11,13},{1... | collective-permute-start | bytes 847880 | tf_op jit(solution)/shard_map/ppermute | solution.py:599
  43.9 2.0 %collective-permute-start.7 = (bf16[128,1024]{1,0:T(8,128)(2,1)S(1)}, bf16[128,1024]{1,0:T(8,128)(2,1)S(1)}, u32[]{:S(2)}, u32[]{:S(2)}) collective-permute-start(bf16[128,1024]{1,0:T(8,128)(2,1)S(1)} %get-tuple-element.84), channel_id=1, source_target_pairs={{0,2},{2,0},{4,6},{6,4},{8,10},{10,8},{12,14},{14,12},{16,18},{18,... | collective-permute-start | bytes 786440 | tf_op jit(solution)/shard_map/ppermute | solution.py:608
  44.0 1.9 %collective-permute-start.8 = (bf16[128,1024]{1,0:T(8,128)(2,1)S(1)}, bf16[128,1024]{1,0:T(8,128)(2,1)S(1)}, u32[]{:S(2)}, u32[]{:S(2)}) collective-permute-start(bf16[128,1024]{1,0:T(8,128)(2,1)S(1)} %get-tuple-element.85), channel_id=1, source_target_pairs={{0,2},{2,0},{4,6},{6,4},{8,10},{10,8},{12,14},{14,12},{16,18},{18,... | collective-permute-start | bytes 786440 | tf_op jit(solution)/shard_map/ppermute | solution.py:608
  44.5 1.8 %collective-permute-start.9 = (bf16[128,1024]{1,0:T(8,128)(2,1)S(1)}, bf16[128,1024]{1,0:T(8,128)(2,1)S(1)}, u32[]{:S(2)}, u32[]{:S(2)}) collective-permute-start(bf16[128,1024]{1,0:T(8,128)(2,1)S(1)} %get-tuple-element.86), channel_id=1, source_target_pairs={{0,2},{2,0},{4,6},{6,4},{8,10},{10,8},{12,14},{14,12},{16,18},{18,... | collective-permute-start | bytes 786440 | tf_op jit(solution)/shard_map/ppermute | solution.py:608

commit v8 on v7

--- a/solution.py
+++ b/solution.py
@@ -118,6 +118,7 @@
         self.pitch = -(-self.slots // 16) * 16
         self.out_rows = -(-(self.total + 1) // 16) * 16
         self.side = columns // 2
+        self.starts = (0, 2 * self.pitch, 3 * self.pitch, self.pitch)
         self.cap = 3 * columns // 4
 
     def slot_parts(self, slot):
@@ -327,7 +328,13 @@
         if group == 0:
             spectra[0][:, b * plan.cap : (b + 1) * plan.cap] = gathered
         else:
-            spectra[b][...] = gathered
+            whole_rows = plan.rows // 16 * 16
+            spectra[b][:whole_rows] = gathered[:whole_rows]
+            tail = gathered[whole_rows:].astype(F32)
+            if spectra[b].shape[0] > plan.rows:
+                spare = jnp.zeros((spectra[b].shape[0] - plan.rows, plan.cap), F32)
+                tail = jnp.concatenate([tail, spare], axis=0)
+            spectra[b][whole_rows:] = tail.astype(BF16)
 
 
 def last_body(plan, group, ids, courant, depth, mask, full, *rest):
@@ -389,23 +396,20 @@
         south = southward(ids, group)
         comp = plan.slot_comp(lax.broadcasted_iota(jnp.int32, (pitch, 128), 0), south) + local * comp_index
         chosen.append(spread(comp, total) == lax.broadcasted_iota(jnp.int32, (pitch, total), 1))
-    for owner in (comp_index, 1 - comp_index):
-        lane = lax.broadcasted_iota(jnp.int32, (8, 2 * pitch), 1)
-        group = jnp.where(lane >= pitch, 1, 0)
-        source = plan.slot_comp(lane - pitch * group, ids[0] == group) + local * owner
-        source = jnp.concatenate([source] * (total // 8), axis=0)
-        hot = one_hot(source == lax.broadcasted_iota(jnp.int32, (total, 2 * pitch), 0))
-        if owner is comp_index:
-            columns[:, : 2 * pitch] = hot
-        else:
-            columns[:, 2 * pitch :] = hot
+    lane = lax.broadcasted_iota(jnp.int32, (8, 4 * pitch), 1)
+    source, summed = jnp.full(lane.shape, -4 * total, jnp.int32), jnp.zeros(lane.shape, F32)
+    for i, start in enumerate(plan.starts):
+        slot = lane - start
+        here = jnp.logical_and(slot >= 0, slot < pitch)
+        owner = comp_index if i < 2 else 1 - comp_index
+        source = jnp.where(here, plan.slot_comp(slot, southward(ids, i % 2)) + local * owner, source)
+        summed = jnp.where(jnp.logical_and(here, slot < plan.slots), 1.0, summed)
+    source = jnp.concatenate([source] * (total // 8), axis=0)
+    columns[...] = one_hot(source == lax.broadcasted_iota(jnp.int32, (total, 4 * pitch), 0))
     first_out[:total] = jnp.dot(first[...], columns[...], preferred_element_type=F32).astype(BF16)
     extra = plan.out_rows - total
-    place = lax.broadcasted_iota(jnp.int32, (extra, 4 * pitch), 1)
-    for i in range(1, 4):
-        place = jnp.where(place >= pitch, place - pitch, place)
     top = lax.broadcasted_iota(jnp.int32, (extra, 4 * pitch), 0) == 0
-    first_out[total:] = one_hot(jnp.logical_and(top, place < plan.slots))
+    first_out[total:] = jnp.where(top, jnp.concatenate([summed] * (extra // 8), axis=0), 0.0).astype(BF16)
     second_out[...] = jnp.dot(second[...], columns[...], preferred_element_type=F32).astype(BF16)
     for group in range(2):
         at = slice(group * pitch, (group + 1) * pitch)
@@ -429,22 +433,21 @@
             cells[i * pitch + whole_rows : (i + 1) * pitch] = tail.astype(BF16)
 
 
-def early_body(plan, ids, first, second, own0, own1_0, own1_1, *rest):
+def early_body(plan, ids, first, second, own0, *rest):
     outs, cells = rest[:4], rest[4]
-    pitch = plan.pitch
-    for b, own1 in enumerate((own1_0, own1_1)):
-        fill_cells(plan, cells, (own0[:, b * plan.cap : (b + 1) * plan.cap], own1[...]))
+    for b in range(2):
+        fill_cells(plan, cells, (own0[:, b * plan.cap : (b + 1) * plan.cap],))
         for c in range(0, plan.cap, TILE):
             at = slice(c, c + TILE)
             for weights, out in ((first, outs[2 * b]), (second, outs[2 * b + 1])):
-                out[:, at] = jnp.dot(weights[:, : 2 * pitch], cells[:, at], preferred_element_type=F32)
-
-
-def middle_body(plan, ids, first, second, peer0, *rest):
+                out[:, at] = jnp.dot(weights[:, : plan.pitch], cells[:, at], preferred_element_type=F32)
+
+
+def middle_body(plan, ids, first, second, own1_0, own1_1, peer0, *rest):
     partial, outs, cells = rest[:4], rest[4:8], rest[8]
-    known = slice(2 * plan.pitch, 3 * plan.pitch)
-    for b in range(2):
-        fill_cells(plan, cells, (peer0[:, b * plan.cap : (b + 1) * plan.cap],))
+    known = slice(plan.starts[1], plan.starts[1] + 2 * plan.pitch)
+    for b, own1 in enumerate((own1_0, own1_1)):
+        fill_cells(plan, cells, (own1[: plan.rows], peer0[:, b * plan.cap : (b + 1) * plan.cap]))
         for c in range(0, plan.cap, TILE):
             at = slice(c, c + TILE)
             for i, weights in ((2 * b, first), (2 * b + 1, second)):
@@ -455,50 +458,47 @@
 def source_body(plan, b, ids, first, second, transfer, growth, *rest):
     early_first, early_second, own0, own1, peer1, sources, sent0, cells = rest
     total, rows, pitch = plan.total, plan.rows, plan.pitch
-    known = 3 * pitch
-    fill_cells(plan, cells, (peer1[...],))
+    known = slice(plan.starts[3], plan.starts[3] + pitch)
+    fill_cells(plan, cells, (peer1[:rows],))
     extra = sent0.shape[0] - rows
-    for c in range(0, plan.cap, TILE):
-        at = slice(c, c + TILE)
-        piece = cells[:, at]
-        forward = early_first[:, at] + jnp.dot(first[:, known:], piece, preferred_element_type=F32)
-        backward = early_second[:, at] + jnp.dot(second[:, known:], piece, preferred_element_type=F32)
-        product = (forward[:total] * backward).astype(BF16)
-        nonlinear = jnp.dot(transfer[...], product, preferred_element_type=F32)
-        level = forward[total : total + 1] / total
-        damping = level * level / (1.0 + level * level)
-        for group in range(2):
-            begin = group * pitch
-            spectra = (own1[:, at] if group else own0[:, b * plan.cap + c : b * plan.cap + c + TILE]).astype(F32)
-            spectra = jnp.concatenate([spectra, jnp.zeros((pitch - rows, TILE), F32)], axis=0)
-            rate = spread(growth[begin : begin + pitch], TILE)
-            source = SOURCE_STEP * (nonlinear[begin : begin + pitch] + (rate - damping) * spectra)
-            source = source.astype(BF16)
-            sources[begin : begin + pitch, at] = source
-            if group == 0:
-                sent0[:, at] = (spectra + source.astype(F32))[: rows + extra].astype(BF16)
+    piece = cells[...]
+    forward = early_first[...] + jnp.dot(first[:, known], piece, preferred_element_type=F32)
+    backward = early_second[...] + jnp.dot(second[:, known], piece, preferred_element_type=F32)
+    product = (forward[:total] * backward).astype(BF16)
+    nonlinear = jnp.dot(transfer[...], product, preferred_element_type=F32)
+    level = forward[total : total + 1] / total
+    damping = level * level / (1.0 + level * level)
+    for group in range(2):
+        begin = group * pitch
+        spectra = (own1[:rows] if group else own0[:, b * plan.cap : (b + 1) * plan.cap]).astype(F32)
+        spectra = jnp.concatenate([spectra, jnp.zeros((pitch - rows, plan.cap), F32)], axis=0)
+        rate = spread(growth[begin : begin + pitch], plan.cap)
+        source = SOURCE_STEP * (nonlinear[begin : begin + pitch] + (rate - damping) * spectra)
+        source = source.astype(BF16)
+        sources[begin : begin + pitch] = source
+        if group == 0:
+            sent0[...] = (spectra + source.astype(F32))[: rows + extra].astype(BF16)
 
 
 SPLIT = 128
 
 
-def spread_body(plan, ids, sources0, sources1, placed0, placed1, half00, half01, half10, half11, full0, full1, *pieces):
+def spread_body(plan, group, ids, sources0, sources1, placed0, placed1, half0, half1, full, *pieces):
     rows, pitch, side = plan.rows, plan.pitch, plan.side
-    halves, fulls = ((half00, half01), (half10, half11)), (full0, full1)
+    own = slice(group * pitch, (group + 1) * pitch)
     for b, (sources, placed) in enumerate(((sources0, placed0), (sources1, placed1))):
         block = slice(b * side, (b + 1) * side)
         for slot in range(2):
+            r = 1 - slot if group else slot
             here = placed[:, slot * side : (slot + 1) * side]
-            spread_out = jnp.dot(sources[...], here, preferred_element_type=F32)
-            for group in range(2):
-                r = 1 - slot if group else slot
-                updated = halves[group][r][:, block] + spread_out[group * pitch : group * pitch + rows]
-                fulls[group][r, :, block] = updated
-                if group:
-                    spare = jnp.zeros((pitch - rows, side), F32)
-                    pieces[r][:, block] = updated[:SPLIT].astype(BF16)
-                    tail = jnp.concatenate([updated[SPLIT:], spare], axis=0).astype(BF16)
-                    pieces[2][r * (pitch - SPLIT) : (r + 1) * (pitch - SPLIT), block] = tail
+            spread_out = jnp.dot(sources[own], here, preferred_element_type=F32)
+            updated = (half0, half1)[r][:, block] + spread_out[:rows]
+            full[r, :, block] = updated
+            if group:
+                spare = jnp.zeros((pitch - rows, side), F32)
+                pieces[r][:, block] = updated[:SPLIT].astype(BF16)
+                tail = jnp.concatenate([updated[SPLIT:], spare], axis=0).astype(BF16)
+                pieces[2][r * (pitch - SPLIT) : (r + 1) * (pitch - SPLIT), block] = tail
 
 
 def paired_shards(energy, depth_speed, ocean_mask, interp_first, interp_second, transfer_matrix, growth):
@@ -522,10 +522,16 @@
     rims = [pltpu.VMEM((2, 8, size), F32)] * 2
     ocean = ocean_mask.astype(F32)
 
+    cap, side = plan.cap, plan.side
+    def place(mask, neighbour, cost):
+        return call(functools.partial(place_body, plan, neighbour), ids, (mask,), [shape(cap, size)] * 2, limit=14, cost=cost)
+
+    placed = place(ocean, False, 2)
+    first_ocean, *placed = lax.optimization_barrier((ocean, *placed))
     field0, field1, courant = call(
         functools.partial(prep_body, plan),
         ids,
-        (energy, ocean),
+        (energy, first_ocean),
         [shape(2, rows, size)] * 2 + [shape(2, 2, rows, 128, kind=F32)],
         [pltpu.VMEM((4 * pitch, 2 * plan.local), BF16)],
         cost=2,
@@ -533,12 +539,6 @@
     halo0 = lax.ppermute(field1, "band", inner)
     halo1 = lax.ppermute(field0, "band", outer)
 
-    cap, side = plan.cap, plan.side
-    def place(mask, neighbour, cost):
-        return call(functools.partial(place_body, plan, neighbour), ids, (mask,), [shape(cap, size)] * 2, cost=cost)
-
-    placed = place(ocean, False, 2)
-    outer_placed = place(halo1, True, 0.01)
 
     def first_step(group, field, halo, spectra):
         operands = (courant, depth_speed, ocean, field, halo, *placed)
@@ -560,27 +560,30 @@
     restore = call(
         functools.partial(restore_body, plan), ids, (rate,), [shape(2 * plan.local, 2 * pitch)] * 2, limit=14, cost=0.5
     )
-    halo1, restore = lax.optimization_barrier((halo1, restore))
-    *half1, own1_0, own1_1 = first_step(1, field1, halo1, [shape(rows, cap)] * 2)
-    own1 = (own1_0, own1_1)
-    peer1 = [lax.ppermute(own, "comp", peers) for own in own1]
     early = call(
         functools.partial(early_body, plan),
         ids,
-        (first, second, own0, own1_0, own1_1),
+        (first, second, own0),
         [shape(plan.out_rows, cap, kind=F32), shape(total, cap, kind=F32)] * 2,
-        [pltpu.VMEM((2 * pitch, cap), BF16)],
-        limit=20,
-        cost=3,
-    )
+        [pltpu.VMEM((pitch, cap), BF16)],
+        limit=14,
+        cost=2,
+    )
+    halo1, restore, early = lax.optimization_barrier((halo1, restore, early))
+    *half1, own1_0, own1_1 = first_step(1, field1, halo1, [shape(rows, cap), shape(pitch, cap)])
+    own1 = (own1_0, own1_1)
+    peer1 = [lax.ppermute(own, "comp", peers) for own in own1]
+    halo1, own1_0 = lax.optimization_barrier((halo1, own1_0))
+    outer_placed = place(halo1, True, 1)
+    peer0, *outer_placed = lax.optimization_barrier((peer0, *outer_placed))
     early = call(
         functools.partial(middle_body, plan),
         ids,
-        (first, second, peer0, *early),
+        (first, second, own1_0, own1_1, peer0, *early),
         [shape(plan.out_rows, cap, kind=F32), shape(total, cap, kind=F32)] * 2,
-        [pltpu.VMEM((pitch, cap), BF16)],
-        limit=20,
-        cost=2,
+        [pltpu.VMEM((2 * pitch, cap), BF16)],
+        limit=14,
+        cost=3,
     )
 
     sources, sent0 = [], []
@@ -597,16 +600,16 @@
         sources.append(source)
         sent0.append(sent)
     rim1 = [lax.ppermute(sent0[0], "band", outer), lax.ppermute(sent0[1], ("band", "comp"), outer_beside)]
-    full0, full1, *pieces = call(
-        functools.partial(spread_body, plan),
-        ids,
-        (*sources, *placed, *half0, *half1),
-        [shape(2, rows, size, kind=F32)] * 2 + [shape(SPLIT, size)] * 2 + [shape(2 * (pitch - SPLIT), size)],
-        limit=14,
-        cost=2,
-    )
+
+    def spread_out(group, half, outs):
+        operands = (*sources, *placed, *half)
+        outs = [shape(2, rows, size, kind=F32)] + outs
+        return call(functools.partial(spread_body, plan, group), ids, operands, outs, limit=14, cost=1)
+
+    full1, *pieces = spread_out(1, half1, [shape(SPLIT, size)] * 2 + [shape(2 * (pitch - SPLIT), size)])
     rim0 = [lax.ppermute(x, "band", inner) for x in pieces]
 
+    (full0,) = spread_out(0, half0, [])
     width = 2 * plan.local
     done = pltpu.VMEM((2 * pitch, size), BF16)
     (partial,) = call(

time: 53 us -> 51.8 us (0.977)
  local copies, waits for them, and re-layouts: 1.41 us -> 0.13 us
    ppermute x2, waiting for transfers between devices: 0.32 us -> 1.82 us  [paired_shards(): peer1 = [lax.ppermute(own, 'comp', peers) for own in own1]]
    unnamed x12, local copies, waits for them, and re-layouts: 1.4 us -> 0.13 us
    ppermute x1, waiting for transfers between devices: 8.66 us -> 7.49 us  [paired_shards(): halo1 = lax.ppermute(field0, 'band', outer)]
    ppermute x1, starting transfers between devices: 1.92 us -> 0.9 us  [paired_shards(): lax.ppermute(sent0[0], 'band', outer)]
    ppermute x1, starting transfers between devices: 1.31 us -> 1.98 us  [paired_shards(): peer0 = lax.ppermute(own0, 'comp', peers)]
    pallas_call x14 -> x15, Pallas kernels: 32 us -> 32 us  [call(): pl.pallas_call(body, in_specs=[SMEM] + [VMEM] * len(operands), out_specs=...]
  transfers between devices with their start and end apart: 10 -> 10, of which waited for: 3 -> 4; matrix products, arithmetic and copies ran while one was open for 0% -> 0% of each run, Pallas kernels for 49% -> 47%
where the time goes in v8:
time: 51.8 us; the launch traced here: 51.5 us
  Pallas kernels  32 us (62%)
  waiting for transfers between devices  9.63 us (19%)
  starting transfers between devices  8.72 us (17%)
  other arithmetic  0.78 us (2%)
    pallas_call x15, Pallas kernels, call(): pl.pallas_call(body, in_specs=[SMEM] + [VMEM] * len(operands), out_specs=...  32 us
    ppermute x1, waiting for transfers between devices, paired_shards(): halo1 = lax.ppermute(field0, 'band', outer)  7.49 us
    ppermute x1, starting transfers between devices, paired_shards(): halo1 = lax.ppermute(field0, 'band', outer)  2.62 us
    ppermute x1, starting transfers between devices, paired_shards(): peer0 = lax.ppermute(own0, 'comp', peers)  1.98 us
    ppermute x2, waiting for transfers between devices, paired_shards(): peer1 = [lax.ppermute(own, 'comp', peers) for own in own1]  1.82 us
    ppermute x2, starting transfers between devices, paired_shards(): peer1 = [lax.ppermute(own, 'comp', peers) for own in own1]  1.78 us
  transfers between devices with their start and end apart: 10, of which 4 were waited for; matrix products, arithmetic and copies ran while one was open for 0% of the time, Pallas kernels for 47%

profile of v8, /device:TPU:1, one launch (start us, length us, event | category | flops | bytes accessed | tf_op | source)
XLA Modules:
  0.0 51.5 jit_solution(15784856564267493122)
XLA Ops:
  0.0 0.7 %convert_element_type.4.mask = f32[2,1024]{1,0:T(2,128)S(1)} convert(s32[2,1024]{1,0:T(2,128)} %param.9) | non-fusion elementwise | flops 2048 | bytes 16384 | tf_op jit(solution)/shard_map/convert_element_type | solution.py:523
  0.7 0.1 pad_add_fusion.ids
  0.8 1.3 %shard_map.73 = (bf16[768,1024]{1,0:T(8,128)(2,1)S(1)}, bf16[768,1024]{1,0:T(8,128)(2,1)S(1)}) custom-call(s32[3]{0:T(128)S(1)} %pad_add_fusion.ids, f32[2,1024]{1,0:T(2,128)S(1)} %convert_element_type.4.mask), custom_call_target="tpu_custom_call" | custom-call | flops 2200000000 | tf_op jit(solution)/shard_map/pallas_call | solution.py:174
  2.1 0.1 copy-done.1
  2.2 2.2 %shard_map.74 = (bf16[2,184,1024]{2,1,0:T(8,128)(2,1)S(1)}, bf16[2,184,1024]{2,1,0:T(8,128)(2,1)S(1)}, f32[2,2,184,128]{3,2,1,0:T(8,128)S(1)}) custom-call(s32[3]{0:T(128)S(1)} %pad_add_fusion.ids, bf16[360,2,1024]{2,1,0:T(2,128)(2,1)S(1)} %copy-done.1, f32[2,1024]{1,0:T(2,128)S(1)} %convert_element_type.4.mask), custom_call_target="tpu_custom_call" | custom-call | flops 2200000000 | tf_op jit(solution)/shard_map/pallas_call | solution.py:174
  4.4 0.1 collective-permute-start
  4.5 2.6 %collective-permute-start.1 = (bf16[2,184,1024]{2,1,0:T(8,128)(2,1)S(1)}, bf16[2,184,1024]{2,1,0:T(8,128)(2,1)S(1)}, u32[]{:S(2)}, u32[]{:S(2)}) collective-permute-start(bf16[2,184,1024]{2,1,0:T(8,128)(2,1)S(1)} %get-tuple-element.62.field), channel_id=1, source_target_pairs={{0,30},{2,4},{4,2},{6,8},{8,6},{10,12},{12,10},{14,16},{16,14},{18... | collective-permute-start | bytes 2261000 | tf_op jit(solution)/shard_map/ppermute | solution.py:540
  7.2 2.5 %shard_map.75 = (f32[184,1024]{1,0:T(8,128)S(1)}, f32[184,1024]{1,0:T(8,128)S(1)}, bf16[184,1536]{1,0:T(8,128)(2,1)S(1)}) custom-call(s32[3]{0:T(128)S(1)} %pad_add_fusion.ids, f32[2,2,184,128]{3,2,1,0:T(8,128)S(1)} %get-tuple-element.61.courant, f32[2,1024]{1,0:T(2,128)S(1)} %copy-done, f32[2,1024]{1,0:T(2,128)S(1)} %convert_element_type.4.mask, ...), custom_call_target="tpu_custom_call" | custom-call | flops 2200000000 | tf_op jit(solution)/shard_map/pallas_call | solution.py:174
  9.6 2.0 %collective-permute-start.2 = (bf16[184,1536]{1,0:T(8,128)(2,1)S(1)}, bf16[184,1536]{1,0:T(8,128)(2,1)S(1)}, u32[]{:S(2)}, u32[]{:S(2)}) collective-permute-start(bf16[184,1536]{1,0:T(8,128)(2,1)S(1)} %get-tuple-element.74.own0.rest_2_), channel_id=1, source_target_pairs={{0,1},{1,0},{2,3},{3,2},{4,5},{5,4},{6,7},{7,6},{8,9},{9,8},{10,11... | collective-permute-start | bytes 1695752 | tf_op jit(solution)/shard_map/ppermute | solution.py:550
  11.7 3.0 %shard_map.76 = (bf16[736,768]{1,0:T(8,128)(2,1)S(1)}, bf16[720,768]{1,0:T(8,128)(2,1)S(1)}, bf16[384,720]{1,0:T(8,128)(2,1)S(1)}, f32[384,128]{1,0:T(8,128)S(1)}) custom-call(s32[3]{0:T(128)S(1)} %pad_add_fusion.ids, bf16[720,720]{1,0:T(8,128)(2,1)S(1)} %copy-done.2, bf16[720,720]{1,0:T(8,128)(2,1)S(1)} %copy-done.3, bf16[720,720]{1,0:T(8,128)(2,1)S(1)} %copy-done.4, ...), custom_call_target="tpu_custom_call" | custom-call | flops 3300000000 | tf_op jit(solution)/shard_map/pallas_call | solution.py:174
  14.7 0.8 %shard_map.77 = (bf16[720,384]{1,0:T(8,128)(2,1)S(1)}, bf16[720,384]{1,0:T(8,128)(2,1)S(1)}) custom-call(s32[3]{0:T(128)S(1)} %pad_add_fusion.ids, f32[384,128]{1,0:T(8,128)S(1)} %get-tuple-element.71.growth), custom_call_target="tpu_custom_call" | custom-call | flops 550000000 | tf_op jit(solution)/shard_map/pallas_call | solution.py:174
  15.5 1.9 %shard_map.78 = (f32[736,768]{1,0:T(8,128)S(1)}, f32[720,768]{1,0:T(8,128)S(1)}, f32[736,768]{1,0:T(8,128)S(1)}, f32[720,768]{1,0:T(8,128)S(1)}) custom-call(s32[3]{0:T(128)S(1)} %pad_add_fusion.ids, bf16[736,768]{1,0:T(8,128)(2,1)S(1)} %get-tuple-element.68.first, bf16[720,768]{1,0:T(8,128)(2,1)S(1)} %get-tuple-element.69.second, ...), custom_call_target="tpu_custom_call" | custom-call | flops 2200000000 | tf_op jit(solution)/shard_map/pallas_call | solution.py:174
  17.3 7.5 %collective-permute-done.1.halo.mask = bf16[2,184,1024]{2,1,0:T(8,128)(2,1)S(1)} collective-permute-done((bf16[2,184,1024]{2,1,0:T(8,128)(2,1)S(1)}, bf16[2,184,1024]{2,1,0:T(8,128)(2,1)S(1)}, u32[]{:S(2)}, u32[]{:S(2)}) %collective-permute-start.1) | collective-permute-done | bytes 753696 | tf_op jit(solution)/shard_map/ppermute | solution.py:540
  24.8 2.5 %shard_map.79 = (f32[184,1024]{1,0:T(8,128)S(1)}, f32[184,1024]{1,0:T(8,128)S(1)}, bf16[184,768]{1,0:T(8,128)(2,1)S(1)}, bf16[192,768]{1,0:T(8,128)(2,1)S(1)}) custom-call(s32[3]{0:T(128)S(1)} %pad_add_fusion.ids, f32[2,2,184,128]{3,2,1,0:T(8,128)S(1)} %get-tuple-element.61.courant, f32[2,1024]{1,0:T(2,128)S(1)} %copy-done, ...), custom_call_target="tpu_custom_call" | custom-call | flops 2200000000 | tf_op jit(solution)/shard_map/pallas_call | solution.py:174
  27.3 1.7 %collective-permute-start.3 = (bf16[184,768]{1,0:T(8,128)(2,1)S(1)}, bf16[184,768]{1,0:T(8,128)(2,1)S(1)}, u32[]{:S(2)}, u32[]{:S(2)}) collective-permute-start(bf16[184,768]{1,0:T(8,128)(2,1)S(1)} %get-tuple-element.81.own1_0.rest_3_), channel_id=1, source_target_pairs={{0,1},{1,0},{2,3},{3,2},{4,5},{5,4},{6,7},{7,6},{8,9},{9,8},{10,11... | collective-permute-start | bytes 847880 | tf_op jit(solution)/shard_map/ppermute | solution.py:575
  29.0 0.1 collective-permute-start.4
  29.1 1.3 %shard_map.80 = (bf16[768,1024]{1,0:T(8,128)(2,1)S(1)}, bf16[768,1024]{1,0:T(8,128)(2,1)S(1)}) custom-call(s32[3]{0:T(128)S(1)} %pad_add_fusion.ids, bf16[2,184,1024]{2,1,0:T(8,128)(2,1)S(1)} %collective-permute-done.1.halo.mask), custom_call_target="tpu_custom_call" | custom-call | flops 1100000000 | tf_op jit(solution)/shard_map/pallas_call | solution.py:174
  30.5 3.1 %shard_map.81 = (f32[736,768]{1,0:T(8,128)S(1)}, f32[720,768]{1,0:T(8,128)S(1)}, f32[736,768]{1,0:T(8,128)S(1)}, f32[720,768]{1,0:T(8,128)S(1)}) custom-call(s32[3]{0:T(128)S(1)} %pad_add_fusion.ids, bf16[736,768]{1,0:T(8,128)(2,1)S(1)} %get-tuple-element.68.first, bf16[720,768]{1,0:T(8,128)(2,1)S(1)} %get-tuple-element.69.second, ...), custom_call_target="tpu_custom_call" | custom-call | flops 3300000000 | tf_op jit(solution)/shard_map/pallas_call | solution.py:174
  33.6 1.5 %collective-permute-done.3.rest_4_ = bf16[184,768]{1,0:T(8,128)(2,1)S(1)} collective-permute-done((bf16[184,768]{1,0:T(8,128)(2,1)S(1)}, bf16[184,768]{1,0:T(8,128)(2,1)S(1)}, u32[]{:S(2)}, u32[]{:S(2)}) %collective-permute-start.3) | collective-permute-done | bytes 282656 | tf_op jit(solution)/shard_map/ppermute | solution.py:575
  35.1 2.3 %shard_map.82 = (bf16[384,768]{1,0:T(8,128)(2,1)S(1)}, bf16[192,768]{1,0:T(8,128)(2,1)S(1)}) custom-call(s32[3]{0:T(128)S(1)} %pad_add_fusion.ids, bf16[736,768]{1,0:T(8,128)(2,1)S(1)} %get-tuple-element.68.first, bf16[720,768]{1,0:T(8,128)(2,1)S(1)} %get-tuple-element.69.second, bf16[384,720]{1,0:T(8,128)(2,1)S(1)} %get-tuple-element.70.transfer, ...), custom_call_target="tpu_custom_call" | custom-call | flops 3300000000 | tf_op jit(solution)/shard_map/pallas_call | solution.py:174
  37.3 0.9 %collective-permute-start.5 = (bf16[192,768]{1,0:T(8,128)(2,1)S(1)}, bf16[192,768]{1,0:T(8,128)(2,1)S(1)}, u32[]{:S(2)}, u32[]{:S(2)}) collective-permute-start(bf16[192,768]{1,0:T(8,128)(2,1)S(1)} %get-tuple-element.100), channel_id=1, source_target_pairs={{0,30},{2,4},{4,2},{6,8},{8,6},{10,12},{12,10},{14,16},{16,14},{18... | collective-permute-start | bytes 884744 | tf_op jit(solution)/shard_map/ppermute | solution.py:602
  38.2 0.3 collective-permute-done.4.rest_4_
  38.5 2.0 %shard_map.83 = (bf16[384,768]{1,0:T(8,128)(2,1)S(1)}, bf16[184,768]{1,0:T(8,128)(2,1)S(1)}) custom-call(s32[3]{0:T(128)S(1)} %pad_add_fusion.ids, bf16[736,768]{1,0:T(8,128)(2,1)S(1)} %get-tuple-element.68.first, bf16[720,768]{1,0:T(8,128)(2,1)S(1)} %get-tuple-element.69.second, bf16[384,720]{1,0:T(8,128)(2,1)S(1)} %get-tuple-element.70.transfer, ...), custom_call_target="tpu_custom_call" | custom-call | flops 3300000000 | tf_op jit(solution)/shard_map/pallas_call | solution.py:174
  40.5 0.7 %collective-permute-start.6 = (bf16[184,768]{1,0:T(8,128)(2,1)S(1)}, bf16[184,768]{1,0:T(8,128)(2,1)S(1)}, u32[]{:S(2)}, u32[]{:S(2)}) collective-permute-start(bf16[184,768]{1,0:T(8,128)(2,1)S(1)} %get-tuple-element.101), channel_id=1, source_target_pairs={{2,4},{3,5},{4,2},{5,3},{6,8},{7,9},{8,6},{9,7},{10,12},{11,13},{1... | collective-permute-start | bytes 847880 | tf_op jit(solution)/shard_map/ppermute | solution.py:602
  41.2 1.4 %shard_map.84 = (f32[2,184,1024]{2,1,0:T(8,128)S(1)}, bf16[128,1024]{1,0:T(8,128)(2,1)S(1)}, bf16[128,1024]{1,0:T(8,128)(2,1)S(1)}, bf16[128,1024]{1,0:T(8,128)(2,1)S(1)}) custom-call(s32[3]{0:T(128)S(1)} %pad_add_fusion.ids, bf16[384,768]{1,0:T(8,128)(2,1)S(1)} %get-tuple-element.93.sources0, bf16[384,768]{1,0:T(8,128)(2,1)S(1)} %get-tuple-element.96.sources1, ...), custom_call_target="tpu_custom_call" | custom-call | flops 1100000000 | tf_op jit(solution)/shard_map/pallas_call | solution.py:174
  42.6 0.1 collective-permute-start.7
  42.7 0.5 collective-permute-start.8
  43.2 0.1 collective-permute-start.9
  43.2 1.4 %shard_map.85.full = f32[2,184,1024]{2,1,0:T(8,128)S(1)} custom-call(s32[3]{0:T(128)S(1)} %pad_add_fusion.ids, bf16[384,768]{1,0:T(8,128)(2,1)S(1)} %get-tuple-element.93.sources0, bf16[384,768]{1,0:T(8,128)(2,1)S(1)} %get-tuple-element.96.sources1, bf16[768,1024]{1,0:T(8,128)(2,1)S(1)} %get-tuple-element.64.placed0, ...), custom_call_target="tpu_custom_call" | custom-call | flops 1100000000 | tf_op jit(solution)/shard_map/pallas_call | solution.py:174
  44.6 0.3 collective-permute-done.9.rest_2_
  44.9 2.3 %shard_map.86.rest_4_ = f32[720,1024]{1,0:T(8,128)S(1)} custom-call(s32[3]{0:T(128)S(1)} %pad_add_fusion.ids, f32[2,2,184,128]{3,2,1,0:T(8,128)S(1)} %get-tuple-element.61.courant, f32[2,1024]{1,0:T(2,128)S(1)} %copy-done, f32[2,1024]{1,0:T(2,128)S(1)} %convert_element_type.4.mask, f32[2,184,1024]{2,1,0:T(8,128)S(1)} %shard_map.85.full, ...), custom_call_target="tpu_custom_call" | custom-call | flops 11000000 | tf_op jit(solution)/shard_map/pallas_call | solution.py:174
  47.3 4.2 %shard_map.87 = bf16[360,2,1024]{2,1,0:T(2,128)(2,1)} custom-call(s32[3]{0:T(128)S(1)} %pad_add_fusion.ids, f32[2,2,184,128]{3,2,1,0:T(8,128)S(1)} %get-tuple-element.61.courant, f32[2,1024]{1,0:T(2,128)S(1)} %copy-done, f32[2,1024]{1,0:T(2,128)S(1)} %convert_element_type.4.mask, f32[2,184,1024]{2,1,0:T(8,128)S(1)} %get-tuple-element.99.full, ...), custom_call_target="tpu_custom_call" | custom-call | flops 4400000000 | tf_op jit(solution)/shard_map/pallas_call | solution.py:174
  (18 shorter events, 0.0 us)
Async XLA Ops:
  0.8 1.4 %copy-start.1 = (bf16[360,2,1024]{2,1,0:T(2,128)(2,1)S(1)}, bf16[360,2,1024]{2,1,0:T(2,128)(2,1)}, u32[]{:S(2)}) copy-start(bf16[360,2,1024]{2,1,0:T(2,128)(2,1)} %energy.1) | copy-start | bytes 4423684
  2.2 5.0 %copy-start = (f32[2,1024]{1,0:T(2,128)S(1)}, f32[2,1024]{1,0:T(2,128)}, u32[]{:S(2)}) copy-start(f32[2,1024]{1,0:T(2,128)} %depth.7) | copy-start | bytes 24580
  4.4 2.7 %collective-permute-start = (bf16[2,184,1024]{2,1,0:T(8,128)(2,1)S(1)}, bf16[2,184,1024]{2,1,0:T(8,128)(2,1)S(1)}, u32[]{:S(2)}, u32[]{:S(2)}) collective-permute-start(bf16[2,184,1024]{2,1,0:T(8,128)(2,1)S(1)} %get-tuple-element.63.field), channel_id=1, source_target_pairs={{0,2},{2,0},{4,6},{6,4},{8,10},{10,8},{12,14},{14,12},{16,18},{18,... | collective-permute-start | bytes 2261000 | tf_op jit(solution)/shard_map/ppermute | solution.py:539
  4.5 20.3 %collective-permute-start.1 = (bf16[2,184,1024]{2,1,0:T(8,128)(2,1)S(1)}, bf16[2,184,1024]{2,1,0:T(8,128)(2,1)S(1)}, u32[]{:S(2)}, u32[]{:S(2)}) collective-permute-start(bf16[2,184,1024]{2,1,0:T(8,128)(2,1)S(1)} %get-tuple-element.62.field), channel_id=1, source_target_pairs={{0,30},{2,4},{4,2},{6,8},{8,6},{10,12},{12,10},{14,16},{16,14},{18... | collective-permute-start | bytes 2261000 | tf_op jit(solution)/shard_map/ppermute | solution.py:540
  7.1 4.5 %copy-start.5 = (f32[720]{0:T(1024)S(1)}, f32[720]{0:T(1024)}, u32[]{:S(2)}) copy-start(f32[720]{0:T(1024)} %param.13) | copy-start | bytes 8644
  7.1 4.5 %copy-start.2 = (bf16[720,720]{1,0:T(8,128)(2,1)S(1)}, bf16[720,720]{1,0:T(8,128)(2,1)}, u32[]{:S(2)}) copy-start(bf16[720,720]{1,0:T(8,128)(2,1)} %first.1) | copy-start | bytes 3110404
  7.1 4.5 %copy-start.3 = (bf16[720,720]{1,0:T(8,128)(2,1)S(1)}, bf16[720,720]{1,0:T(8,128)(2,1)}, u32[]{:S(2)}) copy-start(bf16[720,720]{1,0:T(8,128)(2,1)} %second.1) | copy-start | bytes 3110404
  7.1 4.5 %copy-start.4 = (bf16[720,720]{1,0:T(8,128)(2,1)S(1)}, bf16[720,720]{1,0:T(8,128)(2,1)}, u32[]{:S(2)}) copy-start(bf16[720,720]{1,0:T(8,128)(2,1)} %transfer.1) | copy-start | bytes 3110404
  9.6 20.8 %collective-permute-start.2 = (bf16[184,1536]{1,0:T(8,128)(2,1)S(1)}, bf16[184,1536]{1,0:T(8,128)(2,1)S(1)}, u32[]{:S(2)}, u32[]{:S(2)}) collective-permute-start(bf16[184,1536]{1,0:T(8,128)(2,1)S(1)} %get-tuple-element.74.own0.rest_2_), channel_id=1, source_target_pairs={{0,1},{1,0},{2,3},{3,2},{4,5},{5,4},{6,7},{7,6},{8,9},{9,8},{10,11... | collective-permute-start | bytes 1695752 | tf_op jit(solution)/shard_map/ppermute | solution.py:550
  27.3 7.7 %collective-permute-start.3 = (bf16[184,768]{1,0:T(8,128)(2,1)S(1)}, bf16[184,768]{1,0:T(8,128)(2,1)S(1)}, u32[]{:S(2)}, u32[]{:S(2)}) collective-permute-start(bf16[184,768]{1,0:T(8,128)(2,1)S(1)} %get-tuple-element.81.own1_0.rest_3_), channel_id=1, source_target_pairs={{0,1},{1,0},{2,3},{3,2},{4,5},{5,4},{6,7},{7,6},{8,9},{9,8},{10,11... | collective-permute-start | bytes 847880 | tf_op jit(solution)/shard_map/ppermute | solution.py:575
  29.0 9.5 %collective-permute-start.4 = (bf16[192,768]{1,0:T(8,128)(2,1)S(1)}, bf16[192,768]{1,0:T(8,128)(2,1)S(1)}, u32[]{:S(2)}, u32[]{:S(2)}) collective-permute-start(bf16[192,768]{1,0:T(8,128)(2,1)S(1)} %get-tuple-element.82.own1_1.rest_3_), channel_id=1, source_target_pairs={{0,1},{1,0},{2,3},{3,2},{4,5},{5,4},{6,7},{7,6},{8,9},{9,8},{10,11... | collective-permute-start | bytes 884744 | tf_op jit(solution)/shard_map/ppermute | solution.py:575
  37.3 9.9 %collective-permute-start.5 = (bf16[192,768]{1,0:T(8,128)(2,1)S(1)}, bf16[192,768]{1,0:T(8,128)(2,1)S(1)}, u32[]{:S(2)}, u32[]{:S(2)}) collective-permute-start(bf16[192,768]{1,0:T(8,128)(2,1)S(1)} %get-tuple-element.100), channel_id=1, source_target_pairs={{0,30},{2,4},{4,2},{6,8},{8,6},{10,12},{12,10},{14,16},{16,14},{18... | collective-permute-start | bytes 884744 | tf_op jit(solution)/shard_map/ppermute | solution.py:602
  40.5 6.7 %collective-permute-start.6 = (bf16[184,768]{1,0:T(8,128)(2,1)S(1)}, bf16[184,768]{1,0:T(8,128)(2,1)S(1)}, u32[]{:S(2)}, u32[]{:S(2)}) collective-permute-start(bf16[184,768]{1,0:T(8,128)(2,1)S(1)} %get-tuple-element.101), channel_id=1, source_target_pairs={{2,4},{3,5},{4,2},{5,3},{6,8},{7,9},{8,6},{9,7},{10,12},{11,13},{1... | collective-permute-start | bytes 847880 | tf_op jit(solution)/shard_map/ppermute | solution.py:602
  42.6 2.0 %collective-permute-start.7 = (bf16[128,1024]{1,0:T(8,128)(2,1)S(1)}, bf16[128,1024]{1,0:T(8,128)(2,1)S(1)}, u32[]{:S(2)}, u32[]{:S(2)}) collective-permute-start(bf16[128,1024]{1,0:T(8,128)(2,1)S(1)} %get-tuple-element.106), channel_id=1, source_target_pairs={{0,2},{2,0},{4,6},{6,4},{8,10},{10,8},{12,14},{14,12},{16,18},{18,... | collective-permute-start | bytes 786440 | tf_op jit(solution)/shard_map/ppermute | solution.py:610
  42.7 2.0 %collective-permute-start.8 = (bf16[128,1024]{1,0:T(8,128)(2,1)S(1)}, bf16[128,1024]{1,0:T(8,128)(2,1)S(1)}, u32[]{:S(2)}, u32[]{:S(2)}) collective-permute-start(bf16[128,1024]{1,0:T(8,128)(2,1)S(1)} %get-tuple-element.107), channel_id=1, source_target_pairs={{0,2},{2,0},{4,6},{6,4},{8,10},{10,8},{12,14},{14,12},{16,18},{18,... | collective-permute-start | bytes 786440 | tf_op jit(solution)/shard_map/ppermute | solution.py:610
  43.2 1.8 %collective-permute-start.9 = (bf16[128,1024]{1,0:T(8,128)(2,1)S(1)}, bf16[128,1024]{1,0:T(8,128)(2,1)S(1)}, u32[]{:S(2)}, u32[]{:S(2)}) collective-permute-start(bf16[128,1024]{1,0:T(8,128)(2,1)S(1)} %get-tuple-element.108), channel_id=1, source_target_pairs={{0,2},{2,0},{4,6},{6,4},{8,10},{10,8},{12,14},{14,12},{16,18},{18,... | collective-permute-start | bytes 786440 | tf_op jit(solution)/shard_map/ppermute | solution.py:610
